TPU v7x, 32 devices: a whole 2x2x4 slice. The times are simulated.
32 devices in a mesh: parts: 2 (over y), rows: 8 (over z, x), tp: 2 (over core).
Axes of the slice: x: 2, y: 2, z: 4, core: 2. Of those that a mesh axis runs over, the one named last changes fastest.
Arguments:
- tokens: bfloat16 [256, 8192], P(('parts', 'rows'), 'tp'), parts along dimension 0, may hold values from -6 to 6
- gate_weight: bfloat16 [8192, 28672], P('tp', 'rows'), may hold values from -0.0625 to 0.0625
- down_panels: bfloat16 [8, 64, 8192], P('rows', None, 'tp'), may hold values from -0.0625 to 0.0625
- up_panels: bfloat16 [8, 64, 8, 2, 1792], P('rows', None, None, 'tp'), may hold values from -0.75 to 0.75
- adapter_scales: float32 [8], P('rows'), may hold values from 0.25 to 2
- adapter_per_row: int32 [256, 1], P('parts'), parts along dimension 0, may hold values from 0 to 7; in each aligned block of 128 rows (0 to 127, 128 to 255, ...) at most 32 rows name the same one
- storage_index_map: int32 [8], replicated, may hold values from 0 to 7, each once
Outputs:
- gate_out: bfloat16 [256, 28672], P('parts', ('rows', 'tp')), parts along dimension 0
There are 2 independent parts, one for each index of `parts`. A program takes and returns all parts, laid end to end along the dimension named above; an argument that names none is the same for every part. Nothing has to cross between parts.
Inputs may be any that keep to these rules, and one draw needn't show every extreme that they name: `adapter_per_row`: at most 32 rows name one adapter, and one adapter is named by exactly 32 rows; every adapter is named by some row. A permutation: adapter a's panels and scale stand at index storage_index_map[a] of down_panels, up_panels and adapter_scales.
All inputs are finite; a program needn't handle non-finite values.
Results may differ from a plain program's by a relative error of at most 0.0051.
Values may be sent and summed in bfloat16 or wider, within the bound.
No kernel may reach another device: no remote copies, remote signals or barrier semaphores. Data moves between devices by JAX's collectives and lax.ppermute only.
A program may use at most 128 MiB of HBM per device.

v0:
```python
import jax
import jax.numpy as jnp
from jax import lax
from jax.sharding import PartitionSpec as P

CAP = 32


def slot_layout(adapter_per_row, storage_index_map, owner_indices, slot_depth):
    row_total = adapter_per_row.shape[0]
    stored = jnp.take(storage_index_map, adapter_per_row[:, 0], axis=0)
    row_order = jnp.argsort(stored, stable=True)
    arranged = jnp.take(stored, row_order, axis=0)
    matches = (stored[:, None] == jnp.arange(owner_indices, dtype=jnp.int32)[None, :]).astype(
        jnp.int32
    )
    counts = jnp.sum(matches, axis=0)
    starts = jnp.cumsum(counts) - counts
    within = jnp.arange(row_total, dtype=jnp.int32) - jnp.take(starts, arranged, axis=0)
    placed = arranged * slot_depth + within
    slot_of_row = jnp.zeros((row_total,), jnp.int32).at[row_order].set(placed)
    row_of_slot = (
        jnp.full((owner_indices * slot_depth,), row_total, jnp.int32)
        .at[slot_of_row]
        .set(jnp.arange(row_total, dtype=jnp.int32))
    )
    return (slot_of_row, row_of_slot)


def on_device(
    tokens, gate_weight, down_panels, up_panels, adapter_scales, adapter_per_row, storage_index_map
):
    owner_indices = lax.axis_size("rows")
    myself = lax.axis_index("rows")
    rank_columns = down_panels.shape[1]
    slot_of_row, row_of_slot = slot_layout(adapter_per_row, storage_index_map, owner_indices, CAP)
    my_rows = lax.dynamic_slice_in_dim(row_of_slot, myself * CAP, CAP, 0)
    piece = lax.all_gather(tokens, "rows", axis=0, tiled=True)
    selected_panels = jnp.zeros((CAP, tokens.shape[1]), tokens.dtype)
    block = jnp.dot(piece, gate_weight, preferred_element_type=jnp.float32)
    partial_value = block
    inside = (my_rows >= 0) & (my_rows < piece.shape[0])
    taken = jnp.take(piece, jnp.clip(my_rows, 0, piece.shape[0] - 1), axis=0)
    selected_panels = jnp.where(inside[:, None], taken, selected_panels)
    partial_value, selected_panels = (partial_value, selected_panels)
    halves = lax.psum_scatter(partial_value, "tp", scatter_dimension=1, tiled=True)
    output_width = halves.shape[1]
    reduced_rank = lax.dot_general(
        selected_panels,
        down_panels[0],
        (((1,), (1,)), ((), ())),
        preferred_element_type=jnp.float32,
    )
    reduced_rank = reduced_rank * adapter_scales[0]
    local_panel = up_panels.reshape(rank_columns, owner_indices, output_width)
    spread = jnp.zeros((owner_indices, CAP, rank_columns), jnp.float32)
    spread = lax.dynamic_update_slice_in_dim(spread, reduced_rank[None], myself, 0)
    combined = lax.psum(spread, ("rows", "tp"))
    scaled = combined.astype(jnp.bfloat16)
    arrived = lax.all_to_all(local_panel, "rows", split_axis=1, concat_axis=0, tiled=True)
    arrived = arrived.reshape(owner_indices, rank_columns, output_width)
    delta_slots = jnp.einsum(
        "ocr,orf->ocf", scaled, arrived, preferred_element_type=jnp.float32
    ).astype(jnp.bfloat16)
    delta_slots = delta_slots.reshape(owner_indices * CAP, output_width)
    delta_rows = jnp.take(delta_slots, slot_of_row, axis=0)
    return (halves + delta_rows.astype(jnp.float32)).astype(jnp.bfloat16)


def solution(mesh):
    placed = (
        P(("parts", "rows"), "tp"),
        P("tp", "rows"),
        P("rows", None, "tp"),
        P("rows", None, None, "tp", None),
        P("rows"),
        P("parts", None),
        P(),
    )
    return jax.shard_map(
        on_device, mesh=mesh, in_specs=placed, out_specs=P("parts", ("rows", "tp")), check_vma=False
    )
```

profile of v0, /device:TPU:0, one launch (start us, length us, event | category | flops | bytes accessed | tf_op | source)
XLA Modules:
  0.0 169.6 jit_solution(6028178634230639363)
XLA Ops:
  6.5 0.0 copy-start
  6.5 0.0 all-gather.2.cloned.1.call-start
  6.5 0.7 all-gather.2.cloned.1.call-update
  7.3 0.0 reduce-scatter.2.cloned.1.call-start
  7.3 45.1 %all-gather.2.cloned.1.call-done = bf16[128,4096]{1,0:T(8,128)(2,1)} async-done(((bf16[16,4096]{1,0:T(8,128)(2,1)}), bf16[128,4096]{1,0:T(8,128)(2,1)}) %all-gather.2.cloned.1.call-update) | async-done | bytes 1048592 | tf_op jit(solution)/shard_map/all_gather | solution.py:38
  52.4 14.9 %fusion.21 = f32[128,3584]{1,0:T(8,128)} fusion(bf16[128,4096]{1,0:T(8,128)(2,1)} %all-gather.2.cloned.1.call-done, bf16[4096,3584]{1,0:T(8,128)(2,1)} %param.10), kind=kOutput, calls=%fused_computation.61 | convolution fusion | flops 3758096384 | bytes 32243712 | tf_op jit(solution)/shard_map/dot_general | solution.py:40
  67.3 0.0 reduce-scatter.2.cloned.1.call-update
  67.3 1.5 copy-done.2
  68.8 1.5 copy.12
  70.3 3.7 %all-to-all-start = ((bf16[64,8,1792]{2,0,1:T(8,128)(2,1)}), bf16[64,8,1792]{2,0,1:T(8,128)(2,1)S(1)}, u32[]{:S(2)}, u32[]{:S(2)}) async-start(bf16[64,8,1792]{2,0,1:T(8,128)(2,1)} %bitcast.42), calls=%async_computation.1 | async-start | bytes 3670016 | tf_op jit(solution)/shard_map/all_to_all | solution.py:60
  74.7 0.0 copy-done.3
  74.7 0.7 fusion.20
  75.4 0.0 copy-done.4
  75.4 5.0 %and_select_fusion.1 = s32[128]{0:T(128)S(1)} fusion(s32[128,1]{0,1:T(1,128)S(1)} %copy-done.4, s32[]{:T(128)} %bitcast.8, s32[]{:T(128)} %bitcast.7, s32[]{:T(128)} %bitcast.6, s32[]{:T(128)} %bitcast.5, s32[]{:T(128)} %bitcast.4, s32[]{:T(128)} %bitcast.3, s32[]{:T(128)} %bitcast.2, s32[]{:T(128)} %bitcast.1), kind=kLoop, calls=%fused_computation.45 | loop fusion | flops 2688 | bytes 1056 | tf_op jit(solution)/shard_map/jit(_take)/select_n | solution.py:11
  80.4 0.1 convert_reduce_fusion
  80.5 0.2 reduce-window.9
  80.7 2.5 %sort.17 = (s32[128]{0:T(128)}, s32[128]{0:T(128)S(1)}) sort(s32[128]{0:T(128)S(1)} %and_select_fusion.1, s32[128]{0:T(128)S(1)} %iota.14), dimensions={0}, to_apply=%region_1.3 | sort | flops 896 | bytes 2048 | tf_op jit(solution)/shard_map/jit(argsort)/sort | solution.py:12
  83.3 1.2 gather_fusion
  84.5 0.7 fusion.19
  85.2 5.0 %fusion.12 = s32[128]{0:T(128)S(1)} fusion(s32[128]{0:T(128)S(1)} %gather_fusion, s32[]{:T(128)} %bitcast.18, s32[]{:T(128)} %bitcast.17, s32[]{:T(128)} %bitcast.16, s32[]{:T(128)} %bitcast.15, s32[]{:T(128)} %bitcast.14, s32[]{:T(128)} %bitcast.13, s32[]{:T(128)} %bitcast.12, s32[]{:T(128)} %bitcast.11, s32[128]{0:T(128)S(1)} %get-tuple-element.7), kind=kLoop, calls=%fused_computation.51 | loop fusion | flops 3968 | bytes 1568 | tf_op jit(solution)/shard_map/add | solution.py:20
  90.2 1.0 scatter_custom_fusion
  91.2 1.0 scatter_custom_fusion.1
  92.2 0.1 compare_and_fusion
  92.3 1.4 gather_fusion.1
  93.8 0.0 copy-done
  93.8 1.3 fusion.2
  95.0 64.2 %psum.7 = bf16[8,32,64]{2,1,0:T(8,128)(2,1)S(1)} all-reduce(f32[8,32,64]{2,1,0:T(8,128)S(1)} %fusion.2), channel_id=1, replica_groups=mesh['parts'=2,'rows'=8,'tp'=2] {'rows','tp'}, use_global_device_ids=true, to_apply=%region_6.8 | all-reduce | flops 16384 | bytes 98304 | tf_op jit(solution)/shard_map/psum | solution.py:58
  159.2 0.0 all-to-all-done
  159.2 0.4 convolution_convert_fusion
  159.6 0.9 gather_fusion.2
  160.6 0.0 reduce-scatter.2.cloned.1.call-done
  160.6 2.1 %add_convert_fusion = bf16[128,1792]{1,0:T(8,128)(2,1)} fusion(f32[128,1792]{1,0:T(8,128)} %reduce-scatter.2.cloned.1.call-done, bf16[128,1792]{1,0:T(8,128)(2,1)S(1)} %gather_fusion.2, pred[128]{0:T(512)(128)(4,1)S(1)} %compare_and_fusion.2), kind=kLoop, calls=%fused_computation.11 | loop fusion | flops 917504 | bytes 1835136 | tf_op jit(solution)/shard_map/convert_element_type | solution.py:67
  (15 shorter events, 0.1 us)
Async XLA Ops:
  6.5 87.2 %copy-start = (bf16[1,64,4096]{2,1,0:T(8,128)(2,1)S(1)}, bf16[1,64,4096]{2,1,0:T(8,128)(2,1)}, u32[]{:S(2)}) copy-start(bf16[1,64,4096]{2,1,0:T(8,128)(2,1)} %param.11) | copy-start | bytes 1572868
  6.5 45.8 %all-gather.2.cloned.1.call-start = ((), (), s32[]{:S(2)}) async-start(), calls=%async_computation.2 | async-start | bytes 1179648 | tf_op jit(solution)/shard_map/all_gather | solution.py:38
  7.3 153.3 %reduce-scatter.2.cloned.1.call-start = ((), (), s32[]{:S(2)}) async-start(), calls=%async_computation.3 | async-start | bytes 2752512 | tf_op jit(solution)/shard_map/reduce_scatter | solution.py:46
  67.3 1.5 copy-start.2
  70.3 4.4 %copy-start.3 = (s32[8]{0:T(128)S(1)}, s32[8]{0:T(128)}, u32[]{:S(2)}) copy-start(s32[8]{0:T(128)} %param.15) | copy-start | bytes 100
  70.3 5.1 %copy-start.4 = (s32[128,1]{0,1:T(1,128)S(1)}, s32[128,1]{0,1:T(1,128)}, u32[]{:S(2)}) copy-start(s32[128,1]{0,1:T(1,128)} %param.14) | copy-start | bytes 1540
  70.3 22.0 %copy-start.1 = (bf16[128,4096]{1,0:T(8,128)(2,1)S(1)}, bf16[128,4096]{1,0:T(8,128)(2,1)}, u32[]{:S(2)}) copy-start(bf16[128,4096]{1,0:T(8,128)(2,1)} %all-gather.2.cloned.1.call-done) | copy-start | bytes 3145732
  70.3 88.9 %all-to-all-start = ((bf16[64,8,1792]{2,0,1:T(8,128)(2,1)}), bf16[64,8,1792]{2,0,1:T(8,128)(2,1)S(1)}, u32[]{:S(2)}, u32[]{:S(2)}) async-start(bf16[64,8,1792]{2,0,1:T(8,128)(2,1)} %bitcast.42), calls=%async_computation.1 | async-start | bytes 3670016 | tf_op jit(solution)/shard_map/all_to_all | solution.py:60
Sparse Core Ops, SparseCore 0:
  9.5 42.8 all-gather.1
  67.4 8.1 reduce-scatter.1
where the time goes:
time: 170 us
  blocking collectives  64.2 us (38%)
  waiting for transfers between devices  45.8 us (27%)
  matrix products  16.6 us (10%)
  other arithmetic  15.1 us (9%)
  between operations  14.2 us (8%)
  local copies, waits for them, and re-layouts  9.93 us (6%)
  starting transfers between devices  3.77 us (2%)
    psum x1, blocking collectives, on_device(): combined = lax.psum(spread, ('rows', 'tp'))  64.2 us
    all_gather x1, waiting for transfers between devices, on_device(): piece = lax.all_gather(tokens, 'rows', axis=0, tiled=True)  45.1 us
    dot_general x1, matrix products, on_device(): block = jnp.dot(piece, gate_weight, preferred_element_type=jnp.float32)  14.9 us
    add x1, other arithmetic, slot_layout(): placed = arranged * slot_depth + within  5 us
    select_n x1, other arithmetic, slot_layout(): stored = jnp.take(storage_index_map, adapter_per_row[:, 0], axis=0)  5 us
    all_to_all x1, starting transfers between devices, on_device(): lax.all_to_all(local_panel, 'rows', split_axis=1, concat_axis=0, tiled=True)  3.73 us
  transfers between devices with their start and end apart: 3, of which 1 were waited for; matrix products, arithmetic and copies ran while one was open for 14% of the time, Pallas kernels for 0%

commit v1 on v0

v1 whole, which is shorter than its diff:
```python
import functools

import jax
import jax.numpy as jnp
from jax import lax
from jax.experimental import pallas as pl
from jax.experimental.pallas import tpu as pltpu
from jax.sharding import PartitionSpec as P

CAP = 32
F32 = jnp.float32
BF16 = jnp.bfloat16
VMEM = pl.BlockSpec(memory_space=pltpu.VMEM)
SMEM = pl.BlockSpec(memory_space=pltpu.SMEM)


def slot_layout(adapter_per_row, storage_index_map, owner_indices, slot_depth):
    row_total = adapter_per_row.shape[0]
    stored = jnp.take(storage_index_map, adapter_per_row[:, 0], axis=0)
    row_order = jnp.argsort(stored, stable=True)
    arranged = jnp.take(stored, row_order, axis=0)
    matches = (stored[:, None] == jnp.arange(owner_indices, dtype=jnp.int32)[None, :]).astype(
        jnp.int32
    )
    counts = jnp.sum(matches, axis=0)
    starts = jnp.cumsum(counts) - counts
    within = jnp.arange(row_total, dtype=jnp.int32) - jnp.take(starts, arranged, axis=0)
    placed = arranged * slot_depth + within
    slot_of_row = jnp.zeros((row_total,), jnp.int32).at[row_order].set(placed)
    row_of_slot = (
        jnp.full((owner_indices * slot_depth,), row_total, jnp.int32)
        .at[slot_of_row]
        .set(jnp.arange(row_total, dtype=jnp.int32))
    )
    return (slot_of_row, row_of_slot)


def many_groups(
    tokens, gate_weight, down_panels, up_panels, adapter_scales, adapter_per_row, storage_index_map
):
    owner_indices = lax.axis_size("rows")
    myself = lax.axis_index("rows")
    slot_of_row, row_of_slot = slot_layout(adapter_per_row, storage_index_map, owner_indices, CAP)
    my_rows = lax.dynamic_slice_in_dim(row_of_slot, myself * CAP, CAP, 0)
    piece = lax.all_gather(tokens, "rows", axis=0, tiled=True)
    inside = my_rows < piece.shape[0]
    taken = jnp.take(piece, jnp.clip(my_rows, 0, piece.shape[0] - 1), axis=0)
    selected = jnp.where(inside[:, None], taken, jnp.zeros_like(taken))
    block = jnp.dot(piece, gate_weight, preferred_element_type=F32)
    halves = lax.psum_scatter(block, "tp", scatter_dimension=1, tiled=True)
    width = up_panels.shape[-1]
    low = lax.dot_general(
        selected, down_panels[0], (((1,), (1,)), ((), ())), preferred_element_type=F32
    )
    low = low + lax.ppermute(low, "tp", [(0, 1), (1, 0)])
    low = (low * adapter_scales[0]).astype(BF16)
    panel = up_panels.reshape(down_panels.shape[1], owner_indices, width)
    delta = jnp.einsum("cr,rof->ocf", low, panel, preferred_element_type=F32).astype(BF16)
    arrived = lax.all_to_all(delta, "rows", split_axis=0, concat_axis=0, tiled=True)
    delta_rows = jnp.take(arrived.reshape(owner_indices * CAP, width), slot_of_row, axis=0)
    return (halves + delta_rows.astype(F32)).astype(BF16)


def slots_as_row(adapter_ref, map_ref):
    rows = adapter_ref.shape[1]
    count = map_ref.shape[0]
    adapter = adapter_ref[...]
    stored = jnp.zeros_like(adapter)
    for a in range(count):
        stored = jnp.where(adapter == a, map_ref[a], stored)
    index = lax.broadcasted_iota(jnp.int32, (count, rows), 0)
    match = (stored == index).astype(F32)
    earlier = (
        lax.broadcasted_iota(jnp.int32, (rows, rows), 0)
        < lax.broadcasted_iota(jnp.int32, (rows, rows), 1)
    ).astype(F32)
    before = jnp.dot(match.astype(BF16), earlier.astype(BF16), preferred_element_type=F32)
    within = jnp.sum(match * before, axis=0, keepdims=True)
    return stored * CAP + within.astype(jnp.int32)


def lowrank_kernel(groups, *refs):
    where, index_map, adapter = refs[:3]
    pieces = refs[3 : 3 + groups]
    down, out, gathered = refs[3 + groups :]
    me = where[0]
    part = pieces[0].shape[0]
    for d in range(groups):
        start = pl.multiple_of((me ^ d) * part, part)
        gathered[pl.ds(start, part), :] = pieces[d][...]
    slot = slots_as_row(adapter, index_map)
    rows = slot.shape[1]
    mine = lax.broadcasted_iota(jnp.int32, (CAP, rows), 0) + me * CAP
    chosen = (slot == mine).astype(F32).astype(BF16)
    selected = jnp.dot(chosen, gathered[...], preferred_element_type=F32).astype(BF16)
    out[...] = lax.dot_general(
        selected, down[...], (((1,), (1,)), ((), ())), preferred_element_type=F32
    )


def delta_kernel(groups, scale, low_a, low_b, up, out, spread):
    rank = low_a.shape[1]
    low = ((low_a[...] + low_b[...]) * scale[0]).astype(BF16)
    depth = rank * groups
    widen = (
        lax.broadcasted_iota(jnp.int32, (rank, depth), 0)
        == lax.broadcasted_iota(jnp.int32, (rank, depth), 1) // groups
    ).astype(F32).astype(BF16)
    wide = jnp.dot(low, widen, preferred_element_type=F32)
    block = lax.rem(lax.broadcasted_iota(jnp.int32, (CAP, depth), 1), groups)
    for d in range(groups):
        spread[d * CAP : (d + 1) * CAP, :] = jnp.where(block == d, wide, 0.0).astype(BF16)
    result = jnp.dot(spread[...], up[...], preferred_element_type=F32)
    out[...] = result.astype(BF16)


def base_kernel(groups, *refs):
    where = refs[0]
    pieces = refs[1 : 1 + groups]
    weight, _, out, gathered = refs[1 + groups :]
    me = where[0]
    part = pieces[0].shape[0]

    @pl.when(pl.program_id(0) == 0)
    def _():
        for d in range(groups):
            start = pl.multiple_of((me ^ d) * part, part)
            gathered[pl.ds(start, part), :] = pieces[d][...]

    out[...] = jnp.dot(gathered[...], weight[...], preferred_element_type=F32)


def final_kernel(groups, index_map, adapter, own, other, arrived, out):
    slot = slots_as_row(adapter, index_map)
    rows = slot.shape[1]
    place = (
        slot == lax.broadcasted_iota(jnp.int32, (groups * CAP, rows), 0)
    ).astype(F32).astype(BF16)
    delta = lax.dot_general(
        place, arrived[...], (((0,), (0,)), ((), ())), preferred_element_type=F32
    )
    out[...] = (own[...] + other[...] + delta).astype(BF16)


def few_groups(
    tokens, gate_weight, down_panels, up_panels, adapter_scales, adapter_per_row, storage_index_map
):
    groups = lax.axis_size("rows")
    me = lax.axis_index("rows").astype(jnp.int32)
    core = lax.axis_index("tp").astype(jnp.int32)
    part, depth = tokens.shape
    rows = part * groups
    rank = down_panels.shape[1]
    width = up_panels.shape[-1]
    where = me.reshape(1)
    adapter = adapter_per_row.reshape(1, rows)
    swap = [(0, 1), (1, 0)]

    def to(x, d):
        return lax.ppermute(x, "rows", [(i, i ^ d) for i in range(groups)])

    pieces = {0: tokens}
    for d in range(2, groups, 2):
        pieces[d] = to(tokens, d)
    if groups > 1:
        for d in range(0, groups, 2):
            pieces[d + 1] = to(pieces[d], 1)
    pieces = [pieces[d] for d in range(groups)]

    low = pl.pallas_call(
        functools.partial(lowrank_kernel, groups),
        out_shape=jax.ShapeDtypeStruct((CAP, rank), F32),
        in_specs=[SMEM, SMEM, VMEM] + [VMEM] * groups + [VMEM],
        out_specs=VMEM,
        scratch_shapes=[pltpu.VMEM((rows, depth), BF16)],
        compiler_params=pltpu.CompilerParams(vmem_limit_bytes=16 << 20),
        cost_estimate=pl.CostEstimate(flops=10**8, bytes_accessed=2 * 10**6, transcendentals=0),
        name="lowrank",
    )(where, storage_index_map, adapter, *pieces, down_panels[0])
    low_other = lax.ppermute(low, "tp", swap)

    deltas = pl.pallas_call(
        functools.partial(delta_kernel, groups),
        out_shape=jax.ShapeDtypeStruct((groups * CAP, width), BF16),
        in_specs=[SMEM, VMEM, VMEM, VMEM],
        out_specs=VMEM,
        scratch_shapes=[pltpu.VMEM((groups * CAP, rank * groups), BF16)],
        compiler_params=pltpu.CompilerParams(vmem_limit_bytes=32 << 20),
        cost_estimate=pl.CostEstimate(flops=5 * 10**8, bytes_accessed=3 * 10**6, transcendentals=0),
        name="delta",
    )(adapter_scales, low, low_other, up_panels.reshape(rank * groups, width))
    arrived = lax.all_to_all(deltas, "rows", split_axis=0, concat_axis=0, tiled=True)

    tile = 256

    def base(which, after):
        steps = width // tile
        return pl.pallas_call(
            functools.partial(base_kernel, groups),
            grid_spec=pltpu.PrefetchScalarGridSpec(
                num_scalar_prefetch=1,
                grid=(steps,),
                in_specs=[pl.BlockSpec((part, depth), lambda i, s: (0, 0))] * groups
                + [pl.BlockSpec((depth, tile), lambda i, s: (0, s[1] * steps + i))]
                + [pl.BlockSpec(memory_space=pl.ANY)],
                out_specs=pl.BlockSpec((rows, tile), lambda i, s: (0, i)),
                scratch_shapes=[pltpu.VMEM((rows, depth), BF16)],
            ),
            out_shape=jax.ShapeDtypeStruct((rows, width), F32),
            compiler_params=pltpu.CompilerParams(vmem_limit_bytes=32 << 20),
            cost_estimate=pl.CostEstimate(
                flops=rows * depth,
                bytes_accessed=2 * depth,
                transcendentals=0,
            ),
            name="base",
        )(jnp.stack([me, which]), *pieces, gate_weight, after)

    partner = base(1 - core, deltas)
    other = lax.ppermute(partner, "tp", swap)
    own = base(core, partner)

    return pl.pallas_call(
        functools.partial(final_kernel, groups),
        out_shape=jax.ShapeDtypeStruct((rows, width), BF16),
        in_specs=[SMEM, VMEM, VMEM, VMEM, VMEM],
        out_specs=VMEM,
        compiler_params=pltpu.CompilerParams(vmem_limit_bytes=32 << 20),
        cost_estimate=pl.CostEstimate(flops=2 * 10**8, bytes_accessed=4 * 10**6, transcendentals=0),
        name="combine",
    )(storage_index_map, adapter, own, other, arrived)


def on_device(*args):
    if lax.axis_size("rows") in (2, 4, 8):
        return few_groups(*args)
    return many_groups(*args)


def solution(mesh):
    placed = (
        P(("parts", "rows"), "tp"),
        P("tp", "rows"),
        P("rows", None, "tp"),
        P("rows", None, None, "tp", None),
        P("rows"),
        P("parts", None),
        P(),
    )
    return jax.shard_map(
        on_device, mesh=mesh, in_specs=placed, out_specs=P("parts", ("rows", "tp")), check_vma=False
    )
```

time: 170 us -> 63.8 us (0.38)
  blocking collectives: 64.2 us -> 0 us
  waiting for transfers between devices: 45.8 us -> 16.2 us
  Pallas kernels: 0 us -> 22.8 us
  matrix products: 16.6 us -> 0 us
  other arithmetic: 15.1 us -> 0.15 us
  between operations: 14.2 us -> 0.73 us
  starting transfers between devices: 3.77 us -> 15.6 us
  local copies, waits for them, and re-layouts: 9.93 us -> 7.8 us
    psum x1 -> x0, blocking collectives: 64.2 us -> none  [on_device(): combined = lax.psum(spread, ('rows', 'tp'))]
    all_gather x1 -> x0, waiting for transfers between devices: 45.1 us -> none  [on_device(): piece = lax.all_gather(tokens, 'rows', axis=0, tiled=True)]
    pallas_call x0 -> x5, Pallas kernels: none -> 22.8 us  [the longest x2 18.1 us: base(): pl.pallas_call(functools.partial(base_kernel, groups), grid_spec=pltpu.Pr...]
    dot_general x3 -> x0, matrix products: 16.6 us -> none  [the longest x1 14.9 us: on_device(): block = jnp.dot(piece, gate_weight, preferred_element_type=jnp.float32)]
    ppermute x0 -> x9, waiting for transfers between devices: none -> 13.2 us  [the longest x7 12.6 us: to(): return lax.ppermute(x, 'rows', [(i, i ^ d) for i in range(groups)])]
    ppermute x0 -> x9, starting transfers between devices: none -> 11.1 us  [the longest x7 11.1 us: to(): return lax.ppermute(x, 'rows', [(i, i ^ d) for i in range(groups)])]
    select_n x3 -> x0, other arithmetic: 5 us -> none  [the longest x1 5 us: slot_layout(): stored = jnp.take(storage_index_map, adapter_per_row[:, 0], axis=0)]
    add x1 -> x0, other arithmetic: 5 us -> none  [slot_layout(): placed = arranged * slot_depth + within]
  transfers between devices with their start and end apart: 3 -> 10, of which waited for: 1 -> 6; matrix products, arithmetic and copies ran while one was open for 14% -> 0% of each run, Pallas kernels for 0% -> 29%
where the time goes in v1:
time: 63.8 us; the launch traced here: 63.3 us
  Pallas kernels  22.8 us (36%)
  waiting for transfers between devices  16.2 us (25%)
  starting transfers between devices  15.6 us (24%)
  local copies, waits for them, and re-layouts  7.8 us (12%)
  between operations  0.73 us (1%)
    pallas_call x2, Pallas kernels, base(): pl.pallas_call(functools.partial(base_kernel, groups), grid_spec=pltpu.Pr...  18.1 us
    ppermute x7, waiting for transfers between devices, to(): return lax.ppermute(x, 'rows', [(i, i ^ d) for i in range(groups)])  12.6 us
    ppermute x7, starting transfers between devices, to(): return lax.ppermute(x, 'rows', [(i, i ^ d) for i in range(groups)])  11.1 us
    unnamed x20, local copies, waits for them, and re-layouts  7.8 us
    all_to_all x1, starting transfers between devices, few_groups(): lax.all_to_all(deltas, 'rows', split_axis=0, concat_axis=0, tiled=True)  4.49 us
    all_to_all x1, waiting for transfers between devices, few_groups(): lax.all_to_all(deltas, 'rows', split_axis=0, concat_axis=0, tiled=True)  3.05 us
    pallas_call x1, Pallas kernels, few_groups(): pl.pallas_call(functools.partial(final_kernel, groups), out_shape=jax.Sha...  1.81 us
    pallas_call x1, Pallas kernels, few_groups(): pl.pallas_call(functools.partial(delta_kernel, groups), out_shape=jax.Sha...  1.68 us
  transfers between devices with their start and end apart: 10, of which 6 were waited for; matrix products, arithmetic and copies ran while one was open for 0% of the time, Pallas kernels for 29%

profile of v1, /device:TPU:0, one launch (start us, length us, event | category | flops | bytes accessed | tf_op | source)
XLA Modules:
  0.0 63.3 jit_solution(3663177107508206588)
XLA Ops:
  0.0 5.0 %collective-permute-start.5 = (bf16[16,4096]{1,0:T(8,128)(2,1)}, bf16[16,4096]{1,0:T(8,128)(2,1)S(1)}, u32[]{:S(2)}, u32[]{:S(2)}) collective-permute-start(bf16[16,4096]{1,0:T(8,128)(2,1)} %refs_1_.5), channel_id=1, source_target_pairs={{0,12},{2,14},{4,8},{6,10},{8,4},{10,6},{12,0},{14,2},{1,13},{3,15... | collective-permute-start | bytes 393224 | tf_op jit(solution)/shard_map/ppermute | solution.py:160
  5.0 0.0 collective-permute-start.3
  5.1 0.6 collective-permute-start.1
  5.6 1.7 %collective-permute-start = (bf16[16,4096]{1,0:T(8,128)(2,1)}, bf16[16,4096]{1,0:T(8,128)(2,1)S(1)}, u32[]{:S(2)}, u32[]{:S(2)}) collective-permute-start(bf16[16,4096]{1,0:T(8,128)(2,1)} %refs_1_.5), channel_id=1, source_target_pairs={{0,2},{2,0},{4,6},{6,4},{8,10},{10,8},{12,14},{14,12},{1,3},{3,1},... | collective-permute-start | bytes 393224 | tf_op jit(solution)/shard_map/ppermute | solution.py:160
  7.3 2.4 %collective-permute-done.5.refs_9_.refs_7_ = bf16[16,4096]{1,0:T(8,128)(2,1)S(1)} collective-permute-done((bf16[16,4096]{1,0:T(8,128)(2,1)}, bf16[16,4096]{1,0:T(8,128)(2,1)S(1)}, u32[]{:S(2)}, u32[]{:S(2)}) %collective-permute-start.5) | collective-permute-done | bytes 131104 | tf_op jit(solution)/shard_map/ppermute | solution.py:160
  9.7 1.7 %collective-permute-start.6 = (bf16[16,4096]{1,0:T(8,128)(2,1)S(1)}, bf16[16,4096]{1,0:T(8,128)(2,1)S(1)}, u32[]{:S(2)}, u32[]{:S(2)}) collective-permute-start(bf16[16,4096]{1,0:T(8,128)(2,1)S(1)} %collective-permute-done.5.refs_9_.refs_7_), channel_id=1, source_target_pairs={{0,2},{2,0},{4,6},{6,4},{8,10},{10,8},{12,14},{14,12},{1,3},{3,1},... | collective-permute-start | bytes 393224 | tf_op jit(solution)/shard_map/ppermute | solution.py:160
  11.4 5.0 %collective-permute-done.3.refs_7_.refs_5_ = bf16[16,4096]{1,0:T(8,128)(2,1)S(1)} collective-permute-done((bf16[16,4096]{1,0:T(8,128)(2,1)}, bf16[16,4096]{1,0:T(8,128)(2,1)S(1)}, u32[]{:S(2)}, u32[]{:S(2)}) %collective-permute-start.3) | collective-permute-done | bytes 131104 | tf_op jit(solution)/shard_map/ppermute | solution.py:160
  16.3 1.5 %collective-permute-start.4 = (bf16[16,4096]{1,0:T(8,128)(2,1)S(1)}, bf16[16,4096]{1,0:T(8,128)(2,1)S(1)}, u32[]{:S(2)}, u32[]{:S(2)}) collective-permute-start(bf16[16,4096]{1,0:T(8,128)(2,1)S(1)} %collective-permute-done.3.refs_7_.refs_5_), channel_id=1, source_target_pairs={{0,2},{2,0},{4,6},{6,4},{8,10},{10,8},{12,14},{14,12},{1,3},{3,1},... | collective-permute-start | bytes 393224 | tf_op jit(solution)/shard_map/ppermute | solution.py:160
  17.8 0.0 collective-permute-done.1.refs_5_.refs_3_
  17.8 0.5 collective-permute-start.2
  18.4 0.0 collective-permute-done.refs_4_.refs_2_
  18.4 3.9 %collective-permute-done.4.refs_8_.refs_6_ = bf16[16,4096]{1,0:T(8,128)(2,1)S(1)} collective-permute-done((bf16[16,4096]{1,0:T(8,128)(2,1)S(1)}, bf16[16,4096]{1,0:T(8,128)(2,1)S(1)}, u32[]{:S(2)}, u32[]{:S(2)}) %collective-permute-start.4) | collective-permute-done | bytes 131104 | tf_op jit(solution)/shard_map/ppermute | solution.py:160
  22.3 1.4 %collective-permute-done.2.refs_6_.refs_4_ = bf16[16,4096]{1,0:T(8,128)(2,1)S(1)} collective-permute-done((bf16[16,4096]{1,0:T(8,128)(2,1)S(1)}, bf16[16,4096]{1,0:T(8,128)(2,1)S(1)}, u32[]{:S(2)}, u32[]{:S(2)}) %collective-permute-start.2) | collective-permute-done | bytes 131104 | tf_op jit(solution)/shard_map/ppermute | solution.py:160
  23.7 0.9 %copy-done.1 = bf16[16,4096]{1,0:T(8,128)(2,1)S(1)} copy-done((bf16[16,4096]{1,0:T(8,128)(2,1)S(1)}, bf16[16,4096]{1,0:T(8,128)(2,1)}, u32[]{:S(2)}) %copy-start.1) | copy-done | bytes 131096
  24.6 1.0 %copy-done.5 = bf16[1,64,4096]{2,1,0:T(8,128)(2,1)S(1)} copy-done((bf16[1,64,4096]{2,1,0:T(8,128)(2,1)S(1)}, bf16[1,64,4096]{2,1,0:T(8,128)(2,1)}, u32[]{:S(2)}) %copy-start.5) | copy-done | bytes 524312
  25.6 0.7 %copy-done.6 = s32[8]{0:T(128)S(1)} copy-done((s32[8]{0:T(128)S(1)}, s32[8]{0:T(128)}, u32[]{:S(2)}) %copy-start.6) | copy-done | bytes 56
  26.3 0.7 %copy-done.8 = s32[128,1]{0,1:T(1,128)S(1)} copy-done((s32[128,1]{0,1:T(1,128)S(1)}, s32[128,1]{0,1:T(1,128)}, u32[]{:S(2)}) %copy-start.8) | copy-done | bytes 536
  27.0 1.2 %lowrank.1.low_a = f32[32,64]{1,0:T(8,128)S(1)} custom-call(s32[1]{0:T(128)} %bitcast.1.refs_0_, s32[8]{0:T(128)S(1)} %copy-done.6, s32[1,128]{1,0:T(1,128)S(1)} %bitcast.11, bf16[16,4096]{1,0:T(8,128)(2,1)S(1)} %copy-done.1, bf16[16,4096]{1,0:T(8,128)(2,1)S(1)} %collective-permute-done.refs_4_.refs_2_, ...), custom_call_target="tpu_custom_call" | custom-call | flops 100000000 | bytes 2000000 | tf_op jit(solution)/shard_map/lowrank/pallas_call | solution.py:170
  28.8 0.5 collective-permute-done.7.low_b
  29.3 1.5 %copy-done = bf16[1,64,8,1,1792]{4,2,3,1,0:T(8,128)(2,1)S(1)} copy-done((bf16[1,64,8,1,1792]{4,2,3,1,0:T(8,128)(2,1)S(1)}, bf16[1,64,8,1,1792]{4,2,3,1,0:T(8,128)(2,1)}, u32[]{:S(2)}) %copy-start) | copy-done | bytes 1835032
  30.8 1.7 %delta.1.refs_10_ = bf16[256,1792]{1,0:T(8,128)(2,1)} custom-call(f32[1]{0:T(128)S(6)} %copy.8.scale, f32[32,64]{1,0:T(8,128)S(1)} %lowrank.1.low_a, f32[32,64]{1,0:T(8,128)S(1)} %collective-permute-done.7.low_b, bf16[512,1792]{1,0:T(8,128)(2,1)S(1)} %bitcast.9), custom_call_target="tpu_custom_call" | custom-call | flops 500000000 | bytes 3000000 | tf_op jit(solution)/shard_map/delta/pallas_call | solution.py:182
  32.5 4.5 %all-to-all-start = ((bf16[8,32,1792]{2,1,0:T(8,128)(2,1)}), bf16[8,32,1792]{2,1,0:T(8,128)(2,1)S(1)}, u32[]{:S(2)}, u32[]{:S(2)}) async-start(bf16[8,32,1792]{2,1,0:T(8,128)(2,1)} %bitcast.6), calls=%async_computation | async-start | bytes 1835008 | tf_op jit(solution)/shard_map/all_to_all | solution.py:192
  37.0 0.1 pad_add_fusion.1.refs_0_
  37.1 0.9 %copy-done.2 = bf16[16,4096]{1,0:T(8,128)(2,1)S(1)} copy-done((bf16[16,4096]{1,0:T(8,128)(2,1)S(1)}, bf16[16,4096]{1,0:T(8,128)(2,1)}, u32[]{:S(2)}) %copy-start.2) | copy-done | bytes 131096
  38.0 9.1 %base.2.refs_10_ = f32[128,1792]{1,0:T(8,128)S(1)} custom-call(s32[2]{0:T(128)S(1)} %pad_add_fusion.1.refs_0_, bf16[16,4096]{1,0:T(8,128)(2,1)S(1)} %copy-done.2, bf16[16,4096]{1,0:T(8,128)(2,1)S(1)} %collective-permute-done.refs_4_.refs_2_, bf16[16,4096]{1,0:T(8,128)(2,1)S(1)} %collective-permute-done.1.refs_5_.refs_3_, ...), custom_call_target="tpu_custom_call" | custom-call | flops 524288 | bytes 8192 | tf_op jit(solution)/shard_map/base/pallas_call | solution.py:198
  47.0 0.1 collective-permute-start.8
  47.1 0.1 pad_add_fusion.refs_0_
  47.2 9.1 %base.3.own = f32[128,1792]{1,0:T(8,128)S(1)} custom-call(s32[2]{0:T(128)S(1)} %pad_add_fusion.refs_0_, bf16[16,4096]{1,0:T(8,128)(2,1)S(1)} %copy-done.2, bf16[16,4096]{1,0:T(8,128)(2,1)S(1)} %collective-permute-done.refs_4_.refs_2_, bf16[16,4096]{1,0:T(8,128)(2,1)S(1)} %collective-permute-done.1.refs_5_.refs_3_, ...), custom_call_target="tpu_custom_call" | custom-call | flops 524288 | bytes 8192 | tf_op jit(solution)/shard_map/base/pallas_call | solution.py:198
  56.3 0.9 %copy-done.3 = f32[128,1792]{1,0:T(8,128)} copy-done((f32[128,1792]{1,0:T(8,128)}, f32[128,1792]{1,0:T(8,128)S(1)}, u32[]{:S(2)}) %copy-start.3) | copy-done | bytes 917528
  57.2 3.1 %all-to-all-done = bf16[8,32,1792]{2,1,0:T(8,128)(2,1)S(1)} async-done(((bf16[8,32,1792]{2,1,0:T(8,128)(2,1)}), bf16[8,32,1792]{2,1,0:T(8,128)(2,1)S(1)}, u32[]{:S(2)}, u32[]{:S(2)}) %all-to-all-start) | async-done | bytes 917536 | tf_op jit(solution)/shard_map/all_to_all | solution.py:192
  60.3 1.2 %copy-done.4 = f32[128,1792]{1,0:T(8,128)S(1)} copy-done((f32[128,1792]{1,0:T(8,128)S(1)}, f32[128,1792]{1,0:T(8,128)}, u32[]{:S(2)}) %copy-start.4) | copy-done | bytes 917528
  61.5 1.8 %combine.1 = bf16[128,1792]{1,0:T(8,128)(2,1)} custom-call(s32[8]{0:T(128)S(1)} %copy-done.7, s32[1,128]{1,0:T(1,128)S(1)} %bitcast.12, f32[128,1792]{1,0:T(8,128)S(1)} %base.3.own, f32[128,1792]{1,0:T(8,128)S(1)} %copy-done.4, bf16[256,1792]{1,0:T(8,128)(2,1)S(1)} %bitcast.8), custom_call_target="tpu_custom_call" | custom-call | flops 200000000 | bytes 4000000 | tf_op jit(solution)/shard_map/combine/pallas_call | solution.py:223
  (15 shorter events, 0.0 us)
Async XLA Ops:
  0.0 9.7 %collective-permute-start.5 = (bf16[16,4096]{1,0:T(8,128)(2,1)}, bf16[16,4096]{1,0:T(8,128)(2,1)S(1)}, u32[]{:S(2)}, u32[]{:S(2)}) collective-permute-start(bf16[16,4096]{1,0:T(8,128)(2,1)} %refs_1_.5), channel_id=1, source_target_pairs={{0,12},{2,14},{4,8},{6,10},{8,4},{10,6},{12,0},{14,2},{1,13},{3,15... | collective-permute-start | bytes 393224 | tf_op jit(solution)/shard_map/ppermute | solution.py:160
  5.0 11.3 %collective-permute-start.3 = (bf16[16,4096]{1,0:T(8,128)(2,1)}, bf16[16,4096]{1,0:T(8,128)(2,1)S(1)}, u32[]{:S(2)}, u32[]{:S(2)}) collective-permute-start(bf16[16,4096]{1,0:T(8,128)(2,1)} %refs_1_.5), channel_id=1, source_target_pairs={{0,8},{2,10},{4,12},{6,14},{8,0},{10,2},{12,4},{14,6},{1,9},{3,11}... | collective-permute-start | bytes 393224 | tf_op jit(solution)/shard_map/ppermute | solution.py:160
  5.1 12.8 %collective-permute-start.1 = (bf16[16,4096]{1,0:T(8,128)(2,1)}, bf16[16,4096]{1,0:T(8,128)(2,1)S(1)}, u32[]{:S(2)}, u32[]{:S(2)}) collective-permute-start(bf16[16,4096]{1,0:T(8,128)(2,1)} %refs_1_.5), channel_id=1, source_target_pairs={{0,4},{2,6},{4,0},{6,2},{8,12},{10,14},{12,8},{14,10},{1,5},{3,7},... | collective-permute-start | bytes 393224 | tf_op jit(solution)/shard_map/ppermute | solution.py:160
  5.6 12.8 %collective-permute-start = (bf16[16,4096]{1,0:T(8,128)(2,1)}, bf16[16,4096]{1,0:T(8,128)(2,1)S(1)}, u32[]{:S(2)}, u32[]{:S(2)}) collective-permute-start(bf16[16,4096]{1,0:T(8,128)(2,1)} %refs_1_.5), channel_id=1, source_target_pairs={{0,2},{2,0},{4,6},{6,4},{8,10},{10,8},{12,14},{14,12},{1,3},{3,1},... | collective-permute-start | bytes 393224 | tf_op jit(solution)/shard_map/ppermute | solution.py:160
  9.7 8.7 %collective-permute-start.6 = (bf16[16,4096]{1,0:T(8,128)(2,1)S(1)}, bf16[16,4096]{1,0:T(8,128)(2,1)S(1)}, u32[]{:S(2)}, u32[]{:S(2)}) collective-permute-start(bf16[16,4096]{1,0:T(8,128)(2,1)S(1)} %collective-permute-done.5.refs_9_.refs_7_), channel_id=1, source_target_pairs={{0,2},{2,0},{4,6},{6,4},{8,10},{10,8},{12,14},{14,12},{1,3},{3,1},... | collective-permute-start | bytes 393224 | tf_op jit(solution)/shard_map/ppermute | solution.py:160
  16.3 6.0 %collective-permute-start.4 = (bf16[16,4096]{1,0:T(8,128)(2,1)S(1)}, bf16[16,4096]{1,0:T(8,128)(2,1)S(1)}, u32[]{:S(2)}, u32[]{:S(2)}) collective-permute-start(bf16[16,4096]{1,0:T(8,128)(2,1)S(1)} %collective-permute-done.3.refs_7_.refs_5_), channel_id=1, source_target_pairs={{0,2},{2,0},{4,6},{6,4},{8,10},{10,8},{12,14},{14,12},{1,3},{3,1},... | collective-permute-start | bytes 393224 | tf_op jit(solution)/shard_map/ppermute | solution.py:160
  17.8 5.9 %collective-permute-start.2 = (bf16[16,4096]{1,0:T(8,128)(2,1)S(1)}, bf16[16,4096]{1,0:T(8,128)(2,1)S(1)}, u32[]{:S(2)}, u32[]{:S(2)}) collective-permute-start(bf16[16,4096]{1,0:T(8,128)(2,1)S(1)} %collective-permute-done.1.refs_5_.refs_3_), channel_id=1, source_target_pairs={{0,2},{2,0},{4,6},{6,4},{8,10},{10,8},{12,14},{14,12},{1,3},{3,1},... | collective-permute-start | bytes 393224 | tf_op jit(solution)/shard_map/ppermute | solution.py:160
  23.7 0.9 %copy-start.1 = (bf16[16,4096]{1,0:T(8,128)(2,1)S(1)}, bf16[16,4096]{1,0:T(8,128)(2,1)}, u32[]{:S(2)}) copy-start(bf16[16,4096]{1,0:T(8,128)(2,1)} %refs_1_.5) | copy-start | bytes 393220
  24.6 1.0 %copy-start.5 = (bf16[1,64,4096]{2,1,0:T(8,128)(2,1)S(1)}, bf16[1,64,4096]{2,1,0:T(8,128)(2,1)}, u32[]{:S(2)}) copy-start(bf16[1,64,4096]{2,1,0:T(8,128)(2,1)} %param.9) | copy-start | bytes 1572868
  25.6 0.7 %copy-start.6 = (s32[8]{0:T(128)S(1)}, s32[8]{0:T(128)}, u32[]{:S(2)}) copy-start(s32[8]{0:T(128)} %index_map.1) | copy-start | bytes 100
  26.3 0.7 %copy-start.8 = (s32[128,1]{0,1:T(1,128)S(1)}, s32[128,1]{0,1:T(1,128)}, u32[]{:S(2)}) copy-start(s32[128,1]{0,1:T(1,128)} %param.12) | copy-start | bytes 1540
  28.1 1.2 %collective-permute-start.7 = (f32[32,64]{1,0:T(8,128)S(1)}, f32[32,64]{1,0:T(8,128)S(1)}, u32[]{:S(2)}, u32[]{:S(2)}) collective-permute-start(f32[32,64]{1,0:T(8,128)S(1)} %lowrank.1.low_a), channel_id=1, source_target_pairs={{0,1},{1,0},{2,3},{3,2},{4,5},{5,4},{6,7},{7,6},{8,9},{9,8},{10,11... | collective-permute-start | bytes 24584 | tf_op jit(solution)/shard_map/ppermute | solution.py:180
  29.3 1.5 %copy-start = (bf16[1,64,8,1,1792]{4,2,3,1,0:T(8,128)(2,1)S(1)}, bf16[1,64,8,1,1792]{4,2,3,1,0:T(8,128)(2,1)}, u32[]{:S(2)}) copy-start(bf16[1,64,8,1,1792]{4,2,3,1,0:T(8,128)(2,1)} %param.10) | copy-start | bytes 5505028
  32.5 27.8 %all-to-all-start = ((bf16[8,32,1792]{2,1,0:T(8,128)(2,1)}), bf16[8,32,1792]{2,1,0:T(8,128)(2,1)S(1)}, u32[]{:S(2)}, u32[]{:S(2)}) async-start(bf16[8,32,1792]{2,1,0:T(8,128)(2,1)} %bitcast.6), calls=%async_computation | async-start | bytes 1835008 | tf_op jit(solution)/shard_map/all_to_all | solution.py:192
  37.1 0.9 %copy-start.2 = (bf16[16,4096]{1,0:T(8,128)(2,1)S(1)}, bf16[16,4096]{1,0:T(8,128)(2,1)}, u32[]{:S(2)}) copy-start(bf16[16,4096]{1,0:T(8,128)(2,1)} %refs_1_.5) | copy-start | bytes 393220
  38.0 22.3 %copy-start.7 = (s32[8]{0:T(128)S(1)}, s32[8]{0:T(128)}, u32[]{:S(2)}) copy-start(s32[8]{0:T(128)} %index_map.1) | copy-start | bytes 100
  38.0 22.3 %copy-start.9 = (s32[128,1]{0,1:T(1,128)S(1)}, s32[128,1]{0,1:T(1,128)}, u32[]{:S(2)}) copy-start(s32[128,1]{0,1:T(1,128)} %param.12) | copy-start | bytes 1540
  47.0 9.2 %collective-permute-start.8 = (f32[128,1792]{1,0:T(8,128)S(1)}, f32[128,1792]{1,0:T(8,128)S(1)}, u32[]{:S(2)}, u32[]{:S(2)}) collective-permute-start(f32[128,1792]{1,0:T(8,128)S(1)} %base.2.refs_10_), channel_id=1, source_target_pairs={{0,1},{1,0},{2,3},{3,2},{4,5},{5,4},{6,7},{7,6},{8,9},{9,8},{10,11... | collective-permute-start | bytes 2752520 | tf_op jit(solution)/shard_map/ppermute | solution.py:220
  56.3 1.0 %copy-start.3 = (f32[128,1792]{1,0:T(8,128)}, f32[128,1792]{1,0:T(8,128)S(1)}, u32[]{:S(2)}) copy-start(f32[128,1792]{1,0:T(8,128)S(1)} %collective-permute-done.8.other) | copy-start | bytes 2752516
  60.3 1.2 %copy-start.4 = (f32[128,1792]{1,0:T(8,128)S(1)}, f32[128,1792]{1,0:T(8,128)}, u32[]{:S(2)}) copy-start(f32[128,1792]{1,0:T(8,128)} %copy-done.3) | copy-start | bytes 2752516

commit v2 on v1

--- a/solution.py
+++ b/solution.py
@@ -12,6 +12,7 @@
 BF16 = jnp.bfloat16
 VMEM = pl.BlockSpec(memory_space=pltpu.VMEM)
 SMEM = pl.BlockSpec(memory_space=pltpu.SMEM)
+ANY = pl.BlockSpec(memory_space=pl.ANY)
 
 
 def slot_layout(adapter_per_row, storage_index_map, owner_indices, slot_depth):
@@ -79,16 +80,31 @@
     return stored * CAP + within.astype(jnp.int32)
 
 
+def first_kernel(
+    index_map, adapter, tokens, down, up, slot, tokens_here, down_here, up_here, arrival
+):
+    copies = [
+        pltpu.make_async_copy(tokens, tokens_here, arrival.at[0]),
+        pltpu.make_async_copy(down, down_here, arrival.at[1]),
+        pltpu.make_async_copy(up, up_here, arrival.at[2]),
+    ]
+    for copy in copies:
+        copy.start()
+    slot[...] = slots_as_row(adapter, index_map)
+    for copy in copies:
+        copy.wait()
+
+
 def lowrank_kernel(groups, *refs):
-    where, index_map, adapter = refs[:3]
-    pieces = refs[3 : 3 + groups]
-    down, out, gathered = refs[3 + groups :]
+    where, slots = refs[:2]
+    pieces = refs[2 : 2 + groups]
+    down, out, gathered = refs[2 + groups :]
     me = where[0]
     part = pieces[0].shape[0]
     for d in range(groups):
         start = pl.multiple_of((me ^ d) * part, part)
         gathered[pl.ds(start, part), :] = pieces[d][...]
-    slot = slots_as_row(adapter, index_map)
+    slot = slots[...]
     rows = slot.shape[1]
     mine = lax.broadcasted_iota(jnp.int32, (CAP, rows), 0) + me * CAP
     chosen = (slot == mine).astype(F32).astype(BF16)
@@ -114,24 +130,42 @@
     out[...] = result.astype(BF16)
 
 
-def base_kernel(groups, *refs):
+def base_kernel(groups, tile, slots, *refs):
     where = refs[0]
     pieces = refs[1 : 1 + groups]
-    weight, _, out, gathered = refs[1 + groups :]
-    me = where[0]
+    weight, _, partner, own, gathered, held, arrival = refs[1 + groups :]
+    me, core = where[0], where[1]
     part = pieces[0].shape[0]
-
-    @pl.when(pl.program_id(0) == 0)
-    def _():
-        for d in range(groups):
-            start = pl.multiple_of((me ^ d) * part, part)
-            gathered[pl.ds(start, part), :] = pieces[d][...]
-
-    out[...] = jnp.dot(gathered[...], weight[...], preferred_element_type=F32)
-
-
-def final_kernel(groups, index_map, adapter, own, other, arrived, out):
-    slot = slots_as_row(adapter, index_map)
+    width = own.shape[1]
+    count = width // tile
+
+    def fetch(step):
+        half = 1 - core if step < count else core
+        start = half * width + (step % count) * tile
+        return pltpu.make_async_copy(
+            weight.at[:, pl.ds(pl.multiple_of(start, 128), tile)],
+            held.at[step % slots],
+            arrival.at[step % slots],
+        )
+
+    for step in range(slots - 1):
+        fetch(step).start()
+    for d in range(groups):
+        start = pl.multiple_of((me ^ d) * part, part)
+        gathered[pl.ds(start, part), :] = pieces[d][...]
+    for step in range(2 * count):
+        if step + slots - 1 < 2 * count:
+            fetch(step + slots - 1).start()
+        fetch(step).wait()
+        out = partner if step < count else own
+        start = (step % count) * tile
+        out[:, start : start + tile] = jnp.dot(
+            gathered[...], held[step % slots], preferred_element_type=F32
+        )
+
+
+def final_kernel(groups, slots, own, other, arrived, out):
+    slot = slots[...]
     rows = slot.shape[1]
     place = (
         slot == lax.broadcasted_iota(jnp.int32, (groups * CAP, rows), 0)
@@ -159,24 +193,42 @@
     def to(x, d):
         return lax.ppermute(x, "rows", [(i, i ^ d) for i in range(groups)])
 
-    pieces = {0: tokens}
+    def params(limit):
+        return pltpu.CompilerParams(vmem_limit_bytes=limit << 20)
+
+    slot, tokens_here, down_here, up_here = pl.pallas_call(
+        first_kernel,
+        out_shape=[
+            jax.ShapeDtypeStruct((1, rows), jnp.int32),
+            jax.ShapeDtypeStruct((part, depth), BF16),
+            jax.ShapeDtypeStruct((rank, depth), BF16),
+            jax.ShapeDtypeStruct((rank * groups, width), BF16),
+        ],
+        in_specs=[SMEM, VMEM] + [ANY] * 3,
+        out_specs=[VMEM] * 4,
+        scratch_shapes=[pltpu.SemaphoreType.DMA((3,))],
+        compiler_params=params(48),
+        cost_estimate=pl.CostEstimate(flops=10**6, bytes_accessed=5 * 10**6, transcendentals=0),
+        name="first",
+    )(storage_index_map, adapter, tokens, down_panels[0], up_panels.reshape(rank * groups, width))
+
+    pieces = {0: tokens_here}
     for d in range(2, groups, 2):
         pieces[d] = to(tokens, d)
-    if groups > 1:
-        for d in range(0, groups, 2):
-            pieces[d + 1] = to(pieces[d], 1)
+    for d in range(0, groups, 2):
+        pieces[d + 1] = to(pieces[d], 1)
     pieces = [pieces[d] for d in range(groups)]
 
     low = pl.pallas_call(
         functools.partial(lowrank_kernel, groups),
         out_shape=jax.ShapeDtypeStruct((CAP, rank), F32),
-        in_specs=[SMEM, SMEM, VMEM] + [VMEM] * groups + [VMEM],
+        in_specs=[SMEM, VMEM] + [VMEM] * groups + [VMEM],
         out_specs=VMEM,
         scratch_shapes=[pltpu.VMEM((rows, depth), BF16)],
-        compiler_params=pltpu.CompilerParams(vmem_limit_bytes=16 << 20),
+        compiler_params=params(8),
         cost_estimate=pl.CostEstimate(flops=10**8, bytes_accessed=2 * 10**6, transcendentals=0),
         name="lowrank",
-    )(where, storage_index_map, adapter, *pieces, down_panels[0])
+    )(where, slot, *pieces, down_here)
     low_other = lax.ppermute(low, "tp", swap)
 
     deltas = pl.pallas_call(
@@ -185,50 +237,41 @@
         in_specs=[SMEM, VMEM, VMEM, VMEM],
         out_specs=VMEM,
         scratch_shapes=[pltpu.VMEM((groups * CAP, rank * groups), BF16)],
-        compiler_params=pltpu.CompilerParams(vmem_limit_bytes=32 << 20),
+        compiler_params=params(8),
         cost_estimate=pl.CostEstimate(flops=5 * 10**8, bytes_accessed=3 * 10**6, transcendentals=0),
         name="delta",
-    )(adapter_scales, low, low_other, up_panels.reshape(rank * groups, width))
+    )(adapter_scales, low, low_other, up_here)
     arrived = lax.all_to_all(deltas, "rows", split_axis=0, concat_axis=0, tiled=True)
 
-    tile = 256
-
-    def base(which, after):
-        steps = width // tile
-        return pl.pallas_call(
-            functools.partial(base_kernel, groups),
-            grid_spec=pltpu.PrefetchScalarGridSpec(
-                num_scalar_prefetch=1,
-                grid=(steps,),
-                in_specs=[pl.BlockSpec((part, depth), lambda i, s: (0, 0))] * groups
-                + [pl.BlockSpec((depth, tile), lambda i, s: (0, s[1] * steps + i))]
-                + [pl.BlockSpec(memory_space=pl.ANY)],
-                out_specs=pl.BlockSpec((rows, tile), lambda i, s: (0, i)),
-                scratch_shapes=[pltpu.VMEM((rows, depth), BF16)],
-            ),
-            out_shape=jax.ShapeDtypeStruct((rows, width), F32),
-            compiler_params=pltpu.CompilerParams(vmem_limit_bytes=32 << 20),
-            cost_estimate=pl.CostEstimate(
-                flops=rows * depth,
-                bytes_accessed=2 * depth,
-                transcendentals=0,
-            ),
-            name="base",
-        )(jnp.stack([me, which]), *pieces, gate_weight, after)
-
-    partner = base(1 - core, deltas)
+    tile, buffers = 256, 5
+    half = jax.ShapeDtypeStruct((rows, width), F32)
+    partner, own = pl.pallas_call(
+        functools.partial(base_kernel, groups, tile, buffers),
+        in_specs=[SMEM] + [VMEM] * groups + [ANY, ANY],
+        out_specs=[VMEM, VMEM],
+        scratch_shapes=[
+            pltpu.VMEM((rows, depth), BF16),
+            pltpu.VMEM((buffers, depth, tile), BF16),
+            pltpu.SemaphoreType.DMA((buffers,)),
+        ],
+        out_shape=[half, half],
+        compiler_params=params(40),
+        cost_estimate=pl.CostEstimate(
+            flops=4 * rows * depth * width, bytes_accessed=10**7, transcendentals=0
+        ),
+        name="base",
+    )(jnp.stack([me, core]), *pieces, gate_weight, deltas)
     other = lax.ppermute(partner, "tp", swap)
-    own = base(core, partner)
 
     return pl.pallas_call(
         functools.partial(final_kernel, groups),
         out_shape=jax.ShapeDtypeStruct((rows, width), BF16),
-        in_specs=[SMEM, VMEM, VMEM, VMEM, VMEM],
+        in_specs=[VMEM, VMEM, VMEM, VMEM],
         out_specs=VMEM,
-        compiler_params=pltpu.CompilerParams(vmem_limit_bytes=32 << 20),
+        compiler_params=params(8),
         cost_estimate=pl.CostEstimate(flops=2 * 10**8, bytes_accessed=4 * 10**6, transcendentals=0),
         name="combine",
-    )(storage_index_map, adapter, own, other, arrived)
+    )(slot, own, other, arrived)
 
 
 def on_device(*args):

time: 63.8 us -> 58.4 us (0.915)
  Pallas kernels: 22.8 us -> 16.2 us
  waiting for transfers between devices: 16.2 us -> 20.8 us
  local copies, waits for them, and re-layouts: 7.8 us -> 4.75 us
    all_to_all x1, waiting for transfers between devices: 3.05 us -> 8.81 us  [few_groups(): lax.all_to_all(deltas, 'rows', split_axis=0, concat_axis=0, tiled=True)]
    pallas_call x2, Pallas kernels: 18.1 us -> 12.9 us  [the longest x1 11.9 us: few_groups(): pl.pallas_call(functools.partial(base_kernel, groups, tile, buffers), in_...]
    ppermute x7, waiting for transfers between devices: 12.6 us -> 9.05 us  [to(): return lax.ppermute(x, 'rows', [(i, i ^ d) for i in range(groups)])]
    unnamed x20 -> x10, local copies, waits for them, and re-layouts: 7.8 us -> 4.75 us
    ppermute x1, waiting for transfers between devices: 0.01 us -> 2.46 us  [few_groups(): other = lax.ppermute(partner, 'tp', swap)]
    ppermute x7, starting transfers between devices: 11.1 us -> 9.73 us  [to(): return lax.ppermute(x, 'rows', [(i, i ^ d) for i in range(groups)])]
    all_to_all x1, starting transfers between devices: 4.49 us -> 5.74 us  [few_groups(): lax.all_to_all(deltas, 'rows', split_axis=0, concat_axis=0, tiled=True)]
    pallas_call x1, Pallas kernels: 1.81 us -> 1.09 us  [few_groups(): pl.pallas_call(functools.partial(final_kernel, groups), out_shape=jax.Sha...]
  transfers between devices with their start and end apart: 10 -> 10, of which waited for: 6 -> 7; matrix products, arithmetic and copies ran while one was open for 0% -> 0% of each run, Pallas kernels for 29% -> 22%
where the time goes in v2:
time: 58.4 us; the launch traced here: 58.1 us
  waiting for transfers between devices  20.8 us (36%)
  Pallas kernels  16.2 us (28%)
  starting transfers between devices  15.6 us (27%)
  local copies, waits for them, and re-layouts  4.75 us (8%)
  between operations  0.71 us (1%)
    pallas_call x1, Pallas kernels, few_groups(): pl.pallas_call(functools.partial(base_kernel, groups, tile, buffers), in_...  11.9 us
    ppermute x7, starting transfers between devices, to(): return lax.ppermute(x, 'rows', [(i, i ^ d) for i in range(groups)])  9.73 us
    ppermute x7, waiting for transfers between devices, to(): return lax.ppermute(x, 'rows', [(i, i ^ d) for i in range(groups)])  9.05 us
    all_to_all x1, waiting for transfers between devices, few_groups(): lax.all_to_all(deltas, 'rows', split_axis=0, concat_axis=0, tiled=True)  8.81 us
    all_to_all x1, starting transfers between devices, few_groups(): lax.all_to_all(deltas, 'rows', split_axis=0, concat_axis=0, tiled=True)  5.74 us
    unnamed x10, local copies, waits for them, and re-layouts  4.75 us
    ppermute x1, waiting for transfers between devices, few_groups(): other = lax.ppermute(partner, 'tp', swap)  2.46 us
    pallas_call x1, Pallas kernels, few_groups(): pl.pallas_call(functools.partial(delta_kernel, groups), out_shape=jax.Sha...  1.66 us
  transfers between devices with their start and end apart: 10, of which 7 were waited for; matrix products, arithmetic and copies ran while one was open for 0% of the time, Pallas kernels for 22%

profile of v2, /device:TPU:0, one launch (start us, length us, event | category | flops | bytes accessed | tf_op | source)
XLA Modules:
  0.0 58.1 jit_solution(7385986234719336811)
XLA Ops:
  0.0 3.0 %collective-permute-start.1 = (bf16[16,4096]{1,0:T(8,128)(2,1)}, bf16[16,4096]{1,0:T(8,128)(2,1)S(1)}, u32[]{:S(2)}, u32[]{:S(2)}) collective-permute-start(bf16[16,4096]{1,0:T(8,128)(2,1)} %tokens.1), channel_id=1, source_target_pairs={{0,4},{2,6},{4,0},{6,2},{8,12},{10,14},{12,8},{14,10},{1,5},{3,7},... | collective-permute-start | bytes 393224 | tf_op jit(solution)/shard_map/ppermute | solution.py:194
  3.0 2.6 %collective-permute-start.3 = (bf16[16,4096]{1,0:T(8,128)(2,1)}, bf16[16,4096]{1,0:T(8,128)(2,1)S(1)}, u32[]{:S(2)}, u32[]{:S(2)}) collective-permute-start(bf16[16,4096]{1,0:T(8,128)(2,1)} %tokens.1), channel_id=1, source_target_pairs={{0,8},{2,10},{4,12},{6,14},{8,0},{10,2},{12,4},{14,6},{1,9},{3,11}... | collective-permute-start | bytes 393224 | tf_op jit(solution)/shard_map/ppermute | solution.py:194
  5.6 0.0 collective-permute-start.5
  5.6 0.0 copy-start
  5.6 1.5 %copy-done = bf16[1,64,8,1,1792]{4,2,3,1,0:T(8,128)(2,1)S(1)} copy-done((bf16[1,64,8,1,1792]{4,2,3,1,0:T(8,128)(2,1)S(1)}, bf16[1,64,8,1,1792]{4,2,3,1,0:T(8,128)(2,1)}, u32[]{:S(2)}) %copy-start) | copy-done | bytes 1835032
  7.1 1.0 %copy-done.1 = bf16[1,64,4096]{2,1,0:T(8,128)(2,1)S(1)} copy-done((bf16[1,64,4096]{2,1,0:T(8,128)(2,1)S(1)}, bf16[1,64,4096]{2,1,0:T(8,128)(2,1)}, u32[]{:S(2)}) %copy-start.1) | copy-done | bytes 524312
  8.2 0.9 %copy-done.2 = bf16[16,4096]{1,0:T(8,128)(2,1)S(1)} copy-done((bf16[16,4096]{1,0:T(8,128)(2,1)S(1)}, bf16[16,4096]{1,0:T(8,128)(2,1)}, u32[]{:S(2)}) %copy-start.2) | copy-done | bytes 131096
  9.1 0.7 %copy-done.3 = s32[8]{0:T(128)S(1)} copy-done((s32[8]{0:T(128)S(1)}, s32[8]{0:T(128)}, u32[]{:S(2)}) %copy-start.3) | copy-done | bytes 56
  9.7 0.7 %copy-done.4 = s32[128,1]{0,1:T(1,128)S(1)} copy-done((s32[128,1]{0,1:T(1,128)S(1)}, s32[128,1]{0,1:T(1,128)}, u32[]{:S(2)}) %copy-start.4) | copy-done | bytes 536
  10.4 1.0 %first.1 = (s32[1,128]{1,0:T(1,128)S(1)}, bf16[16,4096]{1,0:T(8,128)(2,1)S(1)}, bf16[64,4096]{1,0:T(8,128)(2,1)S(1)}, bf16[512,1792]{1,0:T(8,128)(2,1)S(1)}) custom-call(s32[8]{0:T(128)S(1)} %copy-done.3, s32[1,128]{1,0:T(1,128)S(1)} %bitcast.10, bf16[16,4096]{1,0:T(8,128)(2,1)S(1)} %copy-done.2, bf16[64,4096]{1,0:T(8,128)(2,1)S(1)} %bitcast.9, ...), custom_call_target="tpu_custom_call" | custom-call | flops 1000000 | bytes 5000000 | tf_op jit(solution)/shard_map/first/pallas_call | solution.py:199
  11.4 1.8 %collective-permute-start = (bf16[16,4096]{1,0:T(8,128)(2,1)S(1)}, bf16[16,4096]{1,0:T(8,128)(2,1)S(1)}, u32[]{:S(2)}, u32[]{:S(2)}) collective-permute-start(bf16[16,4096]{1,0:T(8,128)(2,1)S(1)} %get-tuple-element.12.refs_2_.refs_1_), channel_id=1, source_target_pairs={{0,2},{2,0},{4,6},{6,4},{8,10},{10,8},{12,14},{14,12},{1,3},{3,1},... | collective-permute-start | bytes 393224 | tf_op jit(solution)/shard_map/ppermute | solution.py:194
  13.2 0.0 collective-permute-done.1.refs_4_.refs_3_
  13.2 0.3 collective-permute-start.2
  13.5 2.7 %collective-permute-done.3.refs_6_.refs_5_ = bf16[16,4096]{1,0:T(8,128)(2,1)S(1)} collective-permute-done((bf16[16,4096]{1,0:T(8,128)(2,1)}, bf16[16,4096]{1,0:T(8,128)(2,1)S(1)}, u32[]{:S(2)}, u32[]{:S(2)}) %collective-permute-start.3) | collective-permute-done | bytes 131104 | tf_op jit(solution)/shard_map/ppermute | solution.py:194
  16.2 1.5 %collective-permute-start.4 = (bf16[16,4096]{1,0:T(8,128)(2,1)S(1)}, bf16[16,4096]{1,0:T(8,128)(2,1)S(1)}, u32[]{:S(2)}, u32[]{:S(2)}) collective-permute-start(bf16[16,4096]{1,0:T(8,128)(2,1)S(1)} %collective-permute-done.3.refs_6_.refs_5_), channel_id=1, source_target_pairs={{0,2},{2,0},{4,6},{6,4},{8,10},{10,8},{12,14},{14,12},{1,3},{3,1},... | collective-permute-start | bytes 393224 | tf_op jit(solution)/shard_map/ppermute | solution.py:194
  17.7 0.0 collective-permute-done.5.refs_8_.refs_7_
  17.7 0.5 collective-permute-start.6
  18.2 0.0 collective-permute-done.refs_3_.refs_2_
  18.2 2.5 %collective-permute-done.2.refs_5_.refs_4_ = bf16[16,4096]{1,0:T(8,128)(2,1)S(1)} collective-permute-done((bf16[16,4096]{1,0:T(8,128)(2,1)S(1)}, bf16[16,4096]{1,0:T(8,128)(2,1)S(1)}, u32[]{:S(2)}, u32[]{:S(2)}) %collective-permute-start.2) | collective-permute-done | bytes 131104 | tf_op jit(solution)/shard_map/ppermute | solution.py:194
  20.7 2.5 %collective-permute-done.4.refs_7_.refs_6_ = bf16[16,4096]{1,0:T(8,128)(2,1)S(1)} collective-permute-done((bf16[16,4096]{1,0:T(8,128)(2,1)S(1)}, bf16[16,4096]{1,0:T(8,128)(2,1)S(1)}, u32[]{:S(2)}, u32[]{:S(2)}) %collective-permute-start.4) | collective-permute-done | bytes 131104 | tf_op jit(solution)/shard_map/ppermute | solution.py:194
  23.2 1.4 %collective-permute-done.6.refs_9_.refs_8_ = bf16[16,4096]{1,0:T(8,128)(2,1)S(1)} collective-permute-done((bf16[16,4096]{1,0:T(8,128)(2,1)S(1)}, bf16[16,4096]{1,0:T(8,128)(2,1)S(1)}, u32[]{:S(2)}, u32[]{:S(2)}) %collective-permute-start.6) | collective-permute-done | bytes 131104 | tf_op jit(solution)/shard_map/ppermute | solution.py:194
  24.6 0.6 lowrank.1.low_a
  25.2 0.0 collective-permute-start.7
  25.8 0.5 collective-permute-done.7.low_b
  26.4 1.7 %delta.1.refs_10_ = bf16[256,1792]{1,0:T(8,128)(2,1)} custom-call(f32[1]{0:T(128)S(6)} %copy.8.scale, f32[32,64]{1,0:T(8,128)S(1)} %lowrank.1.low_a, f32[32,64]{1,0:T(8,128)S(1)} %collective-permute-done.7.low_b, bf16[512,1792]{1,0:T(8,128)(2,1)S(1)} %get-tuple-element.14.up), custom_call_target="tpu_custom_call" | custom-call | flops 500000000 | bytes 3000000 | tf_op jit(solution)/shard_map/delta/pallas_call | solution.py:234
  28.0 5.7 %all-to-all-start = ((bf16[8,32,1792]{2,1,0:T(8,128)(2,1)}), bf16[8,32,1792]{2,1,0:T(8,128)(2,1)S(1)}, u32[]{:S(2)}, u32[]{:S(2)}) async-start(bf16[8,32,1792]{2,1,0:T(8,128)(2,1)} %bitcast.5), calls=%async_computation | async-start | bytes 1835008 | tf_op jit(solution)/shard_map/all_to_all | solution.py:244
  33.8 0.1 pad_add_fusion.refs_0_
  33.8 11.9 %base.1 = (f32[128,1792]{1,0:T(8,128)S(1)}, f32[128,1792]{1,0:T(8,128)S(1)}) custom-call(s32[2]{0:T(128)S(1)} %pad_add_fusion.refs_0_, bf16[16,4096]{1,0:T(8,128)(2,1)S(1)} %get-tuple-element.12.refs_2_.refs_1_, bf16[16,4096]{1,0:T(8,128)(2,1)S(1)} %collective-permute-done.refs_3_.refs_2_, bf16[16,4096]{1,0:T(8,128)(2,1)S(1)} %collective-permute-done.1.refs_4_.refs_3_, ...), custom_call_target="tpu_custom_call" | custom-call | flops 3758096384 | bytes 10000000 | tf_op jit(solution)/shard_map/base/pallas_call | solution.py:248
  45.7 0.1 collective-permute-start.8
  45.8 2.5 %collective-permute-done.8.other = f32[128,1792]{1,0:T(8,128)S(1)} collective-permute-done((f32[128,1792]{1,0:T(8,128)S(1)}, f32[128,1792]{1,0:T(8,128)S(1)}, u32[]{:S(2)}, u32[]{:S(2)}) %collective-permute-start.8) | collective-permute-done | bytes 917536 | tf_op jit(solution)/shard_map/ppermute | solution.py:264
  48.2 8.8 %all-to-all-done = bf16[8,32,1792]{2,1,0:T(8,128)(2,1)S(1)} async-done(((bf16[8,32,1792]{2,1,0:T(8,128)(2,1)}), bf16[8,32,1792]{2,1,0:T(8,128)(2,1)S(1)}, u32[]{:S(2)}, u32[]{:S(2)}) %all-to-all-start) | async-done | bytes 917536 | tf_op jit(solution)/shard_map/all_to_all | solution.py:244
  57.1 1.1 %combine.1 = bf16[128,1792]{1,0:T(8,128)(2,1)} custom-call(s32[1,128]{1,0:T(1,128)S(1)} %get-tuple-element.11.refs_1_.slots, f32[128,1792]{1,0:T(8,128)S(1)} %get-tuple-element.15.own, f32[128,1792]{1,0:T(8,128)S(1)} %collective-permute-done.8.other, bf16[256,1792]{1,0:T(8,128)(2,1)S(1)} %bitcast.7), custom_call_target="tpu_custom_call" | custom-call | flops 200000000 | bytes 4000000 | tf_op jit(solution)/shard_map/combine/pallas_call | solution.py:266
  (4 shorter events, 0.0 us)
Async XLA Ops:
  0.0 13.2 %collective-permute-start.1 = (bf16[16,4096]{1,0:T(8,128)(2,1)}, bf16[16,4096]{1,0:T(8,128)(2,1)S(1)}, u32[]{:S(2)}, u32[]{:S(2)}) collective-permute-start(bf16[16,4096]{1,0:T(8,128)(2,1)} %tokens.1), channel_id=1, source_target_pairs={{0,4},{2,6},{4,0},{6,2},{8,12},{10,14},{12,8},{14,10},{1,5},{3,7},... | collective-permute-start | bytes 393224 | tf_op jit(solution)/shard_map/ppermute | solution.py:194
  3.0 13.2 %collective-permute-start.3 = (bf16[16,4096]{1,0:T(8,128)(2,1)}, bf16[16,4096]{1,0:T(8,128)(2,1)S(1)}, u32[]{:S(2)}, u32[]{:S(2)}) collective-permute-start(bf16[16,4096]{1,0:T(8,128)(2,1)} %tokens.1), channel_id=1, source_target_pairs={{0,8},{2,10},{4,12},{6,14},{8,0},{10,2},{12,4},{14,6},{1,9},{3,11}... | collective-permute-start | bytes 393224 | tf_op jit(solution)/shard_map/ppermute | solution.py:194
  5.6 12.1 %collective-permute-start.5 = (bf16[16,4096]{1,0:T(8,128)(2,1)}, bf16[16,4096]{1,0:T(8,128)(2,1)S(1)}, u32[]{:S(2)}, u32[]{:S(2)}) collective-permute-start(bf16[16,4096]{1,0:T(8,128)(2,1)} %tokens.1), channel_id=1, source_target_pairs={{0,12},{2,14},{4,8},{6,10},{8,4},{10,6},{12,0},{14,2},{1,13},{3,15... | collective-permute-start | bytes 393224 | tf_op jit(solution)/shard_map/ppermute | solution.py:194
  5.6 1.5 %copy-start = (bf16[1,64,8,1,1792]{4,2,3,1,0:T(8,128)(2,1)S(1)}, bf16[1,64,8,1,1792]{4,2,3,1,0:T(8,128)(2,1)}, u32[]{:S(2)}) copy-start(bf16[1,64,8,1,1792]{4,2,3,1,0:T(8,128)(2,1)} %param.10) | copy-start | bytes 5505028
  7.1 1.0 %copy-start.1 = (bf16[1,64,4096]{2,1,0:T(8,128)(2,1)S(1)}, bf16[1,64,4096]{2,1,0:T(8,128)(2,1)}, u32[]{:S(2)}) copy-start(bf16[1,64,4096]{2,1,0:T(8,128)(2,1)} %param.9) | copy-start | bytes 1572868
  8.2 0.9 %copy-start.2 = (bf16[16,4096]{1,0:T(8,128)(2,1)S(1)}, bf16[16,4096]{1,0:T(8,128)(2,1)}, u32[]{:S(2)}) copy-start(bf16[16,4096]{1,0:T(8,128)(2,1)} %tokens.1) | copy-start | bytes 393220
  9.1 0.7 %copy-start.3 = (s32[8]{0:T(128)S(1)}, s32[8]{0:T(128)}, u32[]{:S(2)}) copy-start(s32[8]{0:T(128)} %index_map.1) | copy-start | bytes 100
  9.7 0.7 %copy-start.4 = (s32[128,1]{0,1:T(1,128)S(1)}, s32[128,1]{0,1:T(1,128)}, u32[]{:S(2)}) copy-start(s32[128,1]{0,1:T(1,128)} %param.12) | copy-start | bytes 1540
  11.4 6.8 %collective-permute-start = (bf16[16,4096]{1,0:T(8,128)(2,1)S(1)}, bf16[16,4096]{1,0:T(8,128)(2,1)S(1)}, u32[]{:S(2)}, u32[]{:S(2)}) collective-permute-start(bf16[16,4096]{1,0:T(8,128)(2,1)S(1)} %get-tuple-element.12.refs_2_.refs_1_), channel_id=1, source_target_pairs={{0,2},{2,0},{4,6},{6,4},{8,10},{10,8},{12,14},{14,12},{1,3},{3,1},... | collective-permute-start | bytes 393224 | tf_op jit(solution)/shard_map/ppermute | solution.py:194
  13.2 7.5 %collective-permute-start.2 = (bf16[16,4096]{1,0:T(8,128)(2,1)S(1)}, bf16[16,4096]{1,0:T(8,128)(2,1)S(1)}, u32[]{:S(2)}, u32[]{:S(2)}) collective-permute-start(bf16[16,4096]{1,0:T(8,128)(2,1)S(1)} %collective-permute-done.1.refs_4_.refs_3_), channel_id=1, source_target_pairs={{0,2},{2,0},{4,6},{6,4},{8,10},{10,8},{12,14},{14,12},{1,3},{3,1},... | collective-permute-start | bytes 393224 | tf_op jit(solution)/shard_map/ppermute | solution.py:194
  16.2 7.0 %collective-permute-start.4 = (bf16[16,4096]{1,0:T(8,128)(2,1)S(1)}, bf16[16,4096]{1,0:T(8,128)(2,1)S(1)}, u32[]{:S(2)}, u32[]{:S(2)}) collective-permute-start(bf16[16,4096]{1,0:T(8,128)(2,1)S(1)} %collective-permute-done.3.refs_6_.refs_5_), channel_id=1, source_target_pairs={{0,2},{2,0},{4,6},{6,4},{8,10},{10,8},{12,14},{14,12},{1,3},{3,1},... | collective-permute-start | bytes 393224 | tf_op jit(solution)/shard_map/ppermute | solution.py:194
  17.7 6.9 %collective-permute-start.6 = (bf16[16,4096]{1,0:T(8,128)(2,1)S(1)}, bf16[16,4096]{1,0:T(8,128)(2,1)S(1)}, u32[]{:S(2)}, u32[]{:S(2)}) collective-permute-start(bf16[16,4096]{1,0:T(8,128)(2,1)S(1)} %collective-permute-done.5.refs_8_.refs_7_), channel_id=1, source_target_pairs={{0,2},{2,0},{4,6},{6,4},{8,10},{10,8},{12,14},{14,12},{1,3},{3,1},... | collective-permute-start | bytes 393224 | tf_op jit(solution)/shard_map/ppermute | solution.py:194
  25.2 1.2 %collective-permute-start.7 = (f32[32,64]{1,0:T(8,128)S(1)}, f32[32,64]{1,0:T(8,128)S(1)}, u32[]{:S(2)}, u32[]{:S(2)}) collective-permute-start(f32[32,64]{1,0:T(8,128)S(1)} %lowrank.1.low_a), channel_id=1, source_target_pairs={{0,1},{1,0},{2,3},{3,2},{4,5},{5,4},{6,7},{7,6},{8,9},{9,8},{10,11... | collective-permute-start | bytes 24584 | tf_op jit(solution)/shard_map/ppermute | solution.py:232
  28.0 29.0 %all-to-all-start = ((bf16[8,32,1792]{2,1,0:T(8,128)(2,1)}), bf16[8,32,1792]{2,1,0:T(8,128)(2,1)S(1)}, u32[]{:S(2)}, u32[]{:S(2)}) async-start(bf16[8,32,1792]{2,1,0:T(8,128)(2,1)} %bitcast.5), calls=%async_computation | async-start | bytes 1835008 | tf_op jit(solution)/shard_map/all_to_all | solution.py:244
  45.7 2.5 %collective-permute-start.8 = (f32[128,1792]{1,0:T(8,128)S(1)}, f32[128,1792]{1,0:T(8,128)S(1)}, u32[]{:S(2)}, u32[]{:S(2)}) collective-permute-start(f32[128,1792]{1,0:T(8,128)S(1)} %get-tuple-element.16), channel_id=1, source_target_pairs={{0,1},{1,0},{2,3},{3,2},{4,5},{5,4},{6,7},{7,6},{8,9},{9,8},{10,11... | collective-permute-start | bytes 2752520 | tf_op jit(solution)/shard_map/ppermute | solution.py:264

commit v3 on v2

--- a/solution.py
+++ b/solution.py
@@ -80,19 +80,8 @@
     return stored * CAP + within.astype(jnp.int32)
 
 
-def first_kernel(
-    index_map, adapter, tokens, down, up, slot, tokens_here, down_here, up_here, arrival
-):
-    copies = [
-        pltpu.make_async_copy(tokens, tokens_here, arrival.at[0]),
-        pltpu.make_async_copy(down, down_here, arrival.at[1]),
-        pltpu.make_async_copy(up, up_here, arrival.at[2]),
-    ]
-    for copy in copies:
-        copy.start()
+def slots_kernel(index_map, adapter, slot):
     slot[...] = slots_as_row(adapter, index_map)
-    for copy in copies:
-        copy.wait()
 
 
 def lowrank_kernel(groups, *refs):
@@ -196,23 +185,17 @@
     def params(limit):
         return pltpu.CompilerParams(vmem_limit_bytes=limit << 20)
 
-    slot, tokens_here, down_here, up_here = pl.pallas_call(
-        first_kernel,
-        out_shape=[
-            jax.ShapeDtypeStruct((1, rows), jnp.int32),
-            jax.ShapeDtypeStruct((part, depth), BF16),
-            jax.ShapeDtypeStruct((rank, depth), BF16),
-            jax.ShapeDtypeStruct((rank * groups, width), BF16),
-        ],
-        in_specs=[SMEM, VMEM] + [ANY] * 3,
-        out_specs=[VMEM] * 4,
-        scratch_shapes=[pltpu.SemaphoreType.DMA((3,))],
-        compiler_params=params(48),
-        cost_estimate=pl.CostEstimate(flops=10**6, bytes_accessed=5 * 10**6, transcendentals=0),
-        name="first",
-    )(storage_index_map, adapter, tokens, down_panels[0], up_panels.reshape(rank * groups, width))
-
-    pieces = {0: tokens_here}
+    slot = pl.pallas_call(
+        slots_kernel,
+        out_shape=jax.ShapeDtypeStruct((1, rows), jnp.int32),
+        in_specs=[SMEM, VMEM],
+        out_specs=VMEM,
+        compiler_params=params(2),
+        cost_estimate=pl.CostEstimate(flops=10**11, bytes_accessed=10**8, transcendentals=0),
+        name="slots",
+    )(storage_index_map, adapter)
+
+    pieces = {0: tokens}
     for d in range(2, groups, 2):
         pieces[d] = to(tokens, d)
     for d in range(0, groups, 2):
@@ -228,7 +211,7 @@
         compiler_params=params(8),
         cost_estimate=pl.CostEstimate(flops=10**8, bytes_accessed=2 * 10**6, transcendentals=0),
         name="lowrank",
-    )(where, slot, *pieces, down_here)
+    )(where, slot, *pieces, down_panels[0])
     low_other = lax.ppermute(low, "tp", swap)
 
     deltas = pl.pallas_call(
@@ -240,7 +223,7 @@
         compiler_params=params(8),
         cost_estimate=pl.CostEstimate(flops=5 * 10**8, bytes_accessed=3 * 10**6, transcendentals=0),
         name="delta",
-    )(adapter_scales, low, low_other, up_here)
+    )(adapter_scales, low, low_other, up_panels.reshape(rank * groups, width))
     arrived = lax.all_to_all(deltas, "rows", split_axis=0, concat_axis=0, tiled=True)
 
     tile, buffers = 256, 5

time: 58.4 us -> 55.1 us (0.943)
  local copies, waits for them, and re-layouts: 4.75 us -> 1.32 us
  waiting for transfers between devices: 20.8 us -> 21.4 us
    unnamed x10, local copies, waits for them, and re-layouts: 4.75 us -> 1.32 us
    all_to_all x1, starting transfers between devices: 5.74 us -> 4.39 us  [few_groups(): lax.all_to_all(deltas, 'rows', split_axis=0, concat_axis=0, tiled=True)]
    ppermute x7, starting transfers between devices: 9.73 us -> 11.1 us  [to(): return lax.ppermute(x, 'rows', [(i, i ^ d) for i in range(groups)])]
  transfers between devices with their start and end apart: 10 -> 10, of which waited for: 7 -> 7; matrix products, arithmetic and copies ran while one was open for 0% -> 0% of each run, Pallas kernels for 22% -> 23%
where the time goes in v3:
time: 55.1 us; the launch traced here: 54.9 us
  waiting for transfers between devices  21.4 us (39%)
  Pallas kernels  15.9 us (29%)
  starting transfers between devices  15.5 us (28%)
  local copies, waits for them, and re-layouts  1.32 us (2%)
  between operations  0.71 us (1%)
    pallas_call x1, Pallas kernels, few_groups(): pl.pallas_call(functools.partial(base_kernel, groups, tile, buffers), in_...  11.9 us
    ppermute x7, starting transfers between devices, to(): return lax.ppermute(x, 'rows', [(i, i ^ d) for i in range(groups)])  11.1 us
    ppermute x7, waiting for transfers between devices, to(): return lax.ppermute(x, 'rows', [(i, i ^ d) for i in range(groups)])  9.56 us
    all_to_all x1, waiting for transfers between devices, few_groups(): lax.all_to_all(deltas, 'rows', split_axis=0, concat_axis=0, tiled=True)  8.81 us
    all_to_all x1, starting transfers between devices, few_groups(): lax.all_to_all(deltas, 'rows', split_axis=0, concat_axis=0, tiled=True)  4.39 us
    ppermute x1, waiting for transfers between devices, few_groups(): other = lax.ppermute(partner, 'tp', swap)  2.46 us
    pallas_call x1, Pallas kernels, few_groups(): pl.pallas_call(functools.partial(delta_kernel, groups), out_shape=jax.Sha...  1.67 us
    unnamed x10, local copies, waits for them, and re-layouts  1.32 us
  transfers between devices with their start and end apart: 10, of which 7 were waited for; matrix products, arithmetic and copies ran while one was open for 0% of the time, Pallas kernels for 23%

profile of v3, /device:TPU:0, one launch (start us, length us, event | category | flops | bytes accessed | tf_op | source)
XLA Modules:
  0.0 54.9 jit_solution(9575251941224346761)
XLA Ops:
  0.0 3.0 %collective-permute-start.1 = (bf16[16,4096]{1,0:T(8,128)(2,1)}, bf16[16,4096]{1,0:T(8,128)(2,1)S(1)}, u32[]{:S(2)}, u32[]{:S(2)}) collective-permute-start(bf16[16,4096]{1,0:T(8,128)(2,1)} %refs_1_.1), channel_id=1, source_target_pairs={{0,4},{2,6},{4,0},{6,2},{8,12},{10,14},{12,8},{14,10},{1,5},{3,7},... | collective-permute-start | bytes 393224 | tf_op jit(solution)/shard_map/ppermute | solution.py:183
  3.0 2.6 %collective-permute-start.3 = (bf16[16,4096]{1,0:T(8,128)(2,1)}, bf16[16,4096]{1,0:T(8,128)(2,1)S(1)}, u32[]{:S(2)}, u32[]{:S(2)}) collective-permute-start(bf16[16,4096]{1,0:T(8,128)(2,1)} %refs_1_.1), channel_id=1, source_target_pairs={{0,8},{2,10},{4,12},{6,14},{8,0},{10,2},{12,4},{14,6},{1,9},{3,11}... | collective-permute-start | bytes 393224 | tf_op jit(solution)/shard_map/ppermute | solution.py:183
  5.6 0.0 collective-permute-start.5
  5.6 1.7 %collective-permute-start = (bf16[16,4096]{1,0:T(8,128)(2,1)}, bf16[16,4096]{1,0:T(8,128)(2,1)S(1)}, u32[]{:S(2)}, u32[]{:S(2)}) collective-permute-start(bf16[16,4096]{1,0:T(8,128)(2,1)} %refs_1_.1), channel_id=1, source_target_pairs={{0,2},{2,0},{4,6},{6,4},{8,10},{10,8},{12,14},{14,12},{1,3},{3,1},... | collective-permute-start | bytes 393224 | tf_op jit(solution)/shard_map/ppermute | solution.py:183
  7.3 0.9 %collective-permute-done.1.refs_4_.refs_3_ = bf16[16,4096]{1,0:T(8,128)(2,1)S(1)} collective-permute-done((bf16[16,4096]{1,0:T(8,128)(2,1)}, bf16[16,4096]{1,0:T(8,128)(2,1)S(1)}, u32[]{:S(2)}, u32[]{:S(2)}) %collective-permute-start.1) | collective-permute-done | bytes 131104 | tf_op jit(solution)/shard_map/ppermute | solution.py:183
  8.3 1.7 %collective-permute-start.2 = (bf16[16,4096]{1,0:T(8,128)(2,1)S(1)}, bf16[16,4096]{1,0:T(8,128)(2,1)S(1)}, u32[]{:S(2)}, u32[]{:S(2)}) collective-permute-start(bf16[16,4096]{1,0:T(8,128)(2,1)S(1)} %collective-permute-done.1.refs_4_.refs_3_), channel_id=1, source_target_pairs={{0,2},{2,0},{4,6},{6,4},{8,10},{10,8},{12,14},{14,12},{1,3},{3,1},... | collective-permute-start | bytes 393224 | tf_op jit(solution)/shard_map/ppermute | solution.py:183
  10.0 6.2 %collective-permute-done.3.refs_6_.refs_5_ = bf16[16,4096]{1,0:T(8,128)(2,1)S(1)} collective-permute-done((bf16[16,4096]{1,0:T(8,128)(2,1)}, bf16[16,4096]{1,0:T(8,128)(2,1)S(1)}, u32[]{:S(2)}, u32[]{:S(2)}) %collective-permute-start.3) | collective-permute-done | bytes 131104 | tf_op jit(solution)/shard_map/ppermute | solution.py:183
  16.2 1.5 %collective-permute-start.4 = (bf16[16,4096]{1,0:T(8,128)(2,1)S(1)}, bf16[16,4096]{1,0:T(8,128)(2,1)S(1)}, u32[]{:S(2)}, u32[]{:S(2)}) collective-permute-start(bf16[16,4096]{1,0:T(8,128)(2,1)S(1)} %collective-permute-done.3.refs_6_.refs_5_), channel_id=1, source_target_pairs={{0,2},{2,0},{4,6},{6,4},{8,10},{10,8},{12,14},{14,12},{1,3},{3,1},... | collective-permute-start | bytes 393224 | tf_op jit(solution)/shard_map/ppermute | solution.py:183
  17.7 0.0 collective-permute-done.5.refs_8_.refs_7_
  17.7 0.5 collective-permute-start.6
  18.2 0.7 %copy-done.3 = s32[8]{0:T(128)S(1)} copy-done((s32[8]{0:T(128)S(1)}, s32[8]{0:T(128)}, u32[]{:S(2)}) %copy-start.3) | copy-done | bytes 56
  18.9 0.0 copy-start.4
  18.9 0.7 %copy-done.4 = s32[128,1]{0,1:T(1,128)S(1)} copy-done((s32[128,1]{0,1:T(1,128)S(1)}, s32[128,1]{0,1:T(1,128)}, u32[]{:S(2)}) %copy-start.4) | copy-done | bytes 536
  19.5 0.7 %slots.1.refs_1_ = s32[1,128]{1,0:T(1,128)S(1)} custom-call(s32[8]{0:T(128)S(1)} %copy-done.3, s32[1,128]{1,0:T(1,128)S(1)} %bitcast.10), custom_call_target="tpu_custom_call" | custom-call | flops 99999997952 | bytes 100000000 | tf_op jit(solution)/shard_map/slots/pallas_call | solution.py:188
  20.2 0.0 collective-permute-done.refs_3_.refs_2_
  20.2 0.0 collective-permute-done.2.refs_5_.refs_4_
  20.2 0.9 %collective-permute-done.4.refs_7_.refs_6_ = bf16[16,4096]{1,0:T(8,128)(2,1)S(1)} collective-permute-done((bf16[16,4096]{1,0:T(8,128)(2,1)S(1)}, bf16[16,4096]{1,0:T(8,128)(2,1)S(1)}, u32[]{:S(2)}, u32[]{:S(2)}) %collective-permute-start.4) | collective-permute-done | bytes 131104 | tf_op jit(solution)/shard_map/ppermute | solution.py:183
  21.1 1.5 %collective-permute-done.6.refs_9_.refs_8_ = bf16[16,4096]{1,0:T(8,128)(2,1)S(1)} collective-permute-done((bf16[16,4096]{1,0:T(8,128)(2,1)S(1)}, bf16[16,4096]{1,0:T(8,128)(2,1)S(1)}, u32[]{:S(2)}, u32[]{:S(2)}) %collective-permute-start.6) | collective-permute-done | bytes 131104 | tf_op jit(solution)/shard_map/ppermute | solution.py:183
  22.6 0.0 copy-done.1
  22.6 0.0 copy-done.2
  22.6 0.6 %lowrank.1.low_a = f32[32,64]{1,0:T(8,128)S(1)} custom-call(s32[1]{0:T(128)} %bitcast.1.refs_0_, s32[1,128]{1,0:T(1,128)S(1)} %slots.1.refs_1_, bf16[16,4096]{1,0:T(8,128)(2,1)S(1)} %copy-done.1, bf16[16,4096]{1,0:T(8,128)(2,1)S(1)} %collective-permute-done.refs_3_.refs_2_, bf16[16,4096]{1,0:T(8,128)(2,1)S(1)} %collective-permute-done.1.refs_4_.refs_3_, ...), custom_call_target="tpu_custom_call" | custom-call | flops 100000000 | bytes 2000000 | tf_op jit(solution)/shard_map/lowrank/pallas_call | solution.py:205
  23.2 0.0 collective-permute-start.7
  23.9 0.5 collective-permute-done.7.low_b
  24.4 0.0 copy-done
  24.4 1.7 %delta.1.refs_10_ = bf16[256,1792]{1,0:T(8,128)(2,1)} custom-call(f32[1]{0:T(128)S(6)} %copy.8.scale, f32[32,64]{1,0:T(8,128)S(1)} %lowrank.1.low_a, f32[32,64]{1,0:T(8,128)S(1)} %collective-permute-done.7.low_b, bf16[512,1792]{1,0:T(8,128)(2,1)S(1)} %bitcast.8), custom_call_target="tpu_custom_call" | custom-call | flops 500000000 | bytes 3000000 | tf_op jit(solution)/shard_map/delta/pallas_call | solution.py:217
  26.1 4.4 %all-to-all-start = ((bf16[8,32,1792]{2,1,0:T(8,128)(2,1)}), bf16[8,32,1792]{2,1,0:T(8,128)(2,1)S(1)}, u32[]{:S(2)}, u32[]{:S(2)}) async-start(bf16[8,32,1792]{2,1,0:T(8,128)(2,1)} %bitcast.5), calls=%async_computation | async-start | bytes 1835008 | tf_op jit(solution)/shard_map/all_to_all | solution.py:227
  30.5 0.1 pad_add_fusion.refs_0_
  30.6 11.9 %base.1 = (f32[128,1792]{1,0:T(8,128)S(1)}, f32[128,1792]{1,0:T(8,128)S(1)}) custom-call(s32[2]{0:T(128)S(1)} %pad_add_fusion.refs_0_, bf16[16,4096]{1,0:T(8,128)(2,1)S(1)} %copy-done.1, bf16[16,4096]{1,0:T(8,128)(2,1)S(1)} %collective-permute-done.refs_3_.refs_2_, bf16[16,4096]{1,0:T(8,128)(2,1)S(1)} %collective-permute-done.1.refs_4_.refs_3_, ...), custom_call_target="tpu_custom_call" | custom-call | flops 3758096384 | bytes 10000000 | tf_op jit(solution)/shard_map/base/pallas_call | solution.py:231
  42.4 0.1 collective-permute-start.8
  42.5 2.5 %collective-permute-done.8.other = f32[128,1792]{1,0:T(8,128)S(1)} collective-permute-done((f32[128,1792]{1,0:T(8,128)S(1)}, f32[128,1792]{1,0:T(8,128)S(1)}, u32[]{:S(2)}, u32[]{:S(2)}) %collective-permute-start.8) | collective-permute-done | bytes 917536 | tf_op jit(solution)/shard_map/ppermute | solution.py:247
  45.0 8.8 %all-to-all-done = bf16[8,32,1792]{2,1,0:T(8,128)(2,1)S(1)} async-done(((bf16[8,32,1792]{2,1,0:T(8,128)(2,1)}), bf16[8,32,1792]{2,1,0:T(8,128)(2,1)S(1)}, u32[]{:S(2)}, u32[]{:S(2)}) %all-to-all-start) | async-done | bytes 917536 | tf_op jit(solution)/shard_map/all_to_all | solution.py:227
  53.8 1.1 %combine.1 = bf16[128,1792]{1,0:T(8,128)(2,1)} custom-call(s32[1,128]{1,0:T(1,128)S(1)} %slots.1.refs_1_, f32[128,1792]{1,0:T(8,128)S(1)} %get-tuple-element.7.own, f32[128,1792]{1,0:T(8,128)S(1)} %collective-permute-done.8.other, bf16[256,1792]{1,0:T(8,128)(2,1)S(1)} %bitcast.7), custom_call_target="tpu_custom_call" | custom-call | flops 200000000 | bytes 4000000 | tf_op jit(solution)/shard_map/combine/pallas_call | solution.py:249
  (4 shorter events, 0.0 us)
Async XLA Ops:
  0.0 8.3 %collective-permute-start.1 = (bf16[16,4096]{1,0:T(8,128)(2,1)}, bf16[16,4096]{1,0:T(8,128)(2,1)S(1)}, u32[]{:S(2)}, u32[]{:S(2)}) collective-permute-start(bf16[16,4096]{1,0:T(8,128)(2,1)} %refs_1_.1), channel_id=1, source_target_pairs={{0,4},{2,6},{4,0},{6,2},{8,12},{10,14},{12,8},{14,10},{1,5},{3,7},... | collective-permute-start | bytes 393224 | tf_op jit(solution)/shard_map/ppermute | solution.py:183
  3.0 13.2 %collective-permute-start.3 = (bf16[16,4096]{1,0:T(8,128)(2,1)}, bf16[16,4096]{1,0:T(8,128)(2,1)S(1)}, u32[]{:S(2)}, u32[]{:S(2)}) collective-permute-start(bf16[16,4096]{1,0:T(8,128)(2,1)} %refs_1_.1), channel_id=1, source_target_pairs={{0,8},{2,10},{4,12},{6,14},{8,0},{10,2},{12,4},{14,6},{1,9},{3,11}... | collective-permute-start | bytes 393224 | tf_op jit(solution)/shard_map/ppermute | solution.py:183
  5.6 12.1 %collective-permute-start.5 = (bf16[16,4096]{1,0:T(8,128)(2,1)}, bf16[16,4096]{1,0:T(8,128)(2,1)S(1)}, u32[]{:S(2)}, u32[]{:S(2)}) collective-permute-start(bf16[16,4096]{1,0:T(8,128)(2,1)} %refs_1_.1), channel_id=1, source_target_pairs={{0,12},{2,14},{4,8},{6,10},{8,4},{10,6},{12,0},{14,2},{1,13},{3,15... | collective-permute-start | bytes 393224 | tf_op jit(solution)/shard_map/ppermute | solution.py:183
  5.6 14.6 %collective-permute-start = (bf16[16,4096]{1,0:T(8,128)(2,1)}, bf16[16,4096]{1,0:T(8,128)(2,1)S(1)}, u32[]{:S(2)}, u32[]{:S(2)}) collective-permute-start(bf16[16,4096]{1,0:T(8,128)(2,1)} %refs_1_.1), channel_id=1, source_target_pairs={{0,2},{2,0},{4,6},{6,4},{8,10},{10,8},{12,14},{14,12},{1,3},{3,1},... | collective-permute-start | bytes 393224 | tf_op jit(solution)/shard_map/ppermute | solution.py:183
  8.3 11.9 %collective-permute-start.2 = (bf16[16,4096]{1,0:T(8,128)(2,1)S(1)}, bf16[16,4096]{1,0:T(8,128)(2,1)S(1)}, u32[]{:S(2)}, u32[]{:S(2)}) collective-permute-start(bf16[16,4096]{1,0:T(8,128)(2,1)S(1)} %collective-permute-done.1.refs_4_.refs_3_), channel_id=1, source_target_pairs={{0,2},{2,0},{4,6},{6,4},{8,10},{10,8},{12,14},{14,12},{1,3},{3,1},... | collective-permute-start | bytes 393224 | tf_op jit(solution)/shard_map/ppermute | solution.py:183
  16.2 5.0 %collective-permute-start.4 = (bf16[16,4096]{1,0:T(8,128)(2,1)S(1)}, bf16[16,4096]{1,0:T(8,128)(2,1)S(1)}, u32[]{:S(2)}, u32[]{:S(2)}) collective-permute-start(bf16[16,4096]{1,0:T(8,128)(2,1)S(1)} %collective-permute-done.3.refs_6_.refs_5_), channel_id=1, source_target_pairs={{0,2},{2,0},{4,6},{6,4},{8,10},{10,8},{12,14},{14,12},{1,3},{3,1},... | collective-permute-start | bytes 393224 | tf_op jit(solution)/shard_map/ppermute | solution.py:183
  17.7 5.0 %collective-permute-start.6 = (bf16[16,4096]{1,0:T(8,128)(2,1)S(1)}, bf16[16,4096]{1,0:T(8,128)(2,1)S(1)}, u32[]{:S(2)}, u32[]{:S(2)}) collective-permute-start(bf16[16,4096]{1,0:T(8,128)(2,1)S(1)} %collective-permute-done.5.refs_8_.refs_7_), channel_id=1, source_target_pairs={{0,2},{2,0},{4,6},{6,4},{8,10},{10,8},{12,14},{14,12},{1,3},{3,1},... | collective-permute-start | bytes 393224 | tf_op jit(solution)/shard_map/ppermute | solution.py:183
  18.2 0.7 %copy-start.3 = (s32[8]{0:T(128)S(1)}, s32[8]{0:T(128)}, u32[]{:S(2)}) copy-start(s32[8]{0:T(128)} %index_map.1) | copy-start | bytes 100
  18.9 0.7 %copy-start.4 = (s32[128,1]{0,1:T(1,128)S(1)}, s32[128,1]{0,1:T(1,128)}, u32[]{:S(2)}) copy-start(s32[128,1]{0,1:T(1,128)} %param.12) | copy-start | bytes 1540
  19.5 3.1 %copy-start.1 = (bf16[16,4096]{1,0:T(8,128)(2,1)S(1)}, bf16[16,4096]{1,0:T(8,128)(2,1)}, u32[]{:S(2)}) copy-start(bf16[16,4096]{1,0:T(8,128)(2,1)} %refs_1_.1) | copy-start | bytes 393220
  19.5 3.1 %copy-start.2 = (bf16[1,64,4096]{2,1,0:T(8,128)(2,1)S(1)}, bf16[1,64,4096]{2,1,0:T(8,128)(2,1)}, u32[]{:S(2)}) copy-start(bf16[1,64,4096]{2,1,0:T(8,128)(2,1)} %param.9) | copy-start | bytes 1572868
  19.5 4.9 %copy-start = (bf16[1,64,8,1,1792]{4,2,3,1,0:T(8,128)(2,1)S(1)}, bf16[1,64,8,1,1792]{4,2,3,1,0:T(8,128)(2,1)}, u32[]{:S(2)}) copy-start(bf16[1,64,8,1,1792]{4,2,3,1,0:T(8,128)(2,1)} %param.10) | copy-start | bytes 5505028
  23.2 1.2 %collective-permute-start.7 = (f32[32,64]{1,0:T(8,128)S(1)}, f32[32,64]{1,0:T(8,128)S(1)}, u32[]{:S(2)}, u32[]{:S(2)}) collective-permute-start(f32[32,64]{1,0:T(8,128)S(1)} %lowrank.1.low_a), channel_id=1, source_target_pairs={{0,1},{1,0},{2,3},{3,2},{4,5},{5,4},{6,7},{7,6},{8,9},{9,8},{10,11... | collective-permute-start | bytes 24584 | tf_op jit(solution)/shard_map/ppermute | solution.py:215
  26.1 27.7 %all-to-all-start = ((bf16[8,32,1792]{2,1,0:T(8,128)(2,1)}), bf16[8,32,1792]{2,1,0:T(8,128)(2,1)S(1)}, u32[]{:S(2)}, u32[]{:S(2)}) async-start(bf16[8,32,1792]{2,1,0:T(8,128)(2,1)} %bitcast.5), calls=%async_computation | async-start | bytes 1835008 | tf_op jit(solution)/shard_map/all_to_all | solution.py:227
  42.4 2.5 %collective-permute-start.8 = (f32[128,1792]{1,0:T(8,128)S(1)}, f32[128,1792]{1,0:T(8,128)S(1)}, u32[]{:S(2)}, u32[]{:S(2)}) collective-permute-start(f32[128,1792]{1,0:T(8,128)S(1)} %get-tuple-element.8), channel_id=1, source_target_pairs={{0,1},{1,0},{2,3},{3,2},{4,5},{5,4},{6,7},{7,6},{8,9},{9,8},{10,11... | collective-permute-start | bytes 2752520 | tf_op jit(solution)/shard_map/ppermute | solution.py:247

commit v4 on v3

--- a/solution.py
+++ b/solution.py
@@ -80,8 +80,13 @@
     return stored * CAP + within.astype(jnp.int32)
 
 
-def slots_kernel(index_map, adapter, slot):
+def slots_kernel(where, index_map, adapter, weight, slot, ahead, arrival):
+    width = weight.shape[1] // 2
+    start = pl.multiple_of((1 - where[1]) * width, 128)
+    copy = pltpu.make_async_copy(weight.at[:, pl.ds(start, ahead.shape[1])], ahead, arrival.at[0])
+    copy.start()
     slot[...] = slots_as_row(adapter, index_map)
+    copy.wait()
 
 
 def lowrank_kernel(groups, *refs):
@@ -103,7 +108,9 @@
     )
 
 
-def delta_kernel(groups, scale, low_a, low_b, up, out, spread):
+def delta_kernel(groups, offsets, where, scale, low_a, low_b, up, _, *refs):
+    outs, spread = refs[:-1], refs[-1]
+    me = where[0]
     rank = low_a.shape[1]
     low = ((low_a[...] + low_b[...]) * scale[0]).astype(BF16)
     depth = rank * groups
@@ -113,20 +120,24 @@
     ).astype(F32).astype(BF16)
     wide = jnp.dot(low, widen, preferred_element_type=F32)
     block = lax.rem(lax.broadcasted_iota(jnp.int32, (CAP, depth), 1), groups)
-    for d in range(groups):
-        spread[d * CAP : (d + 1) * CAP, :] = jnp.where(block == d, wide, 0.0).astype(BF16)
-    result = jnp.dot(spread[...], up[...], preferred_element_type=F32)
-    out[...] = result.astype(BF16)
-
-
-def base_kernel(groups, tile, slots, *refs):
+    for i, d in enumerate(offsets):
+        spread[i * CAP : (i + 1) * CAP, :] = jnp.where(block == (me ^ d), wide, 0.0).astype(BF16)
+    result = jnp.dot(spread[...], up[...], preferred_element_type=F32).astype(BF16)
+    for i, out in enumerate(outs):
+        out[...] = result[i * CAP : (i + 1) * CAP, :]
+
+
+def base_kernel(groups, *refs):
     where = refs[0]
     pieces = refs[1 : 1 + groups]
-    weight, _, partner, own, gathered, held, arrival = refs[1 + groups :]
+    ahead, weight, _, _, partner, own, gathered, held, arrival = refs[1 + groups :]
     me, core = where[0], where[1]
     part = pieces[0].shape[0]
     width = own.shape[1]
+    slots, _, tile = held.shape
+    ready = ahead.shape[1] // tile
     count = width // tile
+    last = 2 * count
 
     def fetch(step):
         half = 1 - core if step < count else core
@@ -137,30 +148,40 @@
             arrival.at[step % slots],
         )
 
-    for step in range(slots - 1):
+    for step in range(ready, ready + slots - 1):
         fetch(step).start()
     for d in range(groups):
         start = pl.multiple_of((me ^ d) * part, part)
         gathered[pl.ds(start, part), :] = pieces[d][...]
-    for step in range(2 * count):
-        if step + slots - 1 < 2 * count:
-            fetch(step + slots - 1).start()
-        fetch(step).wait()
+    for step in range(last):
+        if step < ready:
+            columns = ahead[:, step * tile : (step + 1) * tile]
+        else:
+            if step + slots - 1 < last:
+                fetch(step + slots - 1).start()
+            fetch(step).wait()
+            columns = held[step % slots]
         out = partner if step < count else own
         start = (step % count) * tile
         out[:, start : start + tile] = jnp.dot(
-            gathered[...], held[step % slots], preferred_element_type=F32
+            gathered[...], columns, preferred_element_type=F32
         )
 
 
-def final_kernel(groups, slots, own, other, arrived, out):
-    slot = slots[...]
-    rows = slot.shape[1]
-    place = (
-        slot == lax.broadcasted_iota(jnp.int32, (groups * CAP, rows), 0)
+def place_kernel(slots, place):
+    place[...] = (
+        slots[...] == lax.broadcasted_iota(jnp.int32, place.shape, 0)
     ).astype(F32).astype(BF16)
+
+
+def final_kernel(groups, where, place, own, other, *refs):
+    pieces, out, arrived = refs[:groups], refs[-2], refs[-1]
+    me = where[0]
+    for d in range(groups):
+        start = pl.multiple_of((me ^ d) * CAP, CAP)
+        arrived[pl.ds(start, CAP), :] = pieces[d][...]
     delta = lax.dot_general(
-        place, arrived[...], (((0,), (0,)), ((), ())), preferred_element_type=F32
+        place[...], arrived[...], (((0,), (0,)), ((), ())), preferred_element_type=F32
     )
     out[...] = (own[...] + other[...] + delta).astype(BF16)
 
@@ -185,21 +206,32 @@
     def params(limit):
         return pltpu.CompilerParams(vmem_limit_bytes=limit << 20)
 
-    slot = pl.pallas_call(
+    tile, buffers, ready = 256, 5, 4
+    both = jnp.stack([me, core])
+    slot, ahead = pl.pallas_call(
         slots_kernel,
-        out_shape=jax.ShapeDtypeStruct((1, rows), jnp.int32),
-        in_specs=[SMEM, VMEM],
-        out_specs=VMEM,
-        compiler_params=params(2),
+        out_shape=[
+            jax.ShapeDtypeStruct((1, rows), jnp.int32),
+            jax.ShapeDtypeStruct((depth, ready * tile), BF16),
+        ],
+        in_specs=[SMEM, SMEM, VMEM, ANY],
+        out_specs=[VMEM, VMEM],
+        scratch_shapes=[pltpu.SemaphoreType.DMA((1,))],
+        compiler_params=params(37),
         cost_estimate=pl.CostEstimate(flops=10**11, bytes_accessed=10**8, transcendentals=0),
         name="slots",
-    )(storage_index_map, adapter)
+    )(both, storage_index_map, adapter, gate_weight)
 
     pieces = {0: tokens}
-    for d in range(2, groups, 2):
+    steps = [1 << i for i in range(groups.bit_length() - 1)]
+    for d in reversed(steps):
         pieces[d] = to(tokens, d)
-    for d in range(0, groups, 2):
-        pieces[d + 1] = to(pieces[d], 1)
+    if groups > 2:
+        pieces[groups - 1] = to(tokens, groups - 1)
+    for d in range(1, groups):
+        if d not in pieces:
+            far = max(step for step in steps if step <= d)
+            pieces[d] = to(pieces[far], d - far)
     pieces = [pieces[d] for d in range(groups)]
 
     low = pl.pallas_call(
@@ -214,23 +246,33 @@
     )(where, slot, *pieces, down_panels[0])
     low_other = lax.ppermute(low, "tp", swap)
 
-    deltas = pl.pallas_call(
-        functools.partial(delta_kernel, groups),
-        out_shape=jax.ShapeDtypeStruct((groups * CAP, width), BF16),
-        in_specs=[SMEM, VMEM, VMEM, VMEM],
-        out_specs=VMEM,
-        scratch_shapes=[pltpu.VMEM((groups * CAP, rank * groups), BF16)],
-        compiler_params=params(8),
-        cost_estimate=pl.CostEstimate(flops=5 * 10**8, bytes_accessed=3 * 10**6, transcendentals=0),
-        name="delta",
-    )(adapter_scales, low, low_other, up_panels.reshape(rank * groups, width))
-    arrived = lax.all_to_all(deltas, "rows", split_axis=0, concat_axis=0, tiled=True)
-
-    tile, buffers = 256, 5
+    up = up_panels.reshape(rank * groups, width)
+
+    def deltas(offsets, after):
+        return pl.pallas_call(
+            functools.partial(delta_kernel, groups, offsets),
+            out_shape=[jax.ShapeDtypeStruct((CAP, width), BF16)] * len(offsets),
+            in_specs=[SMEM, SMEM, VMEM, VMEM, VMEM, ANY],
+            out_specs=[VMEM] * len(offsets),
+            scratch_shapes=[pltpu.VMEM((len(offsets) * CAP, rank * groups), BF16)],
+            compiler_params=params(8),
+            cost_estimate=pl.CostEstimate(flops=10**6, bytes_accessed=10**6, transcendentals=0),
+            name="delta",
+        )(where, adapter_scales, low, low_other, up, after)
+
+    arrived = [None] * groups
+    blocks = deltas((0, 2, 1, 4, 5, 6), low)
+    for d, x in zip((0, 2, 1, 4, 5, 6), blocks):
+        arrived[d] = to(x, d) if d else x
+    seventh = deltas((7,), arrived[1])[0]
+    arrived[7] = to(seventh, 7)
+    eighth = deltas((3,), arrived[2])[0]
+    arrived[3] = to(eighth, 3)
+
     half = jax.ShapeDtypeStruct((rows, width), F32)
     partner, own = pl.pallas_call(
-        functools.partial(base_kernel, groups, tile, buffers),
-        in_specs=[SMEM] + [VMEM] * groups + [ANY, ANY],
+        functools.partial(base_kernel, groups),
+        in_specs=[SMEM] + [VMEM] * groups + [VMEM, ANY, ANY, ANY],
         out_specs=[VMEM, VMEM],
         scratch_shapes=[
             pltpu.VMEM((rows, depth), BF16),
@@ -238,27 +280,38 @@
             pltpu.SemaphoreType.DMA((buffers,)),
         ],
         out_shape=[half, half],
-        compiler_params=params(40),
+        compiler_params=params(37),
         cost_estimate=pl.CostEstimate(
             flops=4 * rows * depth * width, bytes_accessed=10**7, transcendentals=0
         ),
         name="base",
-    )(jnp.stack([me, core]), *pieces, gate_weight, deltas)
+    )(both, *pieces, ahead, gate_weight, seventh, eighth)
     other = lax.ppermute(partner, "tp", swap)
+
+    place = pl.pallas_call(
+        place_kernel,
+        out_shape=jax.ShapeDtypeStruct((groups * CAP, rows), BF16),
+        in_specs=[VMEM],
+        out_specs=VMEM,
+        compiler_params=params(2),
+        cost_estimate=pl.CostEstimate(flops=10**11, bytes_accessed=10**8, transcendentals=0),
+        name="place",
+    )(slot)
 
     return pl.pallas_call(
         functools.partial(final_kernel, groups),
         out_shape=jax.ShapeDtypeStruct((rows, width), BF16),
-        in_specs=[VMEM, VMEM, VMEM, VMEM],
+        in_specs=[SMEM, VMEM, VMEM, VMEM] + [VMEM] * groups,
         out_specs=VMEM,
+        scratch_shapes=[pltpu.VMEM((groups * CAP, width), BF16)],
         compiler_params=params(8),
         cost_estimate=pl.CostEstimate(flops=2 * 10**8, bytes_accessed=4 * 10**6, transcendentals=0),
         name="combine",
-    )(slot, own, other, arrived)
+    )(where, place, own, other, *arrived)
 
 
 def on_device(*args):
-    if lax.axis_size("rows") in (2, 4, 8):
+    if lax.axis_size("rows") == 8:
         return few_groups(*args)
     return many_groups(*args)
 

time: 55.1 us -> 49.5 us (0.90)
  waiting for transfers between devices: 21.4 us -> 8.2 us
  starting transfers between devices: 15.5 us -> 21.2 us
  Pallas kernels: 15.9 us -> 17.7 us
    ppermute x7 -> x14, starting transfers between devices: 11.1 us -> 21.2 us  [to(): return lax.ppermute(x, 'rows', [(i, i ^ d) for i in range(groups)])]
    all_to_all x1 -> x0, waiting for transfers between devices: 8.81 us -> none  [few_groups(): lax.all_to_all(deltas, 'rows', split_axis=0, concat_axis=0, tiled=True)]
    all_to_all x1 -> x0, starting transfers between devices: 4.39 us -> none  [few_groups(): lax.all_to_all(deltas, 'rows', split_axis=0, concat_axis=0, tiled=True)]
    ppermute x7 -> x14, waiting for transfers between devices: 9.56 us -> 5.28 us  [to(): return lax.ppermute(x, 'rows', [(i, i ^ d) for i in range(groups)])]
    pallas_call x3 -> x6, Pallas kernels: 14.2 us -> 16 us  [the longest x1 10.2 us: few_groups(): pl.pallas_call(functools.partial(base_kernel, groups), in_specs=[SMEM] +...]
  transfers between devices with their start and end apart: 10 -> 16, of which waited for: 7 -> 4; matrix products, arithmetic and copies ran while one was open for 0% -> 0% of each run, Pallas kernels for 23% -> 31%
where the time goes in v4:
time: 49.5 us; the launch traced here: 49.4 us
  starting transfers between devices  21.2 us (43%)
  Pallas kernels  17.7 us (36%)
  waiting for transfers between devices  8.2 us (17%)
  local copies, waits for them, and re-layouts  1.32 us (3%)
  between operations  0.81 us (2%)
    ppermute x14, starting transfers between devices, to(): return lax.ppermute(x, 'rows', [(i, i ^ d) for i in range(groups)])  21.2 us
    pallas_call x1, Pallas kernels, few_groups(): pl.pallas_call(functools.partial(base_kernel, groups), in_specs=[SMEM] +...  10.2 us
    ppermute x14, waiting for transfers between devices, to(): return lax.ppermute(x, 'rows', [(i, i ^ d) for i in range(groups)])  5.28 us
    pallas_call x1, Pallas kernels, few_groups(): pl.pallas_call(slots_kernel, out_shape=[jax.ShapeDtypeStruct((1, rows), j...  4.16 us
    ppermute x1, waiting for transfers between devices, few_groups(): other = lax.ppermute(partner, 'tp', swap)  2.39 us
    pallas_call x3, Pallas kernels, deltas(): pl.pallas_call(functools.partial(delta_kernel, groups, offsets), out_shap...  1.6 us
    unnamed x10, local copies, waits for them, and re-layouts  1.32 us
    pallas_call x1, Pallas kernels, few_groups(): pl.pallas_call(functools.partial(final_kernel, groups), out_shape=jax.Sha...  1.13 us
  transfers between devices with their start and end apart: 16, of which 4 were waited for; matrix products, arithmetic and copies ran while one was open for 0% of the time, Pallas kernels for 31%

profile of v4, /device:TPU:0, one launch (start us, length us, event | category | flops | bytes accessed | tf_op | source)
XLA Modules:
  0.0 49.4 jit_solution(15078379175403364058)
XLA Ops:
  0.0 4.0 %collective-permute-start.3 = (bf16[16,4096]{1,0:T(8,128)(2,1)}, bf16[16,4096]{1,0:T(8,128)(2,1)S(1)}, u32[]{:S(2)}, u32[]{:S(2)}) collective-permute-start(bf16[16,4096]{1,0:T(8,128)(2,1)} %refs_1_.1), channel_id=1, source_target_pairs={{0,8},{2,10},{4,12},{6,14},{8,0},{10,2},{12,4},{14,6},{1,9},{3,11}... | collective-permute-start | bytes 393224 | tf_op jit(solution)/shard_map/ppermute | solution.py:204
  4.0 1.6 %collective-permute-start.1 = (bf16[16,4096]{1,0:T(8,128)(2,1)}, bf16[16,4096]{1,0:T(8,128)(2,1)S(1)}, u32[]{:S(2)}, u32[]{:S(2)}) collective-permute-start(bf16[16,4096]{1,0:T(8,128)(2,1)} %refs_1_.1), channel_id=1, source_target_pairs={{0,4},{2,6},{4,0},{6,2},{8,12},{10,14},{12,8},{14,10},{1,5},{3,7},... | collective-permute-start | bytes 393224 | tf_op jit(solution)/shard_map/ppermute | solution.py:204
  5.6 1.5 %collective-permute-start = (bf16[16,4096]{1,0:T(8,128)(2,1)}, bf16[16,4096]{1,0:T(8,128)(2,1)S(1)}, u32[]{:S(2)}, u32[]{:S(2)}) collective-permute-start(bf16[16,4096]{1,0:T(8,128)(2,1)} %refs_1_.1), channel_id=1, source_target_pairs={{0,2},{2,0},{4,6},{6,4},{8,10},{10,8},{12,14},{14,12},{1,3},{3,1},... | collective-permute-start | bytes 393224 | tf_op jit(solution)/shard_map/ppermute | solution.py:204
  7.1 0.1 pad_add_fusion.where.refs_0_
  7.2 4.8 %collective-permute-done.3.refs_6_.refs_5_ = bf16[16,4096]{1,0:T(8,128)(2,1)S(1)} collective-permute-done((bf16[16,4096]{1,0:T(8,128)(2,1)}, bf16[16,4096]{1,0:T(8,128)(2,1)S(1)}, u32[]{:S(2)}, u32[]{:S(2)}) %collective-permute-start.3) | collective-permute-done | bytes 131104 | tf_op jit(solution)/shard_map/ppermute | solution.py:204
  12.0 2.1 %collective-permute-start.4 = (bf16[16,4096]{1,0:T(8,128)(2,1)S(1)}, bf16[16,4096]{1,0:T(8,128)(2,1)S(1)}, u32[]{:S(2)}, u32[]{:S(2)}) collective-permute-start(bf16[16,4096]{1,0:T(8,128)(2,1)S(1)} %collective-permute-done.3.refs_6_.refs_5_), channel_id=1, source_target_pairs={{0,2},{2,0},{4,6},{6,4},{8,10},{10,8},{12,14},{14,12},{1,3},{3,1},... | collective-permute-start | bytes 393224 | tf_op jit(solution)/shard_map/ppermute | solution.py:204
  14.1 0.0 collective-permute-start.5
  14.2 0.0 collective-permute-done.1.refs_4_.refs_3_
  14.2 0.3 collective-permute-start.2
  14.4 0.7 %copy-done.3 = s32[8]{0:T(128)S(1)} copy-done((s32[8]{0:T(128)S(1)}, s32[8]{0:T(128)}, u32[]{:S(2)}) %copy-start.3) | copy-done | bytes 56
  15.1 0.7 %copy-done.4 = s32[128,1]{0,1:T(1,128)S(1)} copy-done((s32[128,1]{0,1:T(1,128)S(1)}, s32[128,1]{0,1:T(1,128)}, u32[]{:S(2)}) %copy-start.4) | copy-done | bytes 536
  15.7 4.2 %slots.1 = (s32[1,128]{1,0:T(1,128)S(1)}, bf16[4096,1024]{1,0:T(8,128)(2,1)S(1)}) custom-call(s32[2]{0:T(128)S(1)} %pad_add_fusion.where.refs_0_, s32[8]{0:T(128)S(1)} %copy-done.3, s32[1,128]{1,0:T(1,128)S(1)} %bitcast.9, bf16[4096,3584]{1,0:T(8,128)(2,1)} %refs_10_.1), custom_call_target="tpu_custom_call" | custom-call | flops 99999997952 | bytes 100000000 | tf_op jit(solution)/shard_map/slots/pallas_call | solution.py:211
  19.9 0.0 collective-permute-done.refs_3_.refs_2_
  19.9 0.0 collective-permute-done.5.refs_8_.refs_7_
  19.9 0.4 collective-permute-done.2.refs_5_.refs_4_
  20.4 0.6 %lowrank.1.low_a._ = f32[32,64]{1,0:T(8,128)S(1)} custom-call(s32[1]{0:T(128)} %bitcast.refs_0_.where, s32[1,128]{1,0:T(1,128)S(1)} %get-tuple-element.15.slots.refs_1_, bf16[16,4096]{1,0:T(8,128)(2,1)S(1)} %copy-done.1, bf16[16,4096]{1,0:T(8,128)(2,1)S(1)} %collective-permute-done.refs_3_.refs_2_, ...), custom_call_target="tpu_custom_call" | custom-call | flops 100000000 | bytes 2000000 | tf_op jit(solution)/shard_map/lowrank/pallas_call | solution.py:237
  20.9 0.0 collective-permute-start.7
  21.6 0.5 %collective-permute-done.7.low_b = f32[32,64]{1,0:T(8,128)S(1)} collective-permute-done((f32[32,64]{1,0:T(8,128)S(1)}, f32[32,64]{1,0:T(8,128)S(1)}, u32[]{:S(2)}, u32[]{:S(2)}) %collective-permute-start.7) | collective-permute-done | bytes 8224 | tf_op jit(solution)/shard_map/ppermute | solution.py:247
  22.1 0.6 %delta.3 = (bf16[32,1792]{1,0:T(8,128)(2,1)S(1)}, bf16[32,1792]{1,0:T(8,128)(2,1)S(1)}, bf16[32,1792]{1,0:T(8,128)(2,1)S(1)}, bf16[32,1792]{1,0:T(8,128)(2,1)S(1...) custom-call(s32[1]{0:T(128)} %bitcast.refs_0_.where, f32[1]{0:T(128)S(6)} %copy.8.scale, ...), custom_call_target="tpu_custom_call" | custom-call | flops 1000000 | bytes 1000000 | tf_op jit(solution)/shard_map/delta/pallas_call | solution.py:252
  22.8 1.5 %collective-permute-start.9 = (bf16[32,1792]{1,0:T(8,128)(2,1)S(1)}, bf16[32,1792]{1,0:T(8,128)(2,1)S(1)}, u32[]{:S(2)}, u32[]{:S(2)}) collective-permute-start(bf16[32,1792]{1,0:T(8,128)(2,1)S(1)} %get-tuple-element.18), channel_id=1, source_target_pairs={{0,4},{2,6},{4,0},{6,2},{8,12},{10,14},{12,8},{14,10},{1,5},{3,7},... | collective-permute-start | bytes 344072 | tf_op jit(solution)/shard_map/ppermute | solution.py:204
  24.3 1.9 %collective-permute-start.8 = (bf16[32,1792]{1,0:T(8,128)(2,1)S(1)}, bf16[32,1792]{1,0:T(8,128)(2,1)S(1)}, u32[]{:S(2)}, u32[]{:S(2)}) collective-permute-start(bf16[32,1792]{1,0:T(8,128)(2,1)S(1)} %get-tuple-element.17), channel_id=1, source_target_pairs={{0,2},{2,0},{4,6},{6,4},{8,10},{10,8},{12,14},{14,12},{1,3},{3,1},... | collective-permute-start | bytes 344072 | tf_op jit(solution)/shard_map/ppermute | solution.py:204
  26.2 1.7 %collective-permute-start.12 = (bf16[32,1792]{1,0:T(8,128)(2,1)S(1)}, bf16[32,1792]{1,0:T(8,128)(2,1)S(1)}, u32[]{:S(2)}, u32[]{:S(2)}) collective-permute-start(bf16[32,1792]{1,0:T(8,128)(2,1)S(1)} %get-tuple-element.22), channel_id=1, source_target_pairs={{0,8},{2,10},{4,12},{6,14},{8,0},{10,2},{12,4},{14,6},{1,9},{3,11}... | collective-permute-start | bytes 344072 | tf_op jit(solution)/shard_map/ppermute | solution.py:204
  27.9 0.8 %collective-permute-start.13 = (bf16[32,1792]{1,0:T(8,128)(2,1)S(1)}, bf16[32,1792]{1,0:T(8,128)(2,1)S(1)}, u32[]{:S(2)}, u32[]{:S(2)}) collective-permute-start(bf16[32,1792]{1,0:T(8,128)(2,1)S(1)} %get-tuple-element.23), channel_id=1, source_target_pairs={{0,10},{2,8},{4,14},{6,12},{8,2},{10,0},{12,6},{14,4},{1,11},{3,9}... | collective-permute-start | bytes 344072 | tf_op jit(solution)/shard_map/ppermute | solution.py:204
  28.7 3.1 %collective-permute-start.14 = (bf16[32,1792]{1,0:T(8,128)(2,1)S(1)}, bf16[32,1792]{1,0:T(8,128)(2,1)S(1)}, u32[]{:S(2)}, u32[]{:S(2)}) collective-permute-start(bf16[32,1792]{1,0:T(8,128)(2,1)S(1)} %get-tuple-element.24), channel_id=1, source_target_pairs={{0,12},{2,14},{4,8},{6,10},{8,4},{10,6},{12,0},{14,2},{1,13},{3,15... | collective-permute-start | bytes 344072 | tf_op jit(solution)/shard_map/ppermute | solution.py:204
  31.8 0.5 delta.5.refs_12_
  32.3 0.5 %collective-permute-start.11 = (bf16[32,1792]{1,0:T(8,128)(2,1)S(1)}, bf16[32,1792]{1,0:T(8,128)(2,1)S(1)}, u32[]{:S(2)}, u32[]{:S(2)}) collective-permute-start(bf16[32,1792]{1,0:T(8,128)(2,1)S(1)} %delta.5.refs_12_), channel_id=1, source_target_pairs={{0,6},{2,4},{4,2},{6,0},{8,14},{10,12},{12,10},{14,8},{1,7},{3,5},... | collective-permute-start | bytes 344072 | tf_op jit(solution)/shard_map/ppermute | solution.py:204
  32.9 0.5 delta.4.refs_11_
  33.3 2.1 %collective-permute-start.15 = (bf16[32,1792]{1,0:T(8,128)(2,1)S(1)}, bf16[32,1792]{1,0:T(8,128)(2,1)S(1)}, u32[]{:S(2)}, u32[]{:S(2)}) collective-permute-start(bf16[32,1792]{1,0:T(8,128)(2,1)S(1)} %delta.4.refs_11_), channel_id=1, source_target_pairs={{0,14},{2,12},{4,10},{6,8},{8,6},{10,4},{12,2},{14,0},{1,15},{3,13... | collective-permute-start | bytes 344072 | tf_op jit(solution)/shard_map/ppermute | solution.py:204
  35.4 10.2 %base.1 = (f32[128,1792]{1,0:T(8,128)S(1)}, f32[128,1792]{1,0:T(8,128)S(1)}) custom-call(s32[2]{0:T(128)S(1)} %pad_add_fusion.where.refs_0_, bf16[16,4096]{1,0:T(8,128)(2,1)S(1)} %copy-done.1, bf16[16,4096]{1,0:T(8,128)(2,1)S(1)} %collective-permute-done.refs_3_.refs_2_, bf16[16,4096]{1,0:T(8,128)(2,1)S(1)} %collective-permute-done.1.refs_4_.refs_3_, ...), custom_call_target="tpu_custom_call" | custom-call | flops 3758096384 | bytes 10000000 | tf_op jit(solution)/shard_map/base/pallas_call | solution.py:273
  45.7 0.1 collective-permute-start.10
  45.9 2.4 %collective-permute-done.10.other = f32[128,1792]{1,0:T(8,128)S(1)} collective-permute-done((f32[128,1792]{1,0:T(8,128)S(1)}, f32[128,1792]{1,0:T(8,128)S(1)}, u32[]{:S(2)}, u32[]{:S(2)}) %collective-permute-start.10) | collective-permute-done | bytes 917536 | tf_op jit(solution)/shard_map/ppermute | solution.py:289
  48.2 1.1 %combine.1 = bf16[128,1792]{1,0:T(8,128)(2,1)} custom-call(s32[1]{0:T(128)} %bitcast.refs_0_.where, bf16[256,128]{1,0:T(8,128)(2,1)S(1)} %place.1, f32[128,1792]{1,0:T(8,128)S(1)} %get-tuple-element.19.own, f32[128,1792]{1,0:T(8,128)S(1)} %collective-permute-done.10.other, bf16[32,1792]{1,0:T(8,128)(2,1)S(1)} %get-tuple-element.21.refs_0_, ...), custom_call_target="tpu_custom_call" | custom-call | flops 200000000 | bytes 4000000 | tf_op jit(solution)/shard_map/combine/pallas_call | solution.py:301
  (19 shorter events, 0.1 us)
Async XLA Ops:
  0.0 12.0 %collective-permute-start.3 = (bf16[16,4096]{1,0:T(8,128)(2,1)}, bf16[16,4096]{1,0:T(8,128)(2,1)S(1)}, u32[]{:S(2)}, u32[]{:S(2)}) collective-permute-start(bf16[16,4096]{1,0:T(8,128)(2,1)} %refs_1_.1), channel_id=1, source_target_pairs={{0,8},{2,10},{4,12},{6,14},{8,0},{10,2},{12,4},{14,6},{1,9},{3,11}... | collective-permute-start | bytes 393224 | tf_op jit(solution)/shard_map/ppermute | solution.py:204
  4.0 10.1 %collective-permute-start.1 = (bf16[16,4096]{1,0:T(8,128)(2,1)}, bf16[16,4096]{1,0:T(8,128)(2,1)S(1)}, u32[]{:S(2)}, u32[]{:S(2)}) collective-permute-start(bf16[16,4096]{1,0:T(8,128)(2,1)} %refs_1_.1), channel_id=1, source_target_pairs={{0,4},{2,6},{4,0},{6,2},{8,12},{10,14},{12,8},{14,10},{1,5},{3,7},... | collective-permute-start | bytes 393224 | tf_op jit(solution)/shard_map/ppermute | solution.py:204
  5.6 14.3 %collective-permute-start = (bf16[16,4096]{1,0:T(8,128)(2,1)}, bf16[16,4096]{1,0:T(8,128)(2,1)S(1)}, u32[]{:S(2)}, u32[]{:S(2)}) collective-permute-start(bf16[16,4096]{1,0:T(8,128)(2,1)} %refs_1_.1), channel_id=1, source_target_pairs={{0,2},{2,0},{4,6},{6,4},{8,10},{10,8},{12,14},{14,12},{1,3},{3,1},... | collective-permute-start | bytes 393224 | tf_op jit(solution)/shard_map/ppermute | solution.py:204
  7.1 12.8 %collective-permute-start.6 = (bf16[16,4096]{1,0:T(8,128)(2,1)}, bf16[16,4096]{1,0:T(8,128)(2,1)S(1)}, u32[]{:S(2)}, u32[]{:S(2)}) collective-permute-start(bf16[16,4096]{1,0:T(8,128)(2,1)} %refs_1_.1), channel_id=1, source_target_pairs={{0,14},{2,12},{4,10},{6,8},{8,6},{10,4},{12,2},{14,0},{1,15},{3,13... | collective-permute-start | bytes 393224 | tf_op jit(solution)/shard_map/ppermute | solution.py:204
  12.0 7.9 %collective-permute-start.4 = (bf16[16,4096]{1,0:T(8,128)(2,1)S(1)}, bf16[16,4096]{1,0:T(8,128)(2,1)S(1)}, u32[]{:S(2)}, u32[]{:S(2)}) collective-permute-start(bf16[16,4096]{1,0:T(8,128)(2,1)S(1)} %collective-permute-done.3.refs_6_.refs_5_), channel_id=1, source_target_pairs={{0,2},{2,0},{4,6},{6,4},{8,10},{10,8},{12,14},{14,12},{1,3},{3,1},... | collective-permute-start | bytes 393224 | tf_op jit(solution)/shard_map/ppermute | solution.py:204
  14.1 5.8 %collective-permute-start.5 = (bf16[16,4096]{1,0:T(8,128)(2,1)S(1)}, bf16[16,4096]{1,0:T(8,128)(2,1)S(1)}, u32[]{:S(2)}, u32[]{:S(2)}) collective-permute-start(bf16[16,4096]{1,0:T(8,128)(2,1)S(1)} %collective-permute-done.3.refs_6_.refs_5_), channel_id=1, source_target_pairs={{0,4},{2,6},{4,0},{6,2},{8,12},{10,14},{12,8},{14,10},{1,5},{3,7},... | collective-permute-start | bytes 393224 | tf_op jit(solution)/shard_map/ppermute | solution.py:204
  14.2 6.2 %collective-permute-start.2 = (bf16[16,4096]{1,0:T(8,128)(2,1)S(1)}, bf16[16,4096]{1,0:T(8,128)(2,1)S(1)}, u32[]{:S(2)}, u32[]{:S(2)}) collective-permute-start(bf16[16,4096]{1,0:T(8,128)(2,1)S(1)} %collective-permute-done.1.refs_4_.refs_3_), channel_id=1, source_target_pairs={{0,2},{2,0},{4,6},{6,4},{8,10},{10,8},{12,14},{14,12},{1,3},{3,1},... | collective-permute-start | bytes 393224 | tf_op jit(solution)/shard_map/ppermute | solution.py:204
  14.4 0.7 %copy-start.3 = (s32[8]{0:T(128)S(1)}, s32[8]{0:T(128)}, u32[]{:S(2)}) copy-start(s32[8]{0:T(128)} %index_map.1) | copy-start | bytes 100
  15.1 0.7 %copy-start.4 = (s32[128,1]{0,1:T(1,128)S(1)}, s32[128,1]{0,1:T(1,128)}, u32[]{:S(2)}) copy-start(s32[128,1]{0,1:T(1,128)} %param.12) | copy-start | bytes 1540
  15.7 4.6 %copy-start.1 = (bf16[16,4096]{1,0:T(8,128)(2,1)S(1)}, bf16[16,4096]{1,0:T(8,128)(2,1)}, u32[]{:S(2)}) copy-start(bf16[16,4096]{1,0:T(8,128)(2,1)} %refs_1_.1) | copy-start | bytes 393220
  15.7 4.6 %copy-start.2 = (bf16[1,64,4096]{2,1,0:T(8,128)(2,1)S(1)}, bf16[1,64,4096]{2,1,0:T(8,128)(2,1)}, u32[]{:S(2)}) copy-start(bf16[1,64,4096]{2,1,0:T(8,128)(2,1)} %param.9) | copy-start | bytes 1572868
  15.7 6.4 %copy-start = (bf16[1,64,8,1,1792]{4,2,3,1,0:T(8,128)(2,1)S(1)}, bf16[1,64,8,1,1792]{4,2,3,1,0:T(8,128)(2,1)}, u32[]{:S(2)}) copy-start(bf16[1,64,8,1,1792]{4,2,3,1,0:T(8,128)(2,1)} %param.10) | copy-start | bytes 5505028
  20.9 1.2 %collective-permute-start.7 = (f32[32,64]{1,0:T(8,128)S(1)}, f32[32,64]{1,0:T(8,128)S(1)}, u32[]{:S(2)}, u32[]{:S(2)}) collective-permute-start(f32[32,64]{1,0:T(8,128)S(1)} %lowrank.1.low_a._), channel_id=1, source_target_pairs={{0,1},{1,0},{2,3},{3,2},{4,5},{5,4},{6,7},{7,6},{8,9},{9,8},{10,11... | collective-permute-start | bytes 24584 | tf_op jit(solution)/shard_map/ppermute | solution.py:247
  22.8 9.1 %collective-permute-start.9 = (bf16[32,1792]{1,0:T(8,128)(2,1)S(1)}, bf16[32,1792]{1,0:T(8,128)(2,1)S(1)}, u32[]{:S(2)}, u32[]{:S(2)}) collective-permute-start(bf16[32,1792]{1,0:T(8,128)(2,1)S(1)} %get-tuple-element.18), channel_id=1, source_target_pairs={{0,4},{2,6},{4,0},{6,2},{8,12},{10,14},{12,8},{14,10},{1,5},{3,7},... | collective-permute-start | bytes 344072 | tf_op jit(solution)/shard_map/ppermute | solution.py:204
  24.3 8.6 %collective-permute-start.8 = (bf16[32,1792]{1,0:T(8,128)(2,1)S(1)}, bf16[32,1792]{1,0:T(8,128)(2,1)S(1)}, u32[]{:S(2)}, u32[]{:S(2)}) collective-permute-start(bf16[32,1792]{1,0:T(8,128)(2,1)S(1)} %get-tuple-element.17), channel_id=1, source_target_pairs={{0,2},{2,0},{4,6},{6,4},{8,10},{10,8},{12,14},{14,12},{1,3},{3,1},... | collective-permute-start | bytes 344072 | tf_op jit(solution)/shard_map/ppermute | solution.py:204
  26.2 19.5 %collective-permute-start.12 = (bf16[32,1792]{1,0:T(8,128)(2,1)S(1)}, bf16[32,1792]{1,0:T(8,128)(2,1)S(1)}, u32[]{:S(2)}, u32[]{:S(2)}) collective-permute-start(bf16[32,1792]{1,0:T(8,128)(2,1)S(1)} %get-tuple-element.22), channel_id=1, source_target_pairs={{0,8},{2,10},{4,12},{6,14},{8,0},{10,2},{12,4},{14,6},{1,9},{3,11}... | collective-permute-start | bytes 344072 | tf_op jit(solution)/shard_map/ppermute | solution.py:204
  27.9 17.9 %collective-permute-start.13 = (bf16[32,1792]{1,0:T(8,128)(2,1)S(1)}, bf16[32,1792]{1,0:T(8,128)(2,1)S(1)}, u32[]{:S(2)}, u32[]{:S(2)}) collective-permute-start(bf16[32,1792]{1,0:T(8,128)(2,1)S(1)} %get-tuple-element.23), channel_id=1, source_target_pairs={{0,10},{2,8},{4,14},{6,12},{8,2},{10,0},{12,6},{14,4},{1,11},{3,9}... | collective-permute-start | bytes 344072 | tf_op jit(solution)/shard_map/ppermute | solution.py:204
  28.7 17.1 %collective-permute-start.14 = (bf16[32,1792]{1,0:T(8,128)(2,1)S(1)}, bf16[32,1792]{1,0:T(8,128)(2,1)S(1)}, u32[]{:S(2)}, u32[]{:S(2)}) collective-permute-start(bf16[32,1792]{1,0:T(8,128)(2,1)S(1)} %get-tuple-element.24), channel_id=1, source_target_pairs={{0,12},{2,14},{4,8},{6,10},{8,4},{10,6},{12,0},{14,2},{1,13},{3,15... | collective-permute-start | bytes 344072 | tf_op jit(solution)/shard_map/ppermute | solution.py:204
  32.3 13.5 %collective-permute-start.11 = (bf16[32,1792]{1,0:T(8,128)(2,1)S(1)}, bf16[32,1792]{1,0:T(8,128)(2,1)S(1)}, u32[]{:S(2)}, u32[]{:S(2)}) collective-permute-start(bf16[32,1792]{1,0:T(8,128)(2,1)S(1)} %delta.5.refs_12_), channel_id=1, source_target_pairs={{0,6},{2,4},{4,2},{6,0},{8,14},{10,12},{12,10},{14,8},{1,7},{3,5},... | collective-permute-start | bytes 344072 | tf_op jit(solution)/shard_map/ppermute | solution.py:204
  33.3 12.5 %collective-permute-start.15 = (bf16[32,1792]{1,0:T(8,128)(2,1)S(1)}, bf16[32,1792]{1,0:T(8,128)(2,1)S(1)}, u32[]{:S(2)}, u32[]{:S(2)}) collective-permute-start(bf16[32,1792]{1,0:T(8,128)(2,1)S(1)} %delta.4.refs_11_), channel_id=1, source_target_pairs={{0,14},{2,12},{4,10},{6,8},{8,6},{10,4},{12,2},{14,0},{1,15},{3,13... | collective-permute-start | bytes 344072 | tf_op jit(solution)/shard_map/ppermute | solution.py:204
  45.7 2.5 %collective-permute-start.10 = (f32[128,1792]{1,0:T(8,128)S(1)}, f32[128,1792]{1,0:T(8,128)S(1)}, u32[]{:S(2)}, u32[]{:S(2)}) collective-permute-start(f32[128,1792]{1,0:T(8,128)S(1)} %get-tuple-element.20), channel_id=1, source_target_pairs={{0,1},{1,0},{2,3},{3,2},{4,5},{5,4},{6,7},{7,6},{8,9},{9,8},{10,11... | collective-permute-start | bytes 2752520 | tf_op jit(solution)/shard_map/ppermute | solution.py:289

commit v5 on v4

--- a/solution.py
+++ b/solution.py
@@ -108,11 +108,15 @@
     )
 
 
+def relay_kernel(block, _, out):
+    out[...] = block[...]
+
+
 def delta_kernel(groups, offsets, where, scale, low_a, low_b, up, _, *refs):
     outs, spread = refs[:-1], refs[-1]
     me = where[0]
     rank = low_a.shape[1]
-    low = ((low_a[...] + low_b[...]) * scale[0]).astype(BF16)
+    low = ((low_a[...] + low_b[...]) * scale[...]).astype(BF16)
     depth = rank * groups
     widen = (
         lax.broadcasted_iota(jnp.int32, (rank, depth), 0)
@@ -252,21 +256,34 @@
         return pl.pallas_call(
             functools.partial(delta_kernel, groups, offsets),
             out_shape=[jax.ShapeDtypeStruct((CAP, width), BF16)] * len(offsets),
-            in_specs=[SMEM, SMEM, VMEM, VMEM, VMEM, ANY],
+            in_specs=[SMEM, VMEM, VMEM, VMEM, VMEM, ANY],
             out_specs=[VMEM] * len(offsets),
             scratch_shapes=[pltpu.VMEM((len(offsets) * CAP, rank * groups), BF16)],
             compiler_params=params(8),
             cost_estimate=pl.CostEstimate(flops=10**6, bytes_accessed=10**6, transcendentals=0),
             name="delta",
-        )(where, adapter_scales, low, low_other, up, after)
+        )(where, adapter_scales.reshape(1, 1), low, low_other, up, after)
 
     arrived = [None] * groups
-    blocks = deltas((0, 2, 1, 4, 5, 6), low)
-    for d, x in zip((0, 2, 1, 4, 5, 6), blocks):
+    order = (0, 2, 1, 4, 5, 6, 7, 3)
+    blocks = deltas(order, low)
+    for d, x in zip(order[:6], blocks):
         arrived[d] = to(x, d) if d else x
-    seventh = deltas((7,), arrived[1])[0]
+
+    def once(block, after):
+        return pl.pallas_call(
+            relay_kernel,
+            out_shape=jax.ShapeDtypeStruct(block.shape, block.dtype),
+            in_specs=[VMEM, ANY],
+            out_specs=VMEM,
+            compiler_params=params(2),
+            cost_estimate=pl.CostEstimate(flops=10**4, bytes_accessed=10**4, transcendentals=0),
+            name="relay",
+        )(block, after)
+
+    seventh = once(blocks[6], arrived[1])
     arrived[7] = to(seventh, 7)
-    eighth = deltas((3,), arrived[2])[0]
+    eighth = once(blocks[7], arrived[2])
     arrived[3] = to(eighth, 3)
 
     half = jax.ShapeDtypeStruct((rows, width), F32)

time: 49.5 us -> 48.7 us (0.984)
  Pallas kernels: 17.7 us -> 16.9 us
    pallas_call x3 -> x1, Pallas kernels: 1.6 us -> 0.8 us  [deltas(): pl.pallas_call(functools.partial(delta_kernel, groups, offsets), out_shap...]
  transfers between devices with their start and end apart: 16 -> 16, of which waited for: 4 -> 4; matrix products, arithmetic and copies ran while one was open for 0% -> 0% of each run, Pallas kernels for 31% -> 30%
where the time goes in v5:
time: 48.7 us; the launch traced here: 48.6 us
  starting transfers between devices  21.2 us (44%)
  Pallas kernels  16.9 us (35%)
  waiting for transfers between devices  8.2 us (17%)
  local copies, waits for them, and re-layouts  1.32 us (3%)
  between operations  0.8 us (2%)
    ppermute x14, starting transfers between devices, to(): return lax.ppermute(x, 'rows', [(i, i ^ d) for i in range(groups)])  21.2 us
    pallas_call x1, Pallas kernels, few_groups(): pl.pallas_call(functools.partial(base_kernel, groups), in_specs=[SMEM] +...  10.3 us
    ppermute x14, waiting for transfers between devices, to(): return lax.ppermute(x, 'rows', [(i, i ^ d) for i in range(groups)])  5.28 us
    pallas_call x1, Pallas kernels, few_groups(): pl.pallas_call(slots_kernel, out_shape=[jax.ShapeDtypeStruct((1, rows), j...  4.16 us
    ppermute x1, waiting for transfers between devices, few_groups(): other = lax.ppermute(partner, 'tp', swap)  2.39 us
    unnamed x10, local copies, waits for them, and re-layouts  1.32 us
    pallas_call x1, Pallas kernels, few_groups(): pl.pallas_call(functools.partial(final_kernel, groups), out_shape=jax.Sha...  1.13 us
  transfers between devices with their start and end apart: 16, of which 4 were waited for; matrix products, arithmetic and copies ran while one was open for 0% of the time, Pallas kernels for 30%

profile of v5, /device:TPU:0, one launch (start us, length us, event | category | flops | bytes accessed | tf_op | source)
XLA Modules:
  0.0 48.6 jit_solution(11331550592220719946)
XLA Ops:
  0.0 4.0 %collective-permute-start.3 = (bf16[16,4096]{1,0:T(8,128)(2,1)}, bf16[16,4096]{1,0:T(8,128)(2,1)S(1)}, u32[]{:S(2)}, u32[]{:S(2)}) collective-permute-start(bf16[16,4096]{1,0:T(8,128)(2,1)} %refs_1_.1), channel_id=1, source_target_pairs={{0,8},{2,10},{4,12},{6,14},{8,0},{10,2},{12,4},{14,6},{1,9},{3,11}... | collective-permute-start | bytes 393224 | tf_op jit(solution)/shard_map/ppermute | solution.py:208
  4.0 1.6 %collective-permute-start.1 = (bf16[16,4096]{1,0:T(8,128)(2,1)}, bf16[16,4096]{1,0:T(8,128)(2,1)S(1)}, u32[]{:S(2)}, u32[]{:S(2)}) collective-permute-start(bf16[16,4096]{1,0:T(8,128)(2,1)} %refs_1_.1), channel_id=1, source_target_pairs={{0,4},{2,6},{4,0},{6,2},{8,12},{10,14},{12,8},{14,10},{1,5},{3,7},... | collective-permute-start | bytes 393224 | tf_op jit(solution)/shard_map/ppermute | solution.py:208
  5.6 1.5 %collective-permute-start = (bf16[16,4096]{1,0:T(8,128)(2,1)}, bf16[16,4096]{1,0:T(8,128)(2,1)S(1)}, u32[]{:S(2)}, u32[]{:S(2)}) collective-permute-start(bf16[16,4096]{1,0:T(8,128)(2,1)} %refs_1_.1), channel_id=1, source_target_pairs={{0,2},{2,0},{4,6},{6,4},{8,10},{10,8},{12,14},{14,12},{1,3},{3,1},... | collective-permute-start | bytes 393224 | tf_op jit(solution)/shard_map/ppermute | solution.py:208
  7.1 0.1 pad_add_fusion.where.refs_0_
  7.2 4.8 %collective-permute-done.3.refs_6_.refs_5_ = bf16[16,4096]{1,0:T(8,128)(2,1)S(1)} collective-permute-done((bf16[16,4096]{1,0:T(8,128)(2,1)}, bf16[16,4096]{1,0:T(8,128)(2,1)S(1)}, u32[]{:S(2)}, u32[]{:S(2)}) %collective-permute-start.3) | collective-permute-done | bytes 131104 | tf_op jit(solution)/shard_map/ppermute | solution.py:208
  12.0 2.1 %collective-permute-start.4 = (bf16[16,4096]{1,0:T(8,128)(2,1)S(1)}, bf16[16,4096]{1,0:T(8,128)(2,1)S(1)}, u32[]{:S(2)}, u32[]{:S(2)}) collective-permute-start(bf16[16,4096]{1,0:T(8,128)(2,1)S(1)} %collective-permute-done.3.refs_6_.refs_5_), channel_id=1, source_target_pairs={{0,2},{2,0},{4,6},{6,4},{8,10},{10,8},{12,14},{14,12},{1,3},{3,1},... | collective-permute-start | bytes 393224 | tf_op jit(solution)/shard_map/ppermute | solution.py:208
  14.1 0.0 collective-permute-start.5
  14.2 0.0 collective-permute-done.1.refs_4_.refs_3_
  14.2 0.3 collective-permute-start.2
  14.4 0.7 %copy-done.3 = s32[8]{0:T(128)S(1)} copy-done((s32[8]{0:T(128)S(1)}, s32[8]{0:T(128)}, u32[]{:S(2)}) %copy-start.3) | copy-done | bytes 56
  15.1 0.7 %copy-done.4 = s32[128,1]{0,1:T(1,128)S(1)} copy-done((s32[128,1]{0,1:T(1,128)S(1)}, s32[128,1]{0,1:T(1,128)}, u32[]{:S(2)}) %copy-start.4) | copy-done | bytes 536
  15.7 4.2 %slots.1 = (s32[1,128]{1,0:T(1,128)S(1)}, bf16[4096,1024]{1,0:T(8,128)(2,1)S(1)}) custom-call(s32[2]{0:T(128)S(1)} %pad_add_fusion.where.refs_0_, s32[8]{0:T(128)S(1)} %copy-done.3, s32[1,128]{1,0:T(1,128)S(1)} %bitcast.9, bf16[4096,3584]{1,0:T(8,128)(2,1)} %refs_10_.1), custom_call_target="tpu_custom_call" | custom-call | flops 99999997952 | bytes 100000000 | tf_op jit(solution)/shard_map/slots/pallas_call | solution.py:215
  19.9 0.0 collective-permute-done.refs_3_.refs_2_
  19.9 0.0 collective-permute-done.6.refs_9_.refs_8_
  19.9 0.0 collective-permute-done.5.refs_8_.refs_7_
  19.9 0.4 collective-permute-done.2.refs_5_.refs_4_
  20.4 0.6 %lowrank.1.low_a._ = f32[32,64]{1,0:T(8,128)S(1)} custom-call(s32[1]{0:T(128)} %bitcast.refs_0_.where, s32[1,128]{1,0:T(1,128)S(1)} %get-tuple-element.17.slots.refs_1_, bf16[16,4096]{1,0:T(8,128)(2,1)S(1)} %copy-done.1, bf16[16,4096]{1,0:T(8,128)(2,1)S(1)} %collective-permute-done.refs_3_.refs_2_, ...), custom_call_target="tpu_custom_call" | custom-call | flops 100000000 | bytes 2000000 | tf_op jit(solution)/shard_map/lowrank/pallas_call | solution.py:241
  20.9 0.0 collective-permute-start.7
  21.6 0.5 %collective-permute-done.7.low_b = f32[32,64]{1,0:T(8,128)S(1)} collective-permute-done((f32[32,64]{1,0:T(8,128)S(1)}, f32[32,64]{1,0:T(8,128)S(1)}, u32[]{:S(2)}, u32[]{:S(2)}) %collective-permute-start.7) | collective-permute-done | bytes 8224 | tf_op jit(solution)/shard_map/ppermute | solution.py:251
  22.1 0.8 %delta.1 = (bf16[32,1792]{1,0:T(8,128)(2,1)S(1)}, bf16[32,1792]{1,0:T(8,128)(2,1)S(1)}, bf16[32,1792]{1,0:T(8,128)(2,1)S(1)}, bf16[32,1792]{1,0:T(8,128)(2,1)S(1...) custom-call(s32[1]{0:T(128)} %bitcast.refs_0_.where, ...), custom_call_target="tpu_custom_call" | custom-call | flops 1000000 | bytes 1000000 | tf_op jit(solution)/shard_map/delta/pallas_call | solution.py:256
  22.9 1.5 %collective-permute-start.9 = (bf16[32,1792]{1,0:T(8,128)(2,1)S(1)}, bf16[32,1792]{1,0:T(8,128)(2,1)S(1)}, u32[]{:S(2)}, u32[]{:S(2)}) collective-permute-start(bf16[32,1792]{1,0:T(8,128)(2,1)S(1)} %get-tuple-element.22), channel_id=1, source_target_pairs={{0,4},{2,6},{4,0},{6,2},{8,12},{10,14},{12,8},{14,10},{1,5},{3,7},... | collective-permute-start | bytes 344072 | tf_op jit(solution)/shard_map/ppermute | solution.py:208
  24.5 1.9 %collective-permute-start.8 = (bf16[32,1792]{1,0:T(8,128)(2,1)S(1)}, bf16[32,1792]{1,0:T(8,128)(2,1)S(1)}, u32[]{:S(2)}, u32[]{:S(2)}) collective-permute-start(bf16[32,1792]{1,0:T(8,128)(2,1)S(1)} %get-tuple-element.20), channel_id=1, source_target_pairs={{0,2},{2,0},{4,6},{6,4},{8,10},{10,8},{12,14},{14,12},{1,3},{3,1},... | collective-permute-start | bytes 344072 | tf_op jit(solution)/shard_map/ppermute | solution.py:208
  26.4 1.7 %collective-permute-start.12 = (bf16[32,1792]{1,0:T(8,128)(2,1)S(1)}, bf16[32,1792]{1,0:T(8,128)(2,1)S(1)}, u32[]{:S(2)}, u32[]{:S(2)}) collective-permute-start(bf16[32,1792]{1,0:T(8,128)(2,1)S(1)} %get-tuple-element.26), channel_id=1, source_target_pairs={{0,8},{2,10},{4,12},{6,14},{8,0},{10,2},{12,4},{14,6},{1,9},{3,11}... | collective-permute-start | bytes 344072 | tf_op jit(solution)/shard_map/ppermute | solution.py:208
  28.1 0.8 %collective-permute-start.13 = (bf16[32,1792]{1,0:T(8,128)(2,1)S(1)}, bf16[32,1792]{1,0:T(8,128)(2,1)S(1)}, u32[]{:S(2)}, u32[]{:S(2)}) collective-permute-start(bf16[32,1792]{1,0:T(8,128)(2,1)S(1)} %get-tuple-element.27), channel_id=1, source_target_pairs={{0,10},{2,8},{4,14},{6,12},{8,2},{10,0},{12,6},{14,4},{1,11},{3,9}... | collective-permute-start | bytes 344072 | tf_op jit(solution)/shard_map/ppermute | solution.py:208
  28.8 3.1 %collective-permute-start.14 = (bf16[32,1792]{1,0:T(8,128)(2,1)S(1)}, bf16[32,1792]{1,0:T(8,128)(2,1)S(1)}, u32[]{:S(2)}, u32[]{:S(2)}) collective-permute-start(bf16[32,1792]{1,0:T(8,128)(2,1)S(1)} %get-tuple-element.28), channel_id=1, source_target_pairs={{0,12},{2,14},{4,8},{6,10},{8,4},{10,6},{12,0},{14,2},{1,13},{3,15... | collective-permute-start | bytes 344072 | tf_op jit(solution)/shard_map/ppermute | solution.py:208
  32.0 0.0 collective-permute-done.9._.refs_2_
  32.0 0.5 %collective-permute-start.11 = (bf16[32,1792]{1,0:T(8,128)(2,1)S(1)}, bf16[32,1792]{1,0:T(8,128)(2,1)S(1)}, u32[]{:S(2)}, u32[]{:S(2)}) collective-permute-start(bf16[32,1792]{1,0:T(8,128)(2,1)S(1)} %relay.3.refs_12_), channel_id=1, source_target_pairs={{0,6},{2,4},{4,2},{6,0},{8,14},{10,12},{12,10},{14,8},{1,7},{3,5},... | collective-permute-start | bytes 344072 | tf_op jit(solution)/shard_map/ppermute | solution.py:208
  32.6 2.1 %collective-permute-start.15 = (bf16[32,1792]{1,0:T(8,128)(2,1)S(1)}, bf16[32,1792]{1,0:T(8,128)(2,1)S(1)}, u32[]{:S(2)}, u32[]{:S(2)}) collective-permute-start(bf16[32,1792]{1,0:T(8,128)(2,1)S(1)} %relay.2.refs_11_), channel_id=1, source_target_pairs={{0,14},{2,12},{4,10},{6,8},{8,6},{10,4},{12,2},{14,0},{1,15},{3,13... | collective-permute-start | bytes 344072 | tf_op jit(solution)/shard_map/ppermute | solution.py:208
  34.6 10.3 %base.1 = (f32[128,1792]{1,0:T(8,128)S(1)}, f32[128,1792]{1,0:T(8,128)S(1)}) custom-call(s32[2]{0:T(128)S(1)} %pad_add_fusion.where.refs_0_, bf16[16,4096]{1,0:T(8,128)(2,1)S(1)} %copy-done.1, bf16[16,4096]{1,0:T(8,128)(2,1)S(1)} %collective-permute-done.refs_3_.refs_2_, bf16[16,4096]{1,0:T(8,128)(2,1)S(1)} %collective-permute-done.1.refs_4_.refs_3_, ...), custom_call_target="tpu_custom_call" | custom-call | flops 3758096384 | bytes 10000000 | tf_op jit(solution)/shard_map/base/pallas_call | solution.py:290
  44.9 0.1 collective-permute-start.10
  45.1 2.4 %collective-permute-done.10.other = f32[128,1792]{1,0:T(8,128)S(1)} collective-permute-done((f32[128,1792]{1,0:T(8,128)S(1)}, f32[128,1792]{1,0:T(8,128)S(1)}, u32[]{:S(2)}, u32[]{:S(2)}) %collective-permute-start.10) | collective-permute-done | bytes 917536 | tf_op jit(solution)/shard_map/ppermute | solution.py:306
  47.5 1.1 %combine.1 = bf16[128,1792]{1,0:T(8,128)(2,1)} custom-call(s32[1]{0:T(128)} %bitcast.refs_0_.where, bf16[256,128]{1,0:T(8,128)(2,1)S(1)} %place.1, f32[128,1792]{1,0:T(8,128)S(1)} %get-tuple-element.23.own, f32[128,1792]{1,0:T(8,128)S(1)} %collective-permute-done.10.other, bf16[32,1792]{1,0:T(8,128)(2,1)S(1)} %get-tuple-element.25.refs_0_, ...), custom_call_target="tpu_custom_call" | custom-call | flops 200000000 | bytes 4000000 | tf_op jit(solution)/shard_map/combine/pallas_call | solution.py:318
  (19 shorter events, 0.1 us)
Async XLA Ops:
  0.0 12.0 %collective-permute-start.3 = (bf16[16,4096]{1,0:T(8,128)(2,1)}, bf16[16,4096]{1,0:T(8,128)(2,1)S(1)}, u32[]{:S(2)}, u32[]{:S(2)}) collective-permute-start(bf16[16,4096]{1,0:T(8,128)(2,1)} %refs_1_.1), channel_id=1, source_target_pairs={{0,8},{2,10},{4,12},{6,14},{8,0},{10,2},{12,4},{14,6},{1,9},{3,11}... | collective-permute-start | bytes 393224 | tf_op jit(solution)/shard_map/ppermute | solution.py:208
  4.0 10.1 %collective-permute-start.1 = (bf16[16,4096]{1,0:T(8,128)(2,1)}, bf16[16,4096]{1,0:T(8,128)(2,1)S(1)}, u32[]{:S(2)}, u32[]{:S(2)}) collective-permute-start(bf16[16,4096]{1,0:T(8,128)(2,1)} %refs_1_.1), channel_id=1, source_target_pairs={{0,4},{2,6},{4,0},{6,2},{8,12},{10,14},{12,8},{14,10},{1,5},{3,7},... | collective-permute-start | bytes 393224 | tf_op jit(solution)/shard_map/ppermute | solution.py:208
  5.6 14.3 %collective-permute-start = (bf16[16,4096]{1,0:T(8,128)(2,1)}, bf16[16,4096]{1,0:T(8,128)(2,1)S(1)}, u32[]{:S(2)}, u32[]{:S(2)}) collective-permute-start(bf16[16,4096]{1,0:T(8,128)(2,1)} %refs_1_.1), channel_id=1, source_target_pairs={{0,2},{2,0},{4,6},{6,4},{8,10},{10,8},{12,14},{14,12},{1,3},{3,1},... | collective-permute-start | bytes 393224 | tf_op jit(solution)/shard_map/ppermute | solution.py:208
  7.1 12.8 %collective-permute-start.6 = (bf16[16,4096]{1,0:T(8,128)(2,1)}, bf16[16,4096]{1,0:T(8,128)(2,1)S(1)}, u32[]{:S(2)}, u32[]{:S(2)}) collective-permute-start(bf16[16,4096]{1,0:T(8,128)(2,1)} %refs_1_.1), channel_id=1, source_target_pairs={{0,14},{2,12},{4,10},{6,8},{8,6},{10,4},{12,2},{14,0},{1,15},{3,13... | collective-permute-start | bytes 393224 | tf_op jit(solution)/shard_map/ppermute | solution.py:208
  12.0 7.9 %collective-permute-start.4 = (bf16[16,4096]{1,0:T(8,128)(2,1)S(1)}, bf16[16,4096]{1,0:T(8,128)(2,1)S(1)}, u32[]{:S(2)}, u32[]{:S(2)}) collective-permute-start(bf16[16,4096]{1,0:T(8,128)(2,1)S(1)} %collective-permute-done.3.refs_6_.refs_5_), channel_id=1, source_target_pairs={{0,2},{2,0},{4,6},{6,4},{8,10},{10,8},{12,14},{14,12},{1,3},{3,1},... | collective-permute-start | bytes 393224 | tf_op jit(solution)/shard_map/ppermute | solution.py:208
  14.1 5.8 %collective-permute-start.5 = (bf16[16,4096]{1,0:T(8,128)(2,1)S(1)}, bf16[16,4096]{1,0:T(8,128)(2,1)S(1)}, u32[]{:S(2)}, u32[]{:S(2)}) collective-permute-start(bf16[16,4096]{1,0:T(8,128)(2,1)S(1)} %collective-permute-done.3.refs_6_.refs_5_), channel_id=1, source_target_pairs={{0,4},{2,6},{4,0},{6,2},{8,12},{10,14},{12,8},{14,10},{1,5},{3,7},... | collective-permute-start | bytes 393224 | tf_op jit(solution)/shard_map/ppermute | solution.py:208
  14.2 6.2 %collective-permute-start.2 = (bf16[16,4096]{1,0:T(8,128)(2,1)S(1)}, bf16[16,4096]{1,0:T(8,128)(2,1)S(1)}, u32[]{:S(2)}, u32[]{:S(2)}) collective-permute-start(bf16[16,4096]{1,0:T(8,128)(2,1)S(1)} %collective-permute-done.1.refs_4_.refs_3_), channel_id=1, source_target_pairs={{0,2},{2,0},{4,6},{6,4},{8,10},{10,8},{12,14},{14,12},{1,3},{3,1},... | collective-permute-start | bytes 393224 | tf_op jit(solution)/shard_map/ppermute | solution.py:208
  14.4 0.7 %copy-start.3 = (s32[8]{0:T(128)S(1)}, s32[8]{0:T(128)}, u32[]{:S(2)}) copy-start(s32[8]{0:T(128)} %index_map.1) | copy-start | bytes 100
  15.1 0.7 %copy-start.4 = (s32[128,1]{0,1:T(1,128)S(1)}, s32[128,1]{0,1:T(1,128)}, u32[]{:S(2)}) copy-start(s32[128,1]{0,1:T(1,128)} %param.12) | copy-start | bytes 1540
  15.7 4.6 %copy-start.1 = (bf16[16,4096]{1,0:T(8,128)(2,1)S(1)}, bf16[16,4096]{1,0:T(8,128)(2,1)}, u32[]{:S(2)}) copy-start(bf16[16,4096]{1,0:T(8,128)(2,1)} %refs_1_.1) | copy-start | bytes 393220
  15.7 4.6 %copy-start.2 = (bf16[1,64,4096]{2,1,0:T(8,128)(2,1)S(1)}, bf16[1,64,4096]{2,1,0:T(8,128)(2,1)}, u32[]{:S(2)}) copy-start(bf16[1,64,4096]{2,1,0:T(8,128)(2,1)} %param.9) | copy-start | bytes 1572868
  15.7 6.4 %copy-start = (bf16[1,64,8,1,1792]{4,2,3,1,0:T(8,128)(2,1)S(1)}, bf16[1,64,8,1,1792]{4,2,3,1,0:T(8,128)(2,1)}, u32[]{:S(2)}) copy-start(bf16[1,64,8,1,1792]{4,2,3,1,0:T(8,128)(2,1)} %param.10) | copy-start | bytes 5505028
  20.9 1.2 %collective-permute-start.7 = (f32[32,64]{1,0:T(8,128)S(1)}, f32[32,64]{1,0:T(8,128)S(1)}, u32[]{:S(2)}, u32[]{:S(2)}) collective-permute-start(f32[32,64]{1,0:T(8,128)S(1)} %lowrank.1.low_a._), channel_id=1, source_target_pairs={{0,1},{1,0},{2,3},{3,2},{4,5},{5,4},{6,7},{7,6},{8,9},{9,8},{10,11... | collective-permute-start | bytes 24584 | tf_op jit(solution)/shard_map/ppermute | solution.py:251
  22.9 9.1 %collective-permute-start.9 = (bf16[32,1792]{1,0:T(8,128)(2,1)S(1)}, bf16[32,1792]{1,0:T(8,128)(2,1)S(1)}, u32[]{:S(2)}, u32[]{:S(2)}) collective-permute-start(bf16[32,1792]{1,0:T(8,128)(2,1)S(1)} %get-tuple-element.22), channel_id=1, source_target_pairs={{0,4},{2,6},{4,0},{6,2},{8,12},{10,14},{12,8},{14,10},{1,5},{3,7},... | collective-permute-start | bytes 344072 | tf_op jit(solution)/shard_map/ppermute | solution.py:208
  24.5 8.1 %collective-permute-start.8 = (bf16[32,1792]{1,0:T(8,128)(2,1)S(1)}, bf16[32,1792]{1,0:T(8,128)(2,1)S(1)}, u32[]{:S(2)}, u32[]{:S(2)}) collective-permute-start(bf16[32,1792]{1,0:T(8,128)(2,1)S(1)} %get-tuple-element.20), channel_id=1, source_target_pairs={{0,2},{2,0},{4,6},{6,4},{8,10},{10,8},{12,14},{14,12},{1,3},{3,1},... | collective-permute-start | bytes 344072 | tf_op jit(solution)/shard_map/ppermute | solution.py:208
  26.4 18.5 %collective-permute-start.12 = (bf16[32,1792]{1,0:T(8,128)(2,1)S(1)}, bf16[32,1792]{1,0:T(8,128)(2,1)S(1)}, u32[]{:S(2)}, u32[]{:S(2)}) collective-permute-start(bf16[32,1792]{1,0:T(8,128)(2,1)S(1)} %get-tuple-element.26), channel_id=1, source_target_pairs={{0,8},{2,10},{4,12},{6,14},{8,0},{10,2},{12,4},{14,6},{1,9},{3,11}... | collective-permute-start | bytes 344072 | tf_op jit(solution)/shard_map/ppermute | solution.py:208
  28.1 17.0 %collective-permute-start.13 = (bf16[32,1792]{1,0:T(8,128)(2,1)S(1)}, bf16[32,1792]{1,0:T(8,128)(2,1)S(1)}, u32[]{:S(2)}, u32[]{:S(2)}) collective-permute-start(bf16[32,1792]{1,0:T(8,128)(2,1)S(1)} %get-tuple-element.27), channel_id=1, source_target_pairs={{0,10},{2,8},{4,14},{6,12},{8,2},{10,0},{12,6},{14,4},{1,11},{3,9}... | collective-permute-start | bytes 344072 | tf_op jit(solution)/shard_map/ppermute | solution.py:208
  28.8 16.2 %collective-permute-start.14 = (bf16[32,1792]{1,0:T(8,128)(2,1)S(1)}, bf16[32,1792]{1,0:T(8,128)(2,1)S(1)}, u32[]{:S(2)}, u32[]{:S(2)}) collective-permute-start(bf16[32,1792]{1,0:T(8,128)(2,1)S(1)} %get-tuple-element.28), channel_id=1, source_target_pairs={{0,12},{2,14},{4,8},{6,10},{8,4},{10,6},{12,0},{14,2},{1,13},{3,15... | collective-permute-start | bytes 344072 | tf_op jit(solution)/shard_map/ppermute | solution.py:208
  32.0 13.0 %collective-permute-start.11 = (bf16[32,1792]{1,0:T(8,128)(2,1)S(1)}, bf16[32,1792]{1,0:T(8,128)(2,1)S(1)}, u32[]{:S(2)}, u32[]{:S(2)}) collective-permute-start(bf16[32,1792]{1,0:T(8,128)(2,1)S(1)} %relay.3.refs_12_), channel_id=1, source_target_pairs={{0,6},{2,4},{4,2},{6,0},{8,14},{10,12},{12,10},{14,8},{1,7},{3,5},... | collective-permute-start | bytes 344072 | tf_op jit(solution)/shard_map/ppermute | solution.py:208
  32.6 12.5 %collective-permute-start.15 = (bf16[32,1792]{1,0:T(8,128)(2,1)S(1)}, bf16[32,1792]{1,0:T(8,128)(2,1)S(1)}, u32[]{:S(2)}, u32[]{:S(2)}) collective-permute-start(bf16[32,1792]{1,0:T(8,128)(2,1)S(1)} %relay.2.refs_11_), channel_id=1, source_target_pairs={{0,14},{2,12},{4,10},{6,8},{8,6},{10,4},{12,2},{14,0},{1,15},{3,13... | collective-permute-start | bytes 344072 | tf_op jit(solution)/shard_map/ppermute | solution.py:208
  44.9 2.5 %collective-permute-start.10 = (f32[128,1792]{1,0:T(8,128)S(1)}, f32[128,1792]{1,0:T(8,128)S(1)}, u32[]{:S(2)}, u32[]{:S(2)}) collective-permute-start(f32[128,1792]{1,0:T(8,128)S(1)} %get-tuple-element.24), channel_id=1, source_target_pairs={{0,1},{1,0},{2,3},{3,2},{4,5},{5,4},{6,7},{7,6},{8,9},{9,8},{10,11... | collective-permute-start | bytes 2752520 | tf_op jit(solution)/shard_map/ppermute | solution.py:306

commit v6 on v5

--- a/solution.py
+++ b/solution.py
@@ -178,7 +178,7 @@
     ).astype(F32).astype(BF16)
 
 
-def final_kernel(groups, where, place, own, other, *refs):
+def middle_kernel(groups, where, place, own, *refs):
     pieces, out, arrived = refs[:groups], refs[-2], refs[-1]
     me = where[0]
     for d in range(groups):
@@ -187,7 +187,11 @@
     delta = lax.dot_general(
         place[...], arrived[...], (((0,), (0,)), ((), ())), preferred_element_type=F32
     )
-    out[...] = (own[...] + other[...] + delta).astype(BF16)
+    out[...] = own[...] + delta
+
+
+def final_kernel(middle, other, out):
+    out[...] = (middle[...] + other[...]).astype(BF16)
 
 
 def few_groups(
@@ -281,9 +285,9 @@
             name="relay",
         )(block, after)
 
-    seventh = once(blocks[6], arrived[1])
+    seventh = once(blocks[6], arrived[2])
     arrived[7] = to(seventh, 7)
-    eighth = once(blocks[7], arrived[2])
+    eighth = once(blocks[7], arrived[1])
     arrived[3] = to(eighth, 3)
 
     half = jax.ShapeDtypeStruct((rows, width), F32)
@@ -315,16 +319,26 @@
         name="place",
     )(slot)
 
-    return pl.pallas_call(
-        functools.partial(final_kernel, groups),
-        out_shape=jax.ShapeDtypeStruct((rows, width), BF16),
-        in_specs=[SMEM, VMEM, VMEM, VMEM] + [VMEM] * groups,
+    middle = pl.pallas_call(
+        functools.partial(middle_kernel, groups),
+        out_shape=jax.ShapeDtypeStruct((rows, width), F32),
+        in_specs=[SMEM, VMEM, VMEM] + [VMEM] * groups,
         out_specs=VMEM,
         scratch_shapes=[pltpu.VMEM((groups * CAP, width), BF16)],
         compiler_params=params(8),
         cost_estimate=pl.CostEstimate(flops=2 * 10**8, bytes_accessed=4 * 10**6, transcendentals=0),
+        name="middle",
+    )(where, place, own, *arrived)
+
+    return pl.pallas_call(
+        final_kernel,
+        out_shape=jax.ShapeDtypeStruct((rows, width), BF16),
+        in_specs=[VMEM, VMEM],
+        out_specs=VMEM,
+        compiler_params=params(8),
+        cost_estimate=pl.CostEstimate(flops=10**6, bytes_accessed=10**6, transcendentals=0),
         name="combine",
-    )(where, place, own, other, *arrived)
+    )(middle, other)
 
 
 def on_device(*args):

time: 48.7 us -> 48.3 us (level)
    pallas_call x1 -> x2, Pallas kernels: 1.13 us -> 1.21 us  [the longest x1 0.85 us: few_groups(): pl.pallas_call(final_kernel, out_shape=jax.ShapeDtypeStruct((rows, width)...]
  transfers between devices with their start and end apart: 16 -> 16, of which waited for: 4 -> 4; matrix products, arithmetic and copies ran while one was open for 0% -> 0% of each run, Pallas kernels for 30% -> 31%
where the time goes in v6:
time: 48.3 us; the launch traced here: 47.9 us
  starting transfers between devices  20.8 us (43%)
  Pallas kernels  17 us (35%)
  waiting for transfers between devices  7.83 us (16%)
  local copies, waits for them, and re-layouts  1.32 us (3%)
  between operations  0.81 us (2%)
    ppermute x14, starting transfers between devices, to(): return lax.ppermute(x, 'rows', [(i, i ^ d) for i in range(groups)])  20.8 us
    pallas_call x1, Pallas kernels, few_groups(): pl.pallas_call(functools.partial(base_kernel, groups), in_specs=[SMEM] +...  10.3 us
    ppermute x14, waiting for transfers between devices, to(): return lax.ppermute(x, 'rows', [(i, i ^ d) for i in range(groups)])  5.28 us
    pallas_call x1, Pallas kernels, few_groups(): pl.pallas_call(slots_kernel, out_shape=[jax.ShapeDtypeStruct((1, rows), j...  4.16 us
    ppermute x1, waiting for transfers between devices, few_groups(): other = lax.ppermute(partner, 'tp', swap)  2.02 us
    unnamed x10, local copies, waits for them, and re-layouts  1.32 us
  transfers between devices with their start and end apart: 16, of which 4 were waited for; matrix products, arithmetic and copies ran while one was open for 0% of the time, Pallas kernels for 31%

profile of v6, /device:TPU:0, one launch (start us, length us, event | category | flops | bytes accessed | tf_op | source)
XLA Modules:
  0.0 47.9 jit_solution(14531061088250915848)
XLA Ops:
  0.0 4.0 %collective-permute-start.3 = (bf16[16,4096]{1,0:T(8,128)(2,1)}, bf16[16,4096]{1,0:T(8,128)(2,1)S(1)}, u32[]{:S(2)}, u32[]{:S(2)}) collective-permute-start(bf16[16,4096]{1,0:T(8,128)(2,1)} %refs_1_.1), channel_id=1, source_target_pairs={{0,8},{2,10},{4,12},{6,14},{8,0},{10,2},{12,4},{14,6},{1,9},{3,11}... | collective-permute-start | bytes 393224 | tf_op jit(solution)/shard_map/ppermute | solution.py:212
  4.0 1.6 %collective-permute-start.1 = (bf16[16,4096]{1,0:T(8,128)(2,1)}, bf16[16,4096]{1,0:T(8,128)(2,1)S(1)}, u32[]{:S(2)}, u32[]{:S(2)}) collective-permute-start(bf16[16,4096]{1,0:T(8,128)(2,1)} %refs_1_.1), channel_id=1, source_target_pairs={{0,4},{2,6},{4,0},{6,2},{8,12},{10,14},{12,8},{14,10},{1,5},{3,7},... | collective-permute-start | bytes 393224 | tf_op jit(solution)/shard_map/ppermute | solution.py:212
  5.6 1.5 %collective-permute-start = (bf16[16,4096]{1,0:T(8,128)(2,1)}, bf16[16,4096]{1,0:T(8,128)(2,1)S(1)}, u32[]{:S(2)}, u32[]{:S(2)}) collective-permute-start(bf16[16,4096]{1,0:T(8,128)(2,1)} %refs_1_.1), channel_id=1, source_target_pairs={{0,2},{2,0},{4,6},{6,4},{8,10},{10,8},{12,14},{14,12},{1,3},{3,1},... | collective-permute-start | bytes 393224 | tf_op jit(solution)/shard_map/ppermute | solution.py:212
  7.1 0.1 pad_add_fusion.where.refs_0_
  7.2 4.8 %collective-permute-done.3.refs_6_.refs_5_ = bf16[16,4096]{1,0:T(8,128)(2,1)S(1)} collective-permute-done((bf16[16,4096]{1,0:T(8,128)(2,1)}, bf16[16,4096]{1,0:T(8,128)(2,1)S(1)}, u32[]{:S(2)}, u32[]{:S(2)}) %collective-permute-start.3) | collective-permute-done | bytes 131104 | tf_op jit(solution)/shard_map/ppermute | solution.py:212
  12.0 2.1 %collective-permute-start.4 = (bf16[16,4096]{1,0:T(8,128)(2,1)S(1)}, bf16[16,4096]{1,0:T(8,128)(2,1)S(1)}, u32[]{:S(2)}, u32[]{:S(2)}) collective-permute-start(bf16[16,4096]{1,0:T(8,128)(2,1)S(1)} %collective-permute-done.3.refs_6_.refs_5_), channel_id=1, source_target_pairs={{0,2},{2,0},{4,6},{6,4},{8,10},{10,8},{12,14},{14,12},{1,3},{3,1},... | collective-permute-start | bytes 393224 | tf_op jit(solution)/shard_map/ppermute | solution.py:212
  14.2 0.0 collective-permute-done.1.refs_4_.refs_3_
  14.2 0.3 collective-permute-start.2
  14.4 0.7 %copy-done.3 = s32[8]{0:T(128)S(1)} copy-done((s32[8]{0:T(128)S(1)}, s32[8]{0:T(128)}, u32[]{:S(2)}) %copy-start.3) | copy-done | bytes 56
  15.1 0.7 %copy-done.4 = s32[128,1]{0,1:T(1,128)S(1)} copy-done((s32[128,1]{0,1:T(1,128)S(1)}, s32[128,1]{0,1:T(1,128)}, u32[]{:S(2)}) %copy-start.4) | copy-done | bytes 536
  15.7 4.2 %slots.1 = (s32[1,128]{1,0:T(1,128)S(1)}, bf16[4096,1024]{1,0:T(8,128)(2,1)S(1)}) custom-call(s32[2]{0:T(128)S(1)} %pad_add_fusion.where.refs_0_, s32[8]{0:T(128)S(1)} %copy-done.3, s32[1,128]{1,0:T(1,128)S(1)} %bitcast.9, bf16[4096,3584]{1,0:T(8,128)(2,1)} %refs_10_.1), custom_call_target="tpu_custom_call" | custom-call | flops 99999997952 | bytes 100000000 | tf_op jit(solution)/shard_map/slots/pallas_call | solution.py:219
  19.9 0.0 collective-permute-done.refs_3_.refs_2_
  19.9 0.0 collective-permute-done.4.refs_7_.refs_6_
  19.9 0.0 collective-permute-done.5.refs_8_.refs_7_
  19.9 0.4 collective-permute-done.2.refs_5_.refs_4_
  20.4 0.6 %lowrank.1.low_a._ = f32[32,64]{1,0:T(8,128)S(1)} custom-call(s32[1]{0:T(128)} %bitcast.refs_0_.where, s32[1,128]{1,0:T(1,128)S(1)} %get-tuple-element.17.slots.refs_1_, bf16[16,4096]{1,0:T(8,128)(2,1)S(1)} %copy-done.1, bf16[16,4096]{1,0:T(8,128)(2,1)S(1)} %collective-permute-done.refs_3_.refs_2_, ...), custom_call_target="tpu_custom_call" | custom-call | flops 100000000 | bytes 2000000 | tf_op jit(solution)/shard_map/lowrank/pallas_call | solution.py:245
  20.9 0.0 collective-permute-start.7
  21.6 0.5 %collective-permute-done.7.low_b = f32[32,64]{1,0:T(8,128)S(1)} collective-permute-done((f32[32,64]{1,0:T(8,128)S(1)}, f32[32,64]{1,0:T(8,128)S(1)}, u32[]{:S(2)}, u32[]{:S(2)}) %collective-permute-start.7) | collective-permute-done | bytes 8224 | tf_op jit(solution)/shard_map/ppermute | solution.py:255
  22.1 0.8 %delta.1 = (bf16[32,1792]{1,0:T(8,128)(2,1)S(1)}, bf16[32,1792]{1,0:T(8,128)(2,1)S(1)}, bf16[32,1792]{1,0:T(8,128)(2,1)S(1)}, bf16[32,1792]{1,0:T(8,128)(2,1)S(1...) custom-call(s32[1]{0:T(128)} %bitcast.refs_0_.where, ...), custom_call_target="tpu_custom_call" | custom-call | flops 1000000 | bytes 1000000 | tf_op jit(solution)/shard_map/delta/pallas_call | solution.py:260
  22.9 1.4 %collective-permute-start.9 = (bf16[32,1792]{1,0:T(8,128)(2,1)S(1)}, bf16[32,1792]{1,0:T(8,128)(2,1)S(1)}, u32[]{:S(2)}, u32[]{:S(2)}) collective-permute-start(bf16[32,1792]{1,0:T(8,128)(2,1)S(1)} %get-tuple-element.22), channel_id=1, source_target_pairs={{0,2},{2,0},{4,6},{6,4},{8,10},{10,8},{12,14},{14,12},{1,3},{3,1},... | collective-permute-start | bytes 344072 | tf_op jit(solution)/shard_map/ppermute | solution.py:212
  24.4 2.0 %collective-permute-start.8 = (bf16[32,1792]{1,0:T(8,128)(2,1)S(1)}, bf16[32,1792]{1,0:T(8,128)(2,1)S(1)}, u32[]{:S(2)}, u32[]{:S(2)}) collective-permute-start(bf16[32,1792]{1,0:T(8,128)(2,1)S(1)} %get-tuple-element.20), channel_id=1, source_target_pairs={{0,4},{2,6},{4,0},{6,2},{8,12},{10,14},{12,8},{14,10},{1,5},{3,7},... | collective-permute-start | bytes 344072 | tf_op jit(solution)/shard_map/ppermute | solution.py:212
  26.4 1.7 %collective-permute-start.11 = (bf16[32,1792]{1,0:T(8,128)(2,1)S(1)}, bf16[32,1792]{1,0:T(8,128)(2,1)S(1)}, u32[]{:S(2)}, u32[]{:S(2)}) collective-permute-start(bf16[32,1792]{1,0:T(8,128)(2,1)S(1)} %get-tuple-element.25), channel_id=1, source_target_pairs={{0,8},{2,10},{4,12},{6,14},{8,0},{10,2},{12,4},{14,6},{1,9},{3,11}... | collective-permute-start | bytes 344072 | tf_op jit(solution)/shard_map/ppermute | solution.py:212
  28.1 0.8 %collective-permute-start.12 = (bf16[32,1792]{1,0:T(8,128)(2,1)S(1)}, bf16[32,1792]{1,0:T(8,128)(2,1)S(1)}, u32[]{:S(2)}, u32[]{:S(2)}) collective-permute-start(bf16[32,1792]{1,0:T(8,128)(2,1)S(1)} %get-tuple-element.26), channel_id=1, source_target_pairs={{0,10},{2,8},{4,14},{6,12},{8,2},{10,0},{12,6},{14,4},{1,11},{3,9}... | collective-permute-start | bytes 344072 | tf_op jit(solution)/shard_map/ppermute | solution.py:212
  28.8 3.1 %collective-permute-start.13 = (bf16[32,1792]{1,0:T(8,128)(2,1)S(1)}, bf16[32,1792]{1,0:T(8,128)(2,1)S(1)}, u32[]{:S(2)}, u32[]{:S(2)}) collective-permute-start(bf16[32,1792]{1,0:T(8,128)(2,1)S(1)} %get-tuple-element.27), channel_id=1, source_target_pairs={{0,12},{2,14},{4,8},{6,10},{8,4},{10,6},{12,0},{14,2},{1,13},{3,15... | collective-permute-start | bytes 344072 | tf_op jit(solution)/shard_map/ppermute | solution.py:212
  32.0 0.0 collective-permute-done.9._.refs_1_
  32.0 0.5 %collective-permute-start.10 = (bf16[32,1792]{1,0:T(8,128)(2,1)S(1)}, bf16[32,1792]{1,0:T(8,128)(2,1)S(1)}, u32[]{:S(2)}, u32[]{:S(2)}) collective-permute-start(bf16[32,1792]{1,0:T(8,128)(2,1)S(1)} %relay.3.refs_12_), channel_id=1, source_target_pairs={{0,6},{2,4},{4,2},{6,0},{8,14},{10,12},{12,10},{14,8},{1,7},{3,5},... | collective-permute-start | bytes 344072 | tf_op jit(solution)/shard_map/ppermute | solution.py:212
  32.6 1.7 %collective-permute-start.14 = (bf16[32,1792]{1,0:T(8,128)(2,1)S(1)}, bf16[32,1792]{1,0:T(8,128)(2,1)S(1)}, u32[]{:S(2)}, u32[]{:S(2)}) collective-permute-start(bf16[32,1792]{1,0:T(8,128)(2,1)S(1)} %relay.2.refs_11_), channel_id=1, source_target_pairs={{0,14},{2,12},{4,10},{6,8},{8,6},{10,4},{12,2},{14,0},{1,15},{3,13... | collective-permute-start | bytes 344072 | tf_op jit(solution)/shard_map/ppermute | solution.py:212
  34.2 10.3 %base.1 = (f32[128,1792]{1,0:T(8,128)S(1)}, f32[128,1792]{1,0:T(8,128)S(1)}) custom-call(s32[2]{0:T(128)S(1)} %pad_add_fusion.where.refs_0_, bf16[16,4096]{1,0:T(8,128)(2,1)S(1)} %copy-done.1, bf16[16,4096]{1,0:T(8,128)(2,1)S(1)} %collective-permute-done.refs_3_.refs_2_, bf16[16,4096]{1,0:T(8,128)(2,1)S(1)} %collective-permute-done.1.refs_4_.refs_3_, ...), custom_call_target="tpu_custom_call" | custom-call | flops 3758096384 | bytes 10000000 | tf_op jit(solution)/shard_map/base/pallas_call | solution.py:294
  44.5 0.1 collective-permute-start.15
  44.7 0.4 middle.1
  45.0 2.0 %collective-permute-done.15.other = f32[128,1792]{1,0:T(8,128)S(1)} collective-permute-done((f32[128,1792]{1,0:T(8,128)S(1)}, f32[128,1792]{1,0:T(8,128)S(1)}, u32[]{:S(2)}, u32[]{:S(2)}) %collective-permute-start.15) | collective-permute-done | bytes 917536 | tf_op jit(solution)/shard_map/ppermute | solution.py:310
  47.1 0.8 %combine.1 = bf16[128,1792]{1,0:T(8,128)(2,1)} custom-call(f32[128,1792]{1,0:T(8,128)S(1)} %middle.1, f32[128,1792]{1,0:T(8,128)S(1)} %collective-permute-done.15.other), custom_call_target="tpu_custom_call" | custom-call | flops 1000000 | bytes 1000000 | tf_op jit(solution)/shard_map/combine/pallas_call | solution.py:333
  (20 shorter events, 0.1 us)
Async XLA Ops:
  0.0 12.0 %collective-permute-start.3 = (bf16[16,4096]{1,0:T(8,128)(2,1)}, bf16[16,4096]{1,0:T(8,128)(2,1)S(1)}, u32[]{:S(2)}, u32[]{:S(2)}) collective-permute-start(bf16[16,4096]{1,0:T(8,128)(2,1)} %refs_1_.1), channel_id=1, source_target_pairs={{0,8},{2,10},{4,12},{6,14},{8,0},{10,2},{12,4},{14,6},{1,9},{3,11}... | collective-permute-start | bytes 393224 | tf_op jit(solution)/shard_map/ppermute | solution.py:212
  4.0 10.1 %collective-permute-start.1 = (bf16[16,4096]{1,0:T(8,128)(2,1)}, bf16[16,4096]{1,0:T(8,128)(2,1)S(1)}, u32[]{:S(2)}, u32[]{:S(2)}) collective-permute-start(bf16[16,4096]{1,0:T(8,128)(2,1)} %refs_1_.1), channel_id=1, source_target_pairs={{0,4},{2,6},{4,0},{6,2},{8,12},{10,14},{12,8},{14,10},{1,5},{3,7},... | collective-permute-start | bytes 393224 | tf_op jit(solution)/shard_map/ppermute | solution.py:212
  5.6 14.3 %collective-permute-start = (bf16[16,4096]{1,0:T(8,128)(2,1)}, bf16[16,4096]{1,0:T(8,128)(2,1)S(1)}, u32[]{:S(2)}, u32[]{:S(2)}) collective-permute-start(bf16[16,4096]{1,0:T(8,128)(2,1)} %refs_1_.1), channel_id=1, source_target_pairs={{0,2},{2,0},{4,6},{6,4},{8,10},{10,8},{12,14},{14,12},{1,3},{3,1},... | collective-permute-start | bytes 393224 | tf_op jit(solution)/shard_map/ppermute | solution.py:212
  7.1 12.8 %collective-permute-start.6 = (bf16[16,4096]{1,0:T(8,128)(2,1)}, bf16[16,4096]{1,0:T(8,128)(2,1)S(1)}, u32[]{:S(2)}, u32[]{:S(2)}) collective-permute-start(bf16[16,4096]{1,0:T(8,128)(2,1)} %refs_1_.1), channel_id=1, source_target_pairs={{0,14},{2,12},{4,10},{6,8},{8,6},{10,4},{12,2},{14,0},{1,15},{3,13... | collective-permute-start | bytes 393224 | tf_op jit(solution)/shard_map/ppermute | solution.py:212
  12.0 7.9 %collective-permute-start.4 = (bf16[16,4096]{1,0:T(8,128)(2,1)S(1)}, bf16[16,4096]{1,0:T(8,128)(2,1)S(1)}, u32[]{:S(2)}, u32[]{:S(2)}) collective-permute-start(bf16[16,4096]{1,0:T(8,128)(2,1)S(1)} %collective-permute-done.3.refs_6_.refs_5_), channel_id=1, source_target_pairs={{0,2},{2,0},{4,6},{6,4},{8,10},{10,8},{12,14},{14,12},{1,3},{3,1},... | collective-permute-start | bytes 393224 | tf_op jit(solution)/shard_map/ppermute | solution.py:212
  14.1 5.8 %collective-permute-start.5 = (bf16[16,4096]{1,0:T(8,128)(2,1)S(1)}, bf16[16,4096]{1,0:T(8,128)(2,1)S(1)}, u32[]{:S(2)}, u32[]{:S(2)}) collective-permute-start(bf16[16,4096]{1,0:T(8,128)(2,1)S(1)} %collective-permute-done.3.refs_6_.refs_5_), channel_id=1, source_target_pairs={{0,4},{2,6},{4,0},{6,2},{8,12},{10,14},{12,8},{14,10},{1,5},{3,7},... | collective-permute-start | bytes 393224 | tf_op jit(solution)/shard_map/ppermute | solution.py:212
  14.2 6.2 %collective-permute-start.2 = (bf16[16,4096]{1,0:T(8,128)(2,1)S(1)}, bf16[16,4096]{1,0:T(8,128)(2,1)S(1)}, u32[]{:S(2)}, u32[]{:S(2)}) collective-permute-start(bf16[16,4096]{1,0:T(8,128)(2,1)S(1)} %collective-permute-done.1.refs_4_.refs_3_), channel_id=1, source_target_pairs={{0,2},{2,0},{4,6},{6,4},{8,10},{10,8},{12,14},{14,12},{1,3},{3,1},... | collective-permute-start | bytes 393224 | tf_op jit(solution)/shard_map/ppermute | solution.py:212
  14.4 0.7 %copy-start.3 = (s32[8]{0:T(128)S(1)}, s32[8]{0:T(128)}, u32[]{:S(2)}) copy-start(s32[8]{0:T(128)} %index_map.1) | copy-start | bytes 100
  15.1 0.7 %copy-start.4 = (s32[128,1]{0,1:T(1,128)S(1)}, s32[128,1]{0,1:T(1,128)}, u32[]{:S(2)}) copy-start(s32[128,1]{0,1:T(1,128)} %param.12) | copy-start | bytes 1540
  15.7 4.6 %copy-start.1 = (bf16[16,4096]{1,0:T(8,128)(2,1)S(1)}, bf16[16,4096]{1,0:T(8,128)(2,1)}, u32[]{:S(2)}) copy-start(bf16[16,4096]{1,0:T(8,128)(2,1)} %refs_1_.1) | copy-start | bytes 393220
  15.7 4.6 %copy-start.2 = (bf16[1,64,4096]{2,1,0:T(8,128)(2,1)S(1)}, bf16[1,64,4096]{2,1,0:T(8,128)(2,1)}, u32[]{:S(2)}) copy-start(bf16[1,64,4096]{2,1,0:T(8,128)(2,1)} %param.9) | copy-start | bytes 1572868
  15.7 6.4 %copy-start = (bf16[1,64,8,1,1792]{4,2,3,1,0:T(8,128)(2,1)S(1)}, bf16[1,64,8,1,1792]{4,2,3,1,0:T(8,128)(2,1)}, u32[]{:S(2)}) copy-start(bf16[1,64,8,1,1792]{4,2,3,1,0:T(8,128)(2,1)} %param.10) | copy-start | bytes 5505028
  20.9 1.2 %collective-permute-start.7 = (f32[32,64]{1,0:T(8,128)S(1)}, f32[32,64]{1,0:T(8,128)S(1)}, u32[]{:S(2)}, u32[]{:S(2)}) collective-permute-start(f32[32,64]{1,0:T(8,128)S(1)} %lowrank.1.low_a._), channel_id=1, source_target_pairs={{0,1},{1,0},{2,3},{3,2},{4,5},{5,4},{6,7},{7,6},{8,9},{9,8},{10,11... | collective-permute-start | bytes 24584 | tf_op jit(solution)/shard_map/ppermute | solution.py:255
  22.9 9.1 %collective-permute-start.9 = (bf16[32,1792]{1,0:T(8,128)(2,1)S(1)}, bf16[32,1792]{1,0:T(8,128)(2,1)S(1)}, u32[]{:S(2)}, u32[]{:S(2)}) collective-permute-start(bf16[32,1792]{1,0:T(8,128)(2,1)S(1)} %get-tuple-element.22), channel_id=1, source_target_pairs={{0,2},{2,0},{4,6},{6,4},{8,10},{10,8},{12,14},{14,12},{1,3},{3,1},... | collective-permute-start | bytes 344072 | tf_op jit(solution)/shard_map/ppermute | solution.py:212
  24.4 8.2 %collective-permute-start.8 = (bf16[32,1792]{1,0:T(8,128)(2,1)S(1)}, bf16[32,1792]{1,0:T(8,128)(2,1)S(1)}, u32[]{:S(2)}, u32[]{:S(2)}) collective-permute-start(bf16[32,1792]{1,0:T(8,128)(2,1)S(1)} %get-tuple-element.20), channel_id=1, source_target_pairs={{0,4},{2,6},{4,0},{6,2},{8,12},{10,14},{12,8},{14,10},{1,5},{3,7},... | collective-permute-start | bytes 344072 | tf_op jit(solution)/shard_map/ppermute | solution.py:212
  26.4 18.1 %collective-permute-start.11 = (bf16[32,1792]{1,0:T(8,128)(2,1)S(1)}, bf16[32,1792]{1,0:T(8,128)(2,1)S(1)}, u32[]{:S(2)}, u32[]{:S(2)}) collective-permute-start(bf16[32,1792]{1,0:T(8,128)(2,1)S(1)} %get-tuple-element.25), channel_id=1, source_target_pairs={{0,8},{2,10},{4,12},{6,14},{8,0},{10,2},{12,4},{14,6},{1,9},{3,11}... | collective-permute-start | bytes 344072 | tf_op jit(solution)/shard_map/ppermute | solution.py:212
  28.1 16.6 %collective-permute-start.12 = (bf16[32,1792]{1,0:T(8,128)(2,1)S(1)}, bf16[32,1792]{1,0:T(8,128)(2,1)S(1)}, u32[]{:S(2)}, u32[]{:S(2)}) collective-permute-start(bf16[32,1792]{1,0:T(8,128)(2,1)S(1)} %get-tuple-element.26), channel_id=1, source_target_pairs={{0,10},{2,8},{4,14},{6,12},{8,2},{10,0},{12,6},{14,4},{1,11},{3,9}... | collective-permute-start | bytes 344072 | tf_op jit(solution)/shard_map/ppermute | solution.py:212
  28.8 15.8 %collective-permute-start.13 = (bf16[32,1792]{1,0:T(8,128)(2,1)S(1)}, bf16[32,1792]{1,0:T(8,128)(2,1)S(1)}, u32[]{:S(2)}, u32[]{:S(2)}) collective-permute-start(bf16[32,1792]{1,0:T(8,128)(2,1)S(1)} %get-tuple-element.27), channel_id=1, source_target_pairs={{0,12},{2,14},{4,8},{6,10},{8,4},{10,6},{12,0},{14,2},{1,13},{3,15... | collective-permute-start | bytes 344072 | tf_op jit(solution)/shard_map/ppermute | solution.py:212
  32.0 12.6 %collective-permute-start.10 = (bf16[32,1792]{1,0:T(8,128)(2,1)S(1)}, bf16[32,1792]{1,0:T(8,128)(2,1)S(1)}, u32[]{:S(2)}, u32[]{:S(2)}) collective-permute-start(bf16[32,1792]{1,0:T(8,128)(2,1)S(1)} %relay.3.refs_12_), channel_id=1, source_target_pairs={{0,6},{2,4},{4,2},{6,0},{8,14},{10,12},{12,10},{14,8},{1,7},{3,5},... | collective-permute-start | bytes 344072 | tf_op jit(solution)/shard_map/ppermute | solution.py:212
  32.6 12.1 %collective-permute-start.14 = (bf16[32,1792]{1,0:T(8,128)(2,1)S(1)}, bf16[32,1792]{1,0:T(8,128)(2,1)S(1)}, u32[]{:S(2)}, u32[]{:S(2)}) collective-permute-start(bf16[32,1792]{1,0:T(8,128)(2,1)S(1)} %relay.2.refs_11_), channel_id=1, source_target_pairs={{0,14},{2,12},{4,10},{6,8},{8,6},{10,4},{12,2},{14,0},{1,15},{3,13... | collective-permute-start | bytes 344072 | tf_op jit(solution)/shard_map/ppermute | solution.py:212
  44.5 2.5 %collective-permute-start.15 = (f32[128,1792]{1,0:T(8,128)S(1)}, f32[128,1792]{1,0:T(8,128)S(1)}, u32[]{:S(2)}, u32[]{:S(2)}) collective-permute-start(f32[128,1792]{1,0:T(8,128)S(1)} %get-tuple-element.28), channel_id=1, source_target_pairs={{0,1},{1,0},{2,3},{3,2},{4,5},{5,4},{6,7},{7,6},{8,9},{9,8},{10,11... | collective-permute-start | bytes 2752520 | tf_op jit(solution)/shard_map/ppermute | solution.py:310

commit v7 on v6

--- a/solution.py
+++ b/solution.py
@@ -214,7 +214,7 @@
     def params(limit):
         return pltpu.CompilerParams(vmem_limit_bytes=limit << 20)
 
-    tile, buffers, ready = 256, 5, 4
+    tile, buffers, ready = 256, 5, 3
     both = jnp.stack([me, core])
     slot, ahead = pl.pallas_call(
         slots_kernel,

time: 48.3 us -> 48.3 us (level)
  waiting for transfers between devices: 7.83 us -> 8.43 us
    pallas_call x1, Pallas kernels: 10.3 us -> 10.9 us  [few_groups(): pl.pallas_call(functools.partial(base_kernel, groups), in_specs=[SMEM] +...]
    pallas_call x1, Pallas kernels: 4.16 us -> 3.56 us  [few_groups(): pl.pallas_call(slots_kernel, out_shape=[jax.ShapeDtypeStruct((1, rows), j...]
    ppermute x14, waiting for transfers between devices: 5.28 us -> 5.88 us  [to(): return lax.ppermute(x, 'rows', [(i, i ^ d) for i in range(groups)])]
where the time goes in v7:
time: 48.3 us; the launch traced here: 48.1 us
  starting transfers between devices  20.4 us (42%)
  Pallas kernels  17.1 us (35%)
  waiting for transfers between devices  8.43 us (17%)
  local copies, waits for them, and re-layouts  1.32 us (3%)
  between operations  0.81 us (2%)
    ppermute x14, starting transfers between devices, to(): return lax.ppermute(x, 'rows', [(i, i ^ d) for i in range(groups)])  20.3 us
    pallas_call x1, Pallas kernels, few_groups(): pl.pallas_call(functools.partial(base_kernel, groups), in_specs=[SMEM] +...  10.9 us
    ppermute x14, waiting for transfers between devices, to(): return lax.ppermute(x, 'rows', [(i, i ^ d) for i in range(groups)])  5.88 us
    pallas_call x1, Pallas kernels, few_groups(): pl.pallas_call(slots_kernel, out_shape=[jax.ShapeDtypeStruct((1, rows), j...  3.56 us
    ppermute x1, waiting for transfers between devices, few_groups(): other = lax.ppermute(partner, 'tp', swap)  2.03 us
    unnamed x10, local copies, waits for them, and re-layouts  1.32 us
  transfers between devices with their start and end apart: 16, of which 4 were waited for; matrix products, arithmetic and copies ran while one was open for 0% of the time, Pallas kernels for 31%

profile of v7, /device:TPU:0, one launch (start us, length us, event | category | flops | bytes accessed | tf_op | source)
XLA Modules:
  0.0 48.1 jit_solution(3410552088436306634)
XLA Ops:
  0.0 4.0 %collective-permute-start.3 = (bf16[16,4096]{1,0:T(8,128)(2,1)}, bf16[16,4096]{1,0:T(8,128)(2,1)S(1)}, u32[]{:S(2)}, u32[]{:S(2)}) collective-permute-start(bf16[16,4096]{1,0:T(8,128)(2,1)} %refs_1_.1), channel_id=1, source_target_pairs={{0,8},{2,10},{4,12},{6,14},{8,0},{10,2},{12,4},{14,6},{1,9},{3,11}... | collective-permute-start | bytes 393224 | tf_op jit(solution)/shard_map/ppermute | solution.py:212
  4.0 1.6 %collective-permute-start.1 = (bf16[16,4096]{1,0:T(8,128)(2,1)}, bf16[16,4096]{1,0:T(8,128)(2,1)S(1)}, u32[]{:S(2)}, u32[]{:S(2)}) collective-permute-start(bf16[16,4096]{1,0:T(8,128)(2,1)} %refs_1_.1), channel_id=1, source_target_pairs={{0,4},{2,6},{4,0},{6,2},{8,12},{10,14},{12,8},{14,10},{1,5},{3,7},... | collective-permute-start | bytes 393224 | tf_op jit(solution)/shard_map/ppermute | solution.py:212
  5.6 1.5 %collective-permute-start = (bf16[16,4096]{1,0:T(8,128)(2,1)}, bf16[16,4096]{1,0:T(8,128)(2,1)S(1)}, u32[]{:S(2)}, u32[]{:S(2)}) collective-permute-start(bf16[16,4096]{1,0:T(8,128)(2,1)} %refs_1_.1), channel_id=1, source_target_pairs={{0,2},{2,0},{4,6},{6,4},{8,10},{10,8},{12,14},{14,12},{1,3},{3,1},... | collective-permute-start | bytes 393224 | tf_op jit(solution)/shard_map/ppermute | solution.py:212
  7.1 0.0 collective-permute-start.6
  7.1 0.1 pad_add_fusion.where.refs_0_
  7.2 4.8 %collective-permute-done.3.refs_6_.refs_5_ = bf16[16,4096]{1,0:T(8,128)(2,1)S(1)} collective-permute-done((bf16[16,4096]{1,0:T(8,128)(2,1)}, bf16[16,4096]{1,0:T(8,128)(2,1)S(1)}, u32[]{:S(2)}, u32[]{:S(2)}) %collective-permute-start.3) | collective-permute-done | bytes 131104 | tf_op jit(solution)/shard_map/ppermute | solution.py:212
  12.0 2.1 %collective-permute-start.4 = (bf16[16,4096]{1,0:T(8,128)(2,1)S(1)}, bf16[16,4096]{1,0:T(8,128)(2,1)S(1)}, u32[]{:S(2)}, u32[]{:S(2)}) collective-permute-start(bf16[16,4096]{1,0:T(8,128)(2,1)S(1)} %collective-permute-done.3.refs_6_.refs_5_), channel_id=1, source_target_pairs={{0,2},{2,0},{4,6},{6,4},{8,10},{10,8},{12,14},{14,12},{1,3},{3,1},... | collective-permute-start | bytes 393224 | tf_op jit(solution)/shard_map/ppermute | solution.py:212
  14.2 0.3 collective-permute-start.2
  14.4 0.7 %copy-done.3 = s32[8]{0:T(128)S(1)} copy-done((s32[8]{0:T(128)S(1)}, s32[8]{0:T(128)}, u32[]{:S(2)}) %copy-start.3) | copy-done | bytes 56
  15.1 0.7 %copy-done.4 = s32[128,1]{0,1:T(1,128)S(1)} copy-done((s32[128,1]{0,1:T(1,128)S(1)}, s32[128,1]{0,1:T(1,128)}, u32[]{:S(2)}) %copy-start.4) | copy-done | bytes 536
  15.7 3.6 %slots.1 = (s32[1,128]{1,0:T(1,128)S(1)}, bf16[4096,768]{1,0:T(8,128)(2,1)S(1)}) custom-call(s32[2]{0:T(128)S(1)} %pad_add_fusion.where.refs_0_, s32[8]{0:T(128)S(1)} %copy-done.3, s32[1,128]{1,0:T(1,128)S(1)} %bitcast.9, bf16[4096,3584]{1,0:T(8,128)(2,1)} %refs_10_.1), custom_call_target="tpu_custom_call" | custom-call | flops 99999997952 | bytes 100000000 | tf_op jit(solution)/shard_map/slots/pallas_call | solution.py:219
  19.3 0.0 collective-permute-done.4.refs_7_.refs_6_
  19.3 0.0 collective-permute-done.5.refs_8_.refs_7_
  19.3 1.0 %collective-permute-done.2.refs_5_.refs_4_ = bf16[16,4096]{1,0:T(8,128)(2,1)S(1)} collective-permute-done((bf16[16,4096]{1,0:T(8,128)(2,1)S(1)}, bf16[16,4096]{1,0:T(8,128)(2,1)S(1)}, u32[]{:S(2)}, u32[]{:S(2)}) %collective-permute-start.2) | collective-permute-done | bytes 131104 | tf_op jit(solution)/shard_map/ppermute | solution.py:212
  20.4 0.6 %lowrank.1.low_a._ = f32[32,64]{1,0:T(8,128)S(1)} custom-call(s32[1]{0:T(128)} %bitcast.refs_0_.where, s32[1,128]{1,0:T(1,128)S(1)} %get-tuple-element.17.slots.refs_1_, bf16[16,4096]{1,0:T(8,128)(2,1)S(1)} %copy-done.1, bf16[16,4096]{1,0:T(8,128)(2,1)S(1)} %collective-permute-done.refs_3_.refs_2_, ...), custom_call_target="tpu_custom_call" | custom-call | flops 100000000 | bytes 2000000 | tf_op jit(solution)/shard_map/lowrank/pallas_call | solution.py:245
  20.9 0.0 collective-permute-start.7
  21.6 0.5 %collective-permute-done.7.low_b = f32[32,64]{1,0:T(8,128)S(1)} collective-permute-done((f32[32,64]{1,0:T(8,128)S(1)}, f32[32,64]{1,0:T(8,128)S(1)}, u32[]{:S(2)}, u32[]{:S(2)}) %collective-permute-start.7) | collective-permute-done | bytes 8224 | tf_op jit(solution)/shard_map/ppermute | solution.py:255
  22.1 0.8 %delta.1 = (bf16[32,1792]{1,0:T(8,128)(2,1)S(1)}, bf16[32,1792]{1,0:T(8,128)(2,1)S(1)}, bf16[32,1792]{1,0:T(8,128)(2,1)S(1)}, bf16[32,1792]{1,0:T(8,128)(2,1)S(1...) custom-call(s32[1]{0:T(128)} %bitcast.refs_0_.where, ...), custom_call_target="tpu_custom_call" | custom-call | flops 1000000 | bytes 1000000 | tf_op jit(solution)/shard_map/delta/pallas_call | solution.py:260
  22.9 0.8 %collective-permute-start.9 = (bf16[32,1792]{1,0:T(8,128)(2,1)S(1)}, bf16[32,1792]{1,0:T(8,128)(2,1)S(1)}, u32[]{:S(2)}, u32[]{:S(2)}) collective-permute-start(bf16[32,1792]{1,0:T(8,128)(2,1)S(1)} %get-tuple-element.22), channel_id=1, source_target_pairs={{0,2},{2,0},{4,6},{6,4},{8,10},{10,8},{12,14},{14,12},{1,3},{3,1},... | collective-permute-start | bytes 344072 | tf_op jit(solution)/shard_map/ppermute | solution.py:212
  23.8 2.1 %collective-permute-start.8 = (bf16[32,1792]{1,0:T(8,128)(2,1)S(1)}, bf16[32,1792]{1,0:T(8,128)(2,1)S(1)}, u32[]{:S(2)}, u32[]{:S(2)}) collective-permute-start(bf16[32,1792]{1,0:T(8,128)(2,1)S(1)} %get-tuple-element.20), channel_id=1, source_target_pairs={{0,4},{2,6},{4,0},{6,2},{8,12},{10,14},{12,8},{14,10},{1,5},{3,7},... | collective-permute-start | bytes 344072 | tf_op jit(solution)/shard_map/ppermute | solution.py:212
  25.9 2.2 %collective-permute-start.11 = (bf16[32,1792]{1,0:T(8,128)(2,1)S(1)}, bf16[32,1792]{1,0:T(8,128)(2,1)S(1)}, u32[]{:S(2)}, u32[]{:S(2)}) collective-permute-start(bf16[32,1792]{1,0:T(8,128)(2,1)S(1)} %get-tuple-element.25), channel_id=1, source_target_pairs={{0,8},{2,10},{4,12},{6,14},{8,0},{10,2},{12,4},{14,6},{1,9},{3,11}... | collective-permute-start | bytes 344072 | tf_op jit(solution)/shard_map/ppermute | solution.py:212
  28.1 0.8 %collective-permute-start.12 = (bf16[32,1792]{1,0:T(8,128)(2,1)S(1)}, bf16[32,1792]{1,0:T(8,128)(2,1)S(1)}, u32[]{:S(2)}, u32[]{:S(2)}) collective-permute-start(bf16[32,1792]{1,0:T(8,128)(2,1)S(1)} %get-tuple-element.26), channel_id=1, source_target_pairs={{0,10},{2,8},{4,14},{6,12},{8,2},{10,0},{12,6},{14,4},{1,11},{3,9}... | collective-permute-start | bytes 344072 | tf_op jit(solution)/shard_map/ppermute | solution.py:212
  28.8 2.5 %collective-permute-start.13 = (bf16[32,1792]{1,0:T(8,128)(2,1)S(1)}, bf16[32,1792]{1,0:T(8,128)(2,1)S(1)}, u32[]{:S(2)}, u32[]{:S(2)}) collective-permute-start(bf16[32,1792]{1,0:T(8,128)(2,1)S(1)} %get-tuple-element.27), channel_id=1, source_target_pairs={{0,12},{2,14},{4,8},{6,10},{8,4},{10,6},{12,0},{14,2},{1,13},{3,15... | collective-permute-start | bytes 344072 | tf_op jit(solution)/shard_map/ppermute | solution.py:212
  31.4 1.1 %collective-permute-start.10 = (bf16[32,1792]{1,0:T(8,128)(2,1)S(1)}, bf16[32,1792]{1,0:T(8,128)(2,1)S(1)}, u32[]{:S(2)}, u32[]{:S(2)}) collective-permute-start(bf16[32,1792]{1,0:T(8,128)(2,1)S(1)} %relay.3.refs_12_), channel_id=1, source_target_pairs={{0,6},{2,4},{4,2},{6,0},{8,14},{10,12},{12,10},{14,8},{1,7},{3,5},... | collective-permute-start | bytes 344072 | tf_op jit(solution)/shard_map/ppermute | solution.py:212
  32.6 1.2 %collective-permute-start.14 = (bf16[32,1792]{1,0:T(8,128)(2,1)S(1)}, bf16[32,1792]{1,0:T(8,128)(2,1)S(1)}, u32[]{:S(2)}, u32[]{:S(2)}) collective-permute-start(bf16[32,1792]{1,0:T(8,128)(2,1)S(1)} %relay.2.refs_11_), channel_id=1, source_target_pairs={{0,14},{2,12},{4,10},{6,8},{8,6},{10,4},{12,2},{14,0},{1,15},{3,13... | collective-permute-start | bytes 344072 | tf_op jit(solution)/shard_map/ppermute | solution.py:212
  33.8 10.9 %base.1 = (f32[128,1792]{1,0:T(8,128)S(1)}, f32[128,1792]{1,0:T(8,128)S(1)}) custom-call(s32[2]{0:T(128)S(1)} %pad_add_fusion.where.refs_0_, bf16[16,4096]{1,0:T(8,128)(2,1)S(1)} %copy-done.1, bf16[16,4096]{1,0:T(8,128)(2,1)S(1)} %collective-permute-done.refs_3_.refs_2_, bf16[16,4096]{1,0:T(8,128)(2,1)S(1)} %collective-permute-done.1.refs_4_.refs_3_, ...), custom_call_target="tpu_custom_call" | custom-call | flops 3758096384 | bytes 10000000 | tf_op jit(solution)/shard_map/base/pallas_call | solution.py:294
  44.7 0.0 collective-permute-done.11.refs_4_
  44.7 0.1 collective-permute-start.15
  44.8 0.0 collective-permute-done.13.refs_6_
  44.9 0.4 middle.1
  45.2 2.0 %collective-permute-done.15.other = f32[128,1792]{1,0:T(8,128)S(1)} collective-permute-done((f32[128,1792]{1,0:T(8,128)S(1)}, f32[128,1792]{1,0:T(8,128)S(1)}, u32[]{:S(2)}, u32[]{:S(2)}) %collective-permute-start.15) | collective-permute-done | bytes 917536 | tf_op jit(solution)/shard_map/ppermute | solution.py:310
  47.2 0.8 %combine.1 = bf16[128,1792]{1,0:T(8,128)(2,1)} custom-call(f32[128,1792]{1,0:T(8,128)S(1)} %middle.1, f32[128,1792]{1,0:T(8,128)S(1)} %collective-permute-done.15.other), custom_call_target="tpu_custom_call" | custom-call | flops 1000000 | bytes 1000000 | tf_op jit(solution)/shard_map/combine/pallas_call | solution.py:333
  (20 shorter events, 0.1 us)
Async XLA Ops:
  0.0 12.0 %collective-permute-start.3 = (bf16[16,4096]{1,0:T(8,128)(2,1)}, bf16[16,4096]{1,0:T(8,128)(2,1)S(1)}, u32[]{:S(2)}, u32[]{:S(2)}) collective-permute-start(bf16[16,4096]{1,0:T(8,128)(2,1)} %refs_1_.1), channel_id=1, source_target_pairs={{0,8},{2,10},{4,12},{6,14},{8,0},{10,2},{12,4},{14,6},{1,9},{3,11}... | collective-permute-start | bytes 393224 | tf_op jit(solution)/shard_map/ppermute | solution.py:212
  4.0 10.1 %collective-permute-start.1 = (bf16[16,4096]{1,0:T(8,128)(2,1)}, bf16[16,4096]{1,0:T(8,128)(2,1)S(1)}, u32[]{:S(2)}, u32[]{:S(2)}) collective-permute-start(bf16[16,4096]{1,0:T(8,128)(2,1)} %refs_1_.1), channel_id=1, source_target_pairs={{0,4},{2,6},{4,0},{6,2},{8,12},{10,14},{12,8},{14,10},{1,5},{3,7},... | collective-permute-start | bytes 393224 | tf_op jit(solution)/shard_map/ppermute | solution.py:212
  5.6 13.7 %collective-permute-start = (bf16[16,4096]{1,0:T(8,128)(2,1)}, bf16[16,4096]{1,0:T(8,128)(2,1)S(1)}, u32[]{:S(2)}, u32[]{:S(2)}) collective-permute-start(bf16[16,4096]{1,0:T(8,128)(2,1)} %refs_1_.1), channel_id=1, source_target_pairs={{0,2},{2,0},{4,6},{6,4},{8,10},{10,8},{12,14},{14,12},{1,3},{3,1},... | collective-permute-start | bytes 393224 | tf_op jit(solution)/shard_map/ppermute | solution.py:212
  7.1 12.2 %collective-permute-start.6 = (bf16[16,4096]{1,0:T(8,128)(2,1)}, bf16[16,4096]{1,0:T(8,128)(2,1)S(1)}, u32[]{:S(2)}, u32[]{:S(2)}) collective-permute-start(bf16[16,4096]{1,0:T(8,128)(2,1)} %refs_1_.1), channel_id=1, source_target_pairs={{0,14},{2,12},{4,10},{6,8},{8,6},{10,4},{12,2},{14,0},{1,15},{3,13... | collective-permute-start | bytes 393224 | tf_op jit(solution)/shard_map/ppermute | solution.py:212
  12.0 7.3 %collective-permute-start.4 = (bf16[16,4096]{1,0:T(8,128)(2,1)S(1)}, bf16[16,4096]{1,0:T(8,128)(2,1)S(1)}, u32[]{:S(2)}, u32[]{:S(2)}) collective-permute-start(bf16[16,4096]{1,0:T(8,128)(2,1)S(1)} %collective-permute-done.3.refs_6_.refs_5_), channel_id=1, source_target_pairs={{0,2},{2,0},{4,6},{6,4},{8,10},{10,8},{12,14},{14,12},{1,3},{3,1},... | collective-permute-start | bytes 393224 | tf_op jit(solution)/shard_map/ppermute | solution.py:212
  14.1 5.2 %collective-permute-start.5 = (bf16[16,4096]{1,0:T(8,128)(2,1)S(1)}, bf16[16,4096]{1,0:T(8,128)(2,1)S(1)}, u32[]{:S(2)}, u32[]{:S(2)}) collective-permute-start(bf16[16,4096]{1,0:T(8,128)(2,1)S(1)} %collective-permute-done.3.refs_6_.refs_5_), channel_id=1, source_target_pairs={{0,4},{2,6},{4,0},{6,2},{8,12},{10,14},{12,8},{14,10},{1,5},{3,7},... | collective-permute-start | bytes 393224 | tf_op jit(solution)/shard_map/ppermute | solution.py:212
  14.2 6.2 %collective-permute-start.2 = (bf16[16,4096]{1,0:T(8,128)(2,1)S(1)}, bf16[16,4096]{1,0:T(8,128)(2,1)S(1)}, u32[]{:S(2)}, u32[]{:S(2)}) collective-permute-start(bf16[16,4096]{1,0:T(8,128)(2,1)S(1)} %collective-permute-done.1.refs_4_.refs_3_), channel_id=1, source_target_pairs={{0,2},{2,0},{4,6},{6,4},{8,10},{10,8},{12,14},{14,12},{1,3},{3,1},... | collective-permute-start | bytes 393224 | tf_op jit(solution)/shard_map/ppermute | solution.py:212
  14.4 0.7 %copy-start.3 = (s32[8]{0:T(128)S(1)}, s32[8]{0:T(128)}, u32[]{:S(2)}) copy-start(s32[8]{0:T(128)} %index_map.1) | copy-start | bytes 100
  15.1 0.7 %copy-start.4 = (s32[128,1]{0,1:T(1,128)S(1)}, s32[128,1]{0,1:T(1,128)}, u32[]{:S(2)}) copy-start(s32[128,1]{0,1:T(1,128)} %param.12) | copy-start | bytes 1540
  15.7 4.6 %copy-start.1 = (bf16[16,4096]{1,0:T(8,128)(2,1)S(1)}, bf16[16,4096]{1,0:T(8,128)(2,1)}, u32[]{:S(2)}) copy-start(bf16[16,4096]{1,0:T(8,128)(2,1)} %refs_1_.1) | copy-start | bytes 393220
  15.7 4.6 %copy-start.2 = (bf16[1,64,4096]{2,1,0:T(8,128)(2,1)S(1)}, bf16[1,64,4096]{2,1,0:T(8,128)(2,1)}, u32[]{:S(2)}) copy-start(bf16[1,64,4096]{2,1,0:T(8,128)(2,1)} %param.9) | copy-start | bytes 1572868
  15.7 6.4 %copy-start = (bf16[1,64,8,1,1792]{4,2,3,1,0:T(8,128)(2,1)S(1)}, bf16[1,64,8,1,1792]{4,2,3,1,0:T(8,128)(2,1)}, u32[]{:S(2)}) copy-start(bf16[1,64,8,1,1792]{4,2,3,1,0:T(8,128)(2,1)} %param.10) | copy-start | bytes 5505028
  20.9 1.2 %collective-permute-start.7 = (f32[32,64]{1,0:T(8,128)S(1)}, f32[32,64]{1,0:T(8,128)S(1)}, u32[]{:S(2)}, u32[]{:S(2)}) collective-permute-start(f32[32,64]{1,0:T(8,128)S(1)} %lowrank.1.low_a._), channel_id=1, source_target_pairs={{0,1},{1,0},{2,3},{3,2},{4,5},{5,4},{6,7},{7,6},{8,9},{9,8},{10,11... | collective-permute-start | bytes 24584 | tf_op jit(solution)/shard_map/ppermute | solution.py:255
  22.9 8.5 %collective-permute-start.9 = (bf16[32,1792]{1,0:T(8,128)(2,1)S(1)}, bf16[32,1792]{1,0:T(8,128)(2,1)S(1)}, u32[]{:S(2)}, u32[]{:S(2)}) collective-permute-start(bf16[32,1792]{1,0:T(8,128)(2,1)S(1)} %get-tuple-element.22), channel_id=1, source_target_pairs={{0,2},{2,0},{4,6},{6,4},{8,10},{10,8},{12,14},{14,12},{1,3},{3,1},... | collective-permute-start | bytes 344072 | tf_op jit(solution)/shard_map/ppermute | solution.py:212
  23.8 8.8 %collective-permute-start.8 = (bf16[32,1792]{1,0:T(8,128)(2,1)S(1)}, bf16[32,1792]{1,0:T(8,128)(2,1)S(1)}, u32[]{:S(2)}, u32[]{:S(2)}) collective-permute-start(bf16[32,1792]{1,0:T(8,128)(2,1)S(1)} %get-tuple-element.20), channel_id=1, source_target_pairs={{0,4},{2,6},{4,0},{6,2},{8,12},{10,14},{12,8},{14,10},{1,5},{3,7},... | collective-permute-start | bytes 344072 | tf_op jit(solution)/shard_map/ppermute | solution.py:212
  25.9 18.8 %collective-permute-start.11 = (bf16[32,1792]{1,0:T(8,128)(2,1)S(1)}, bf16[32,1792]{1,0:T(8,128)(2,1)S(1)}, u32[]{:S(2)}, u32[]{:S(2)}) collective-permute-start(bf16[32,1792]{1,0:T(8,128)(2,1)S(1)} %get-tuple-element.25), channel_id=1, source_target_pairs={{0,8},{2,10},{4,12},{6,14},{8,0},{10,2},{12,4},{14,6},{1,9},{3,11}... | collective-permute-start | bytes 344072 | tf_op jit(solution)/shard_map/ppermute | solution.py:212
  28.1 16.8 %collective-permute-start.12 = (bf16[32,1792]{1,0:T(8,128)(2,1)S(1)}, bf16[32,1792]{1,0:T(8,128)(2,1)S(1)}, u32[]{:S(2)}, u32[]{:S(2)}) collective-permute-start(bf16[32,1792]{1,0:T(8,128)(2,1)S(1)} %get-tuple-element.26), channel_id=1, source_target_pairs={{0,10},{2,8},{4,14},{6,12},{8,2},{10,0},{12,6},{14,4},{1,11},{3,9}... | collective-permute-start | bytes 344072 | tf_op jit(solution)/shard_map/ppermute | solution.py:212
  28.8 16.0 %collective-permute-start.13 = (bf16[32,1792]{1,0:T(8,128)(2,1)S(1)}, bf16[32,1792]{1,0:T(8,128)(2,1)S(1)}, u32[]{:S(2)}, u32[]{:S(2)}) collective-permute-start(bf16[32,1792]{1,0:T(8,128)(2,1)S(1)} %get-tuple-element.27), channel_id=1, source_target_pairs={{0,12},{2,14},{4,8},{6,10},{8,4},{10,6},{12,0},{14,2},{1,13},{3,15... | collective-permute-start | bytes 344072 | tf_op jit(solution)/shard_map/ppermute | solution.py:212
  31.4 13.4 %collective-permute-start.10 = (bf16[32,1792]{1,0:T(8,128)(2,1)S(1)}, bf16[32,1792]{1,0:T(8,128)(2,1)S(1)}, u32[]{:S(2)}, u32[]{:S(2)}) collective-permute-start(bf16[32,1792]{1,0:T(8,128)(2,1)S(1)} %relay.3.refs_12_), channel_id=1, source_target_pairs={{0,6},{2,4},{4,2},{6,0},{8,14},{10,12},{12,10},{14,8},{1,7},{3,5},... | collective-permute-start | bytes 344072 | tf_op jit(solution)/shard_map/ppermute | solution.py:212
  32.6 12.3 %collective-permute-start.14 = (bf16[32,1792]{1,0:T(8,128)(2,1)S(1)}, bf16[32,1792]{1,0:T(8,128)(2,1)S(1)}, u32[]{:S(2)}, u32[]{:S(2)}) collective-permute-start(bf16[32,1792]{1,0:T(8,128)(2,1)S(1)} %relay.2.refs_11_), channel_id=1, source_target_pairs={{0,14},{2,12},{4,10},{6,8},{8,6},{10,4},{12,2},{14,0},{1,15},{3,13... | collective-permute-start | bytes 344072 | tf_op jit(solution)/shard_map/ppermute | solution.py:212
  44.7 2.5 %collective-permute-start.15 = (f32[128,1792]{1,0:T(8,128)S(1)}, f32[128,1792]{1,0:T(8,128)S(1)}, u32[]{:S(2)}, u32[]{:S(2)}) collective-permute-start(f32[128,1792]{1,0:T(8,128)S(1)} %get-tuple-element.28), channel_id=1, source_target_pairs={{0,1},{1,0},{2,3},{3,2},{4,5},{5,4},{6,7},{7,6},{8,9},{9,8},{10,11... | collective-permute-start | bytes 2752520 | tf_op jit(solution)/shard_map/ppermute | solution.py:310

commit v8 on v7

--- a/solution.py
+++ b/solution.py
@@ -269,7 +269,7 @@
         )(where, adapter_scales.reshape(1, 1), low, low_other, up, after)
 
     arrived = [None] * groups
-    order = (0, 2, 1, 4, 5, 6, 7, 3)
+    order = (0, 2, 1, 4, 5, 7, 6, 3)
     blocks = deltas(order, low)
     for d, x in zip(order[:6], blocks):
         arrived[d] = to(x, d) if d else x
@@ -286,7 +286,7 @@
         )(block, after)
 
     seventh = once(blocks[6], arrived[2])
-    arrived[7] = to(seventh, 7)
+    arrived[6] = to(seventh, 6)
     eighth = once(blocks[7], arrived[1])
     arrived[3] = to(eighth, 3)
 

time: 48.3 us -> 48.2 us (level)
  no operation moved by 1% of the time
where the time goes in v8:
time: 48.2 us; the launch traced here: 48 us
  starting transfers between devices  20.3 us (42%)
  Pallas kernels  17.1 us (35%)
  waiting for transfers between devices  8.43 us (17%)
  local copies, waits for them, and re-layouts  1.32 us (3%)
  between operations  0.81 us (2%)
    ppermute x14, starting transfers between devices, to(): return lax.ppermute(x, 'rows', [(i, i ^ d) for i in range(groups)])  20.3 us
    pallas_call x1, Pallas kernels, few_groups(): pl.pallas_call(functools.partial(base_kernel, groups), in_specs=[SMEM] +...  10.9 us
    ppermute x14, waiting for transfers between devices, to(): return lax.ppermute(x, 'rows', [(i, i ^ d) for i in range(groups)])  5.88 us
    pallas_call x1, Pallas kernels, few_groups(): pl.pallas_call(slots_kernel, out_shape=[jax.ShapeDtypeStruct((1, rows), j...  3.56 us
    ppermute x1, waiting for transfers between devices, few_groups(): other = lax.ppermute(partner, 'tp', swap)  2.02 us
    unnamed x10, local copies, waits for them, and re-layouts  1.32 us
  transfers between devices with their start and end apart: 16, of which 4 were waited for; matrix products, arithmetic and copies ran while one was open for 0% of the time, Pallas kernels for 31%

profile of v8, /device:TPU:0, one launch (start us, length us, event | category | flops | bytes accessed | tf_op | source)
XLA Modules:
  0.0 48.0 jit_solution(6525304928185532635)
XLA Ops:
  0.0 4.0 %collective-permute-start.3 = (bf16[16,4096]{1,0:T(8,128)(2,1)}, bf16[16,4096]{1,0:T(8,128)(2,1)S(1)}, u32[]{:S(2)}, u32[]{:S(2)}) collective-permute-start(bf16[16,4096]{1,0:T(8,128)(2,1)} %refs_1_.1), channel_id=1, source_target_pairs={{0,8},{2,10},{4,12},{6,14},{8,0},{10,2},{12,4},{14,6},{1,9},{3,11}... | collective-permute-start | bytes 393224 | tf_op jit(solution)/shard_map/ppermute | solution.py:212
  4.0 1.6 %collective-permute-start.1 = (bf16[16,4096]{1,0:T(8,128)(2,1)}, bf16[16,4096]{1,0:T(8,128)(2,1)S(1)}, u32[]{:S(2)}, u32[]{:S(2)}) collective-permute-start(bf16[16,4096]{1,0:T(8,128)(2,1)} %refs_1_.1), channel_id=1, source_target_pairs={{0,4},{2,6},{4,0},{6,2},{8,12},{10,14},{12,8},{14,10},{1,5},{3,7},... | collective-permute-start | bytes 393224 | tf_op jit(solution)/shard_map/ppermute | solution.py:212
  5.6 1.5 %collective-permute-start = (bf16[16,4096]{1,0:T(8,128)(2,1)}, bf16[16,4096]{1,0:T(8,128)(2,1)S(1)}, u32[]{:S(2)}, u32[]{:S(2)}) collective-permute-start(bf16[16,4096]{1,0:T(8,128)(2,1)} %refs_1_.1), channel_id=1, source_target_pairs={{0,2},{2,0},{4,6},{6,4},{8,10},{10,8},{12,14},{14,12},{1,3},{3,1},... | collective-permute-start | bytes 393224 | tf_op jit(solution)/shard_map/ppermute | solution.py:212
  7.1 0.0 collective-permute-start.6
  7.1 0.1 pad_add_fusion.where.refs_0_
  7.2 4.8 %collective-permute-done.3.refs_6_.refs_5_ = bf16[16,4096]{1,0:T(8,128)(2,1)S(1)} collective-permute-done((bf16[16,4096]{1,0:T(8,128)(2,1)}, bf16[16,4096]{1,0:T(8,128)(2,1)S(1)}, u32[]{:S(2)}, u32[]{:S(2)}) %collective-permute-start.3) | collective-permute-done | bytes 131104 | tf_op jit(solution)/shard_map/ppermute | solution.py:212
  12.0 2.1 %collective-permute-start.4 = (bf16[16,4096]{1,0:T(8,128)(2,1)S(1)}, bf16[16,4096]{1,0:T(8,128)(2,1)S(1)}, u32[]{:S(2)}, u32[]{:S(2)}) collective-permute-start(bf16[16,4096]{1,0:T(8,128)(2,1)S(1)} %collective-permute-done.3.refs_6_.refs_5_), channel_id=1, source_target_pairs={{0,2},{2,0},{4,6},{6,4},{8,10},{10,8},{12,14},{14,12},{1,3},{3,1},... | collective-permute-start | bytes 393224 | tf_op jit(solution)/shard_map/ppermute | solution.py:212
  14.2 0.3 collective-permute-start.2
  14.4 0.7 %copy-done.3 = s32[8]{0:T(128)S(1)} copy-done((s32[8]{0:T(128)S(1)}, s32[8]{0:T(128)}, u32[]{:S(2)}) %copy-start.3) | copy-done | bytes 56
  15.1 0.7 %copy-done.4 = s32[128,1]{0,1:T(1,128)S(1)} copy-done((s32[128,1]{0,1:T(1,128)S(1)}, s32[128,1]{0,1:T(1,128)}, u32[]{:S(2)}) %copy-start.4) | copy-done | bytes 536
  15.7 3.6 %slots.1 = (s32[1,128]{1,0:T(1,128)S(1)}, bf16[4096,768]{1,0:T(8,128)(2,1)S(1)}) custom-call(s32[2]{0:T(128)S(1)} %pad_add_fusion.where.refs_0_, s32[8]{0:T(128)S(1)} %copy-done.3, s32[1,128]{1,0:T(1,128)S(1)} %bitcast.9, bf16[4096,3584]{1,0:T(8,128)(2,1)} %refs_10_.1), custom_call_target="tpu_custom_call" | custom-call | flops 99999997952 | bytes 100000000 | tf_op jit(solution)/shard_map/slots/pallas_call | solution.py:219
  19.3 0.0 collective-permute-done.refs_3_.refs_2_
  19.3 0.0 collective-permute-done.4.refs_7_.refs_6_
  19.3 0.0 collective-permute-done.5.refs_8_.refs_7_
  19.3 1.0 %collective-permute-done.2.refs_5_.refs_4_ = bf16[16,4096]{1,0:T(8,128)(2,1)S(1)} collective-permute-done((bf16[16,4096]{1,0:T(8,128)(2,1)S(1)}, bf16[16,4096]{1,0:T(8,128)(2,1)S(1)}, u32[]{:S(2)}, u32[]{:S(2)}) %collective-permute-start.2) | collective-permute-done | bytes 131104 | tf_op jit(solution)/shard_map/ppermute | solution.py:212
  20.4 0.6 %lowrank.1.low_a._ = f32[32,64]{1,0:T(8,128)S(1)} custom-call(s32[1]{0:T(128)} %bitcast.refs_0_.where, s32[1,128]{1,0:T(1,128)S(1)} %get-tuple-element.17.slots.refs_1_, bf16[16,4096]{1,0:T(8,128)(2,1)S(1)} %copy-done.1, bf16[16,4096]{1,0:T(8,128)(2,1)S(1)} %collective-permute-done.refs_3_.refs_2_, ...), custom_call_target="tpu_custom_call" | custom-call | flops 100000000 | bytes 2000000 | tf_op jit(solution)/shard_map/lowrank/pallas_call | solution.py:245
  20.9 0.0 collective-permute-start.7
  21.6 0.5 %collective-permute-done.7.low_b = f32[32,64]{1,0:T(8,128)S(1)} collective-permute-done((f32[32,64]{1,0:T(8,128)S(1)}, f32[32,64]{1,0:T(8,128)S(1)}, u32[]{:S(2)}, u32[]{:S(2)}) %collective-permute-start.7) | collective-permute-done | bytes 8224 | tf_op jit(solution)/shard_map/ppermute | solution.py:255
  22.1 0.8 %delta.1 = (bf16[32,1792]{1,0:T(8,128)(2,1)S(1)}, bf16[32,1792]{1,0:T(8,128)(2,1)S(1)}, bf16[32,1792]{1,0:T(8,128)(2,1)S(1)}, bf16[32,1792]{1,0:T(8,128)(2,1)S(1...) custom-call(s32[1]{0:T(128)} %bitcast.refs_0_.where, ...), custom_call_target="tpu_custom_call" | custom-call | flops 1000000 | bytes 1000000 | tf_op jit(solution)/shard_map/delta/pallas_call | solution.py:260
  22.9 0.8 %collective-permute-start.9 = (bf16[32,1792]{1,0:T(8,128)(2,1)S(1)}, bf16[32,1792]{1,0:T(8,128)(2,1)S(1)}, u32[]{:S(2)}, u32[]{:S(2)}) collective-permute-start(bf16[32,1792]{1,0:T(8,128)(2,1)S(1)} %get-tuple-element.22), channel_id=1, source_target_pairs={{0,2},{2,0},{4,6},{6,4},{8,10},{10,8},{12,14},{14,12},{1,3},{3,1},... | collective-permute-start | bytes 344072 | tf_op jit(solution)/shard_map/ppermute | solution.py:212
  23.8 2.1 %collective-permute-start.8 = (bf16[32,1792]{1,0:T(8,128)(2,1)S(1)}, bf16[32,1792]{1,0:T(8,128)(2,1)S(1)}, u32[]{:S(2)}, u32[]{:S(2)}) collective-permute-start(bf16[32,1792]{1,0:T(8,128)(2,1)S(1)} %get-tuple-element.20), channel_id=1, source_target_pairs={{0,4},{2,6},{4,0},{6,2},{8,12},{10,14},{12,8},{14,10},{1,5},{3,7},... | collective-permute-start | bytes 344072 | tf_op jit(solution)/shard_map/ppermute | solution.py:212
  25.9 2.2 %collective-permute-start.11 = (bf16[32,1792]{1,0:T(8,128)(2,1)S(1)}, bf16[32,1792]{1,0:T(8,128)(2,1)S(1)}, u32[]{:S(2)}, u32[]{:S(2)}) collective-permute-start(bf16[32,1792]{1,0:T(8,128)(2,1)S(1)} %get-tuple-element.25), channel_id=1, source_target_pairs={{0,8},{2,10},{4,12},{6,14},{8,0},{10,2},{12,4},{14,6},{1,9},{3,11}... | collective-permute-start | bytes 344072 | tf_op jit(solution)/shard_map/ppermute | solution.py:212
  28.1 0.8 %collective-permute-start.12 = (bf16[32,1792]{1,0:T(8,128)(2,1)S(1)}, bf16[32,1792]{1,0:T(8,128)(2,1)S(1)}, u32[]{:S(2)}, u32[]{:S(2)}) collective-permute-start(bf16[32,1792]{1,0:T(8,128)(2,1)S(1)} %get-tuple-element.26), channel_id=1, source_target_pairs={{0,10},{2,8},{4,14},{6,12},{8,2},{10,0},{12,6},{14,4},{1,11},{3,9}... | collective-permute-start | bytes 344072 | tf_op jit(solution)/shard_map/ppermute | solution.py:212
  28.8 3.5 %collective-permute-start.14 = (bf16[32,1792]{1,0:T(8,128)(2,1)S(1)}, bf16[32,1792]{1,0:T(8,128)(2,1)S(1)}, u32[]{:S(2)}, u32[]{:S(2)}) collective-permute-start(bf16[32,1792]{1,0:T(8,128)(2,1)S(1)} %get-tuple-element.27), channel_id=1, source_target_pairs={{0,14},{2,12},{4,10},{6,8},{8,6},{10,4},{12,2},{14,0},{1,15},{3,13... | collective-permute-start | bytes 344072 | tf_op jit(solution)/shard_map/ppermute | solution.py:212
  32.3 0.0 collective-permute-done.9._.refs_1_
  32.3 0.4 collective-permute-start.10
  32.7 1.0 %collective-permute-start.13 = (bf16[32,1792]{1,0:T(8,128)(2,1)S(1)}, bf16[32,1792]{1,0:T(8,128)(2,1)S(1)}, u32[]{:S(2)}, u32[]{:S(2)}) collective-permute-start(bf16[32,1792]{1,0:T(8,128)(2,1)S(1)} %relay.2.refs_11_), channel_id=1, source_target_pairs={{0,12},{2,14},{4,8},{6,10},{8,4},{10,6},{12,0},{14,2},{1,13},{3,15... | collective-permute-start | bytes 344072 | tf_op jit(solution)/shard_map/ppermute | solution.py:212
  33.7 10.9 %base.1 = (f32[128,1792]{1,0:T(8,128)S(1)}, f32[128,1792]{1,0:T(8,128)S(1)}) custom-call(s32[2]{0:T(128)S(1)} %pad_add_fusion.where.refs_0_, bf16[16,4096]{1,0:T(8,128)(2,1)S(1)} %copy-done.1, bf16[16,4096]{1,0:T(8,128)(2,1)S(1)} %collective-permute-done.refs_3_.refs_2_, bf16[16,4096]{1,0:T(8,128)(2,1)S(1)} %collective-permute-done.1.refs_4_.refs_3_, ...), custom_call_target="tpu_custom_call" | custom-call | flops 3758096384 | bytes 10000000 | tf_op jit(solution)/shard_map/base/pallas_call | solution.py:294
  44.7 0.1 collective-permute-start.15
  44.8 0.4 middle.1
  45.2 2.0 %collective-permute-done.15.other = f32[128,1792]{1,0:T(8,128)S(1)} collective-permute-done((f32[128,1792]{1,0:T(8,128)S(1)}, f32[128,1792]{1,0:T(8,128)S(1)}, u32[]{:S(2)}, u32[]{:S(2)}) %collective-permute-start.15) | collective-permute-done | bytes 917536 | tf_op jit(solution)/shard_map/ppermute | solution.py:310
  47.2 0.8 %combine.1 = bf16[128,1792]{1,0:T(8,128)(2,1)} custom-call(f32[128,1792]{1,0:T(8,128)S(1)} %middle.1, f32[128,1792]{1,0:T(8,128)S(1)} %collective-permute-done.15.other), custom_call_target="tpu_custom_call" | custom-call | flops 1000000 | bytes 1000000 | tf_op jit(solution)/shard_map/combine/pallas_call | solution.py:333
  (20 shorter events, 0.1 us)
Async XLA Ops:
  0.0 12.0 %collective-permute-start.3 = (bf16[16,4096]{1,0:T(8,128)(2,1)}, bf16[16,4096]{1,0:T(8,128)(2,1)S(1)}, u32[]{:S(2)}, u32[]{:S(2)}) collective-permute-start(bf16[16,4096]{1,0:T(8,128)(2,1)} %refs_1_.1), channel_id=1, source_target_pairs={{0,8},{2,10},{4,12},{6,14},{8,0},{10,2},{12,4},{14,6},{1,9},{3,11}... | collective-permute-start | bytes 393224 | tf_op jit(solution)/shard_map/ppermute | solution.py:212
  4.0 10.1 %collective-permute-start.1 = (bf16[16,4096]{1,0:T(8,128)(2,1)}, bf16[16,4096]{1,0:T(8,128)(2,1)S(1)}, u32[]{:S(2)}, u32[]{:S(2)}) collective-permute-start(bf16[16,4096]{1,0:T(8,128)(2,1)} %refs_1_.1), channel_id=1, source_target_pairs={{0,4},{2,6},{4,0},{6,2},{8,12},{10,14},{12,8},{14,10},{1,5},{3,7},... | collective-permute-start | bytes 393224 | tf_op jit(solution)/shard_map/ppermute | solution.py:212
  5.6 13.7 %collective-permute-start = (bf16[16,4096]{1,0:T(8,128)(2,1)}, bf16[16,4096]{1,0:T(8,128)(2,1)S(1)}, u32[]{:S(2)}, u32[]{:S(2)}) collective-permute-start(bf16[16,4096]{1,0:T(8,128)(2,1)} %refs_1_.1), channel_id=1, source_target_pairs={{0,2},{2,0},{4,6},{6,4},{8,10},{10,8},{12,14},{14,12},{1,3},{3,1},... | collective-permute-start | bytes 393224 | tf_op jit(solution)/shard_map/ppermute | solution.py:212
  7.1 12.2 %collective-permute-start.6 = (bf16[16,4096]{1,0:T(8,128)(2,1)}, bf16[16,4096]{1,0:T(8,128)(2,1)S(1)}, u32[]{:S(2)}, u32[]{:S(2)}) collective-permute-start(bf16[16,4096]{1,0:T(8,128)(2,1)} %refs_1_.1), channel_id=1, source_target_pairs={{0,14},{2,12},{4,10},{6,8},{8,6},{10,4},{12,2},{14,0},{1,15},{3,13... | collective-permute-start | bytes 393224 | tf_op jit(solution)/shard_map/ppermute | solution.py:212
  12.0 7.3 %collective-permute-start.4 = (bf16[16,4096]{1,0:T(8,128)(2,1)S(1)}, bf16[16,4096]{1,0:T(8,128)(2,1)S(1)}, u32[]{:S(2)}, u32[]{:S(2)}) collective-permute-start(bf16[16,4096]{1,0:T(8,128)(2,1)S(1)} %collective-permute-done.3.refs_6_.refs_5_), channel_id=1, source_target_pairs={{0,2},{2,0},{4,6},{6,4},{8,10},{10,8},{12,14},{14,12},{1,3},{3,1},... | collective-permute-start | bytes 393224 | tf_op jit(solution)/shard_map/ppermute | solution.py:212
  14.1 5.2 %collective-permute-start.5 = (bf16[16,4096]{1,0:T(8,128)(2,1)S(1)}, bf16[16,4096]{1,0:T(8,128)(2,1)S(1)}, u32[]{:S(2)}, u32[]{:S(2)}) collective-permute-start(bf16[16,4096]{1,0:T(8,128)(2,1)S(1)} %collective-permute-done.3.refs_6_.refs_5_), channel_id=1, source_target_pairs={{0,4},{2,6},{4,0},{6,2},{8,12},{10,14},{12,8},{14,10},{1,5},{3,7},... | collective-permute-start | bytes 393224 | tf_op jit(solution)/shard_map/ppermute | solution.py:212
  14.2 6.2 %collective-permute-start.2 = (bf16[16,4096]{1,0:T(8,128)(2,1)S(1)}, bf16[16,4096]{1,0:T(8,128)(2,1)S(1)}, u32[]{:S(2)}, u32[]{:S(2)}) collective-permute-start(bf16[16,4096]{1,0:T(8,128)(2,1)S(1)} %collective-permute-done.1.refs_4_.refs_3_), channel_id=1, source_target_pairs={{0,2},{2,0},{4,6},{6,4},{8,10},{10,8},{12,14},{14,12},{1,3},{3,1},... | collective-permute-start | bytes 393224 | tf_op jit(solution)/shard_map/ppermute | solution.py:212
  14.4 0.7 %copy-start.3 = (s32[8]{0:T(128)S(1)}, s32[8]{0:T(128)}, u32[]{:S(2)}) copy-start(s32[8]{0:T(128)} %index_map.1) | copy-start | bytes 100
  15.1 0.7 %copy-start.4 = (s32[128,1]{0,1:T(1,128)S(1)}, s32[128,1]{0,1:T(1,128)}, u32[]{:S(2)}) copy-start(s32[128,1]{0,1:T(1,128)} %param.12) | copy-start | bytes 1540
  15.7 4.6 %copy-start.1 = (bf16[16,4096]{1,0:T(8,128)(2,1)S(1)}, bf16[16,4096]{1,0:T(8,128)(2,1)}, u32[]{:S(2)}) copy-start(bf16[16,4096]{1,0:T(8,128)(2,1)} %refs_1_.1) | copy-start | bytes 393220
  15.7 4.6 %copy-start.2 = (bf16[1,64,4096]{2,1,0:T(8,128)(2,1)S(1)}, bf16[1,64,4096]{2,1,0:T(8,128)(2,1)}, u32[]{:S(2)}) copy-start(bf16[1,64,4096]{2,1,0:T(8,128)(2,1)} %param.9) | copy-start | bytes 1572868
  15.7 6.4 %copy-start = (bf16[1,64,8,1,1792]{4,2,3,1,0:T(8,128)(2,1)S(1)}, bf16[1,64,8,1,1792]{4,2,3,1,0:T(8,128)(2,1)}, u32[]{:S(2)}) copy-start(bf16[1,64,8,1,1792]{4,2,3,1,0:T(8,128)(2,1)} %param.10) | copy-start | bytes 5505028
  20.9 1.2 %collective-permute-start.7 = (f32[32,64]{1,0:T(8,128)S(1)}, f32[32,64]{1,0:T(8,128)S(1)}, u32[]{:S(2)}, u32[]{:S(2)}) collective-permute-start(f32[32,64]{1,0:T(8,128)S(1)} %lowrank.1.low_a._), channel_id=1, source_target_pairs={{0,1},{1,0},{2,3},{3,2},{4,5},{5,4},{6,7},{7,6},{8,9},{9,8},{10,11... | collective-permute-start | bytes 24584 | tf_op jit(solution)/shard_map/ppermute | solution.py:255
  22.9 9.4 %collective-permute-start.9 = (bf16[32,1792]{1,0:T(8,128)(2,1)S(1)}, bf16[32,1792]{1,0:T(8,128)(2,1)S(1)}, u32[]{:S(2)}, u32[]{:S(2)}) collective-permute-start(bf16[32,1792]{1,0:T(8,128)(2,1)S(1)} %get-tuple-element.22), channel_id=1, source_target_pairs={{0,2},{2,0},{4,6},{6,4},{8,10},{10,8},{12,14},{14,12},{1,3},{3,1},... | collective-permute-start | bytes 344072 | tf_op jit(solution)/shard_map/ppermute | solution.py:212
  23.8 8.9 %collective-permute-start.8 = (bf16[32,1792]{1,0:T(8,128)(2,1)S(1)}, bf16[32,1792]{1,0:T(8,128)(2,1)S(1)}, u32[]{:S(2)}, u32[]{:S(2)}) collective-permute-start(bf16[32,1792]{1,0:T(8,128)(2,1)S(1)} %get-tuple-element.20), channel_id=1, source_target_pairs={{0,4},{2,6},{4,0},{6,2},{8,12},{10,14},{12,8},{14,10},{1,5},{3,7},... | collective-permute-start | bytes 344072 | tf_op jit(solution)/shard_map/ppermute | solution.py:212
  25.9 18.8 %collective-permute-start.11 = (bf16[32,1792]{1,0:T(8,128)(2,1)S(1)}, bf16[32,1792]{1,0:T(8,128)(2,1)S(1)}, u32[]{:S(2)}, u32[]{:S(2)}) collective-permute-start(bf16[32,1792]{1,0:T(8,128)(2,1)S(1)} %get-tuple-element.25), channel_id=1, source_target_pairs={{0,8},{2,10},{4,12},{6,14},{8,0},{10,2},{12,4},{14,6},{1,9},{3,11}... | collective-permute-start | bytes 344072 | tf_op jit(solution)/shard_map/ppermute | solution.py:212
  28.1 16.7 %collective-permute-start.12 = (bf16[32,1792]{1,0:T(8,128)(2,1)S(1)}, bf16[32,1792]{1,0:T(8,128)(2,1)S(1)}, u32[]{:S(2)}, u32[]{:S(2)}) collective-permute-start(bf16[32,1792]{1,0:T(8,128)(2,1)S(1)} %get-tuple-element.26), channel_id=1, source_target_pairs={{0,10},{2,8},{4,14},{6,12},{8,2},{10,0},{12,6},{14,4},{1,11},{3,9}... | collective-permute-start | bytes 344072 | tf_op jit(solution)/shard_map/ppermute | solution.py:212
  28.8 15.9 %collective-permute-start.14 = (bf16[32,1792]{1,0:T(8,128)(2,1)S(1)}, bf16[32,1792]{1,0:T(8,128)(2,1)S(1)}, u32[]{:S(2)}, u32[]{:S(2)}) collective-permute-start(bf16[32,1792]{1,0:T(8,128)(2,1)S(1)} %get-tuple-element.27), channel_id=1, source_target_pairs={{0,14},{2,12},{4,10},{6,8},{8,6},{10,4},{12,2},{14,0},{1,15},{3,13... | collective-permute-start | bytes 344072 | tf_op jit(solution)/shard_map/ppermute | solution.py:212
  32.3 12.4 %collective-permute-start.10 = (bf16[32,1792]{1,0:T(8,128)(2,1)S(1)}, bf16[32,1792]{1,0:T(8,128)(2,1)S(1)}, u32[]{:S(2)}, u32[]{:S(2)}) collective-permute-start(bf16[32,1792]{1,0:T(8,128)(2,1)S(1)} %relay.3.refs_12_), channel_id=1, source_target_pairs={{0,6},{2,4},{4,2},{6,0},{8,14},{10,12},{12,10},{14,8},{1,7},{3,5},... | collective-permute-start | bytes 344072 | tf_op jit(solution)/shard_map/ppermute | solution.py:212
  32.7 12.1 %collective-permute-start.13 = (bf16[32,1792]{1,0:T(8,128)(2,1)S(1)}, bf16[32,1792]{1,0:T(8,128)(2,1)S(1)}, u32[]{:S(2)}, u32[]{:S(2)}) collective-permute-start(bf16[32,1792]{1,0:T(8,128)(2,1)S(1)} %relay.2.refs_11_), channel_id=1, source_target_pairs={{0,12},{2,14},{4,8},{6,10},{8,4},{10,6},{12,0},{14,2},{1,13},{3,15... | collective-permute-start | bytes 344072 | tf_op jit(solution)/shard_map/ppermute | solution.py:212
  44.7 2.5 %collective-permute-start.15 = (f32[128,1792]{1,0:T(8,128)S(1)}, f32[128,1792]{1,0:T(8,128)S(1)}, u32[]{:S(2)}, u32[]{:S(2)}) collective-permute-start(f32[128,1792]{1,0:T(8,128)S(1)} %get-tuple-element.28), channel_id=1, source_target_pairs={{0,1},{1,0},{2,3},{3,2},{4,5},{5,4},{6,7},{7,6},{8,9},{9,8},{10,11... | collective-permute-start | bytes 2752520 | tf_op jit(solution)/shard_map/ppermute | solution.py:310
